TPU v7x, 32 devices: a whole 2x2x4 slice. The times are simulated.
32 devices in a mesh: blk: 8 (over z, x), head: 4 (over y, core).
Axes of the slice: x: 2, y: 2, z: 4, core: 2. Of those that a mesh axis runs over, the one named last changes fastest.
Arguments:
- long_query: bfloat16 [1024, 4096], P('blk', 'head'), may hold values from -64 to 64
- long_new_kv: bfloat16 [2, 1024, 1024], P(None, 'blk', 'head'), may hold values from -6 to 6
- sink_kv: bfloat16 [2, 2, 4, 1024], P(None, None, None, 'head'), may hold values from -6 to 6
- window: bfloat16 [2, 8192, 1024], P(None, 'blk', 'head'), may hold values from -64 to 64
- long_len: int32 [2], replicated, may hold values from 5 to 32768, as said below
- long_offset: int32 [2], replicated, may hold values from 0 to 4095
- dec_query: bfloat16 [32, 4096], P(('blk', 'head')), may hold values from -64 to 64
- dec_new_kv: bfloat16 [32, 2, 1024], P(('blk', 'head')), may hold values from -6 to 6
- dec_cache: bfloat16 [2, 32, 512, 1024], P(None, 'blk', None, 'head'), may hold values from -64 to 64
- dec_len: int32 [32], P('blk'), may hold values from 1 to 512, as said below
- arrival_order: int32 [32], replicated, may hold values from 0 to 31, each once
Outputs:
- long_out: bfloat16 [1024, 4096], P('blk', 'head')
- dec_out: bfloat16 [32, 4096], P('blk', 'head')
Inputs may be any that keep to these rules, and one draw needn't show every extreme that they name: `long_len`: one prefilling request has exactly 32768 cached tokens. `dec_len`: some decoding request has exactly 512 cached tokens.
All inputs are finite; a program needn't handle non-finite values.
Results may differ from a plain program's by a relative error of at most 0.014.
The roundings to bfloat16 on the way count: a program that leaves them out, or rounds other values in their place, can miss the bound.
Values may be sent and summed in bfloat16 or wider, within the bound.
No kernel may reach another device: no remote copies, remote signals or barrier semaphores. Data moves between devices by JAX's collectives and lax.ppermute only.
A program may use at most 64 MiB of HBM per device.

v0:
```python
import math

import jax
import jax.numpy as jnp
from jax import lax
from jax.sharding import PartitionSpec as P

HEAD_DIM = 128
W = 4096
SINKS = 4
GROUP = 4
SPAN = 512


MASKED_SCORE = -1e30


def for_sending(value):
    return jax.tree.map(lambda a: a.astype(jnp.bfloat16) if a.dtype == jnp.float32 else a, value)


def partner(block, axis, distance):
    count = lax.axis_size(axis)
    route = []
    for low in range(count):
        high = low | 1 << distance
        if high != low and high < count:
            route += [(low, high), (high, low)]
    return lax.ppermute(block, axis, route)


def rotate(vectors, positions):
    halfway = HEAD_DIM // 2
    frequency = 10000.0 ** (-(jnp.arange(halfway, dtype=jnp.float32) * 2.0 / HEAD_DIM))
    angles = positions.astype(jnp.float32)[:, None] * frequency[None, :]
    cosine = jnp.cos(angles)[:, None, :]
    sine_part = jnp.sin(angles)[:, None, :]
    first_half = vectors[..., :halfway]
    second_half = vectors[..., halfway:]
    return jnp.concatenate(
        [
            first_half * cosine - second_half * sine_part,
            second_half * cosine + first_half * sine_part,
        ],
        axis=-1,
    )


def attend_by_head(queries, key_rows, value_rows, visible, score_scale):

    def one_head(operands):
        head_q, head_keys, head_values = operands
        scores = (
            jnp.einsum("ngd,md->ngm", head_q, head_keys, preferred_element_type=jnp.float32)
            * score_scale
        )
        scores = jnp.where(visible[:, None, :], scores, MASKED_SCORE)
        head_top = jnp.max(scores, axis=-1)
        weights = jnp.where(visible[:, None, :], jnp.exp(scores - head_top[..., None]), 0.0)
        head_total = jnp.sum(weights, axis=-1)
        head_mix = jnp.einsum(
            "ngm,md->ngd",
            weights.astype(jnp.bfloat16),
            head_values,
            preferred_element_type=jnp.float32,
        )
        return (head_top, head_total, head_mix)

    tops, totals, mixes = lax.map(
        one_head,
        (jnp.moveaxis(queries, 1, 0), jnp.moveaxis(key_rows, 1, 0), jnp.moveaxis(value_rows, 1, 0)),
    )
    return (jnp.moveaxis(tops, 0, 1), jnp.moveaxis(totals, 0, 1), jnp.moveaxis(mixes, 0, 1))


def join_ordered(flag, mine, theirs, axis_number):
    return jax.tree.map(
        lambda own_piece, peer_piece: jnp.concatenate(
            [jnp.where(flag, peer_piece, own_piece), jnp.where(flag, own_piece, peer_piece)],
            axis=axis_number,
        ),
        mine,
        theirs,
    )


def shards(
    long_query,
    long_new_kv,
    sink_kv,
    window,
    long_len,
    long_offset,
    dec_query,
    dec_new_kv,
    dec_cache,
    dec_len,
    arrival_order,
):
    score_scale = 1.0 / math.sqrt(HEAD_DIM)
    blk_index = lax.axis_index("blk")
    members = GROUP
    depth = members.bit_length() - 1
    request = blk_index // members
    place = blk_index % members
    own_rows = long_query.shape[0]
    q_heads = long_query.shape[1] // HEAD_DIM
    kv_heads = long_new_kv.shape[2] // HEAD_DIM
    group_size = q_heads // kv_heads
    length = lax.dynamic_index_in_dim(long_len, request, 0, keepdims=False)
    offset = lax.dynamic_index_in_dim(long_offset, request, 0, keepdims=False)
    filled = jnp.minimum(length - SINKS, W)
    own_step = place * own_rows + jnp.arange(own_rows, dtype=jnp.int32)
    own_pos = length + own_step
    own_q = rotate(
        long_query.reshape(own_rows, q_heads, HEAD_DIM).astype(jnp.float32), own_pos
    ).astype(jnp.bfloat16)
    own_grouped = own_q.reshape(own_rows, kv_heads, group_size, HEAD_DIM)
    own_key = rotate(
        long_new_kv[0].reshape(own_rows, kv_heads, HEAD_DIM).astype(jnp.float32), own_pos
    ).astype(jnp.bfloat16)
    sink_pair = lax.dynamic_index_in_dim(sink_kv, request, 1, keepdims=False)
    sink_keys = sink_pair[0].reshape(SINKS, kv_heads, HEAD_DIM)
    sink_values = sink_pair[1].reshape(SINKS, kv_heads, HEAD_DIM)
    pieces = (window, jnp.stack([own_key.reshape(own_rows, kv_heads * HEAD_DIM), long_new_kv[1]]))
    for level in range(depth):
        received = jax.tree.map(
            lambda part, own: part.astype(own.dtype),
            partner(for_sending(pieces), "blk", level),
            pieces,
        )
        upper_side = place // (1 << level) % 2 == 1
        pieces = join_ordered(upper_side, pieces, received, 1)
    all_window, all_new = pieces
    key_rows = jnp.concatenate(
        [
            sink_keys,
            all_window[0].reshape(W, kv_heads, HEAD_DIM),
            all_new[0].reshape(SPAN, kv_heads, HEAD_DIM),
        ],
        axis=0,
    )
    value_rows = jnp.concatenate(
        [
            sink_values,
            all_window[1].reshape(W, kv_heads, HEAD_DIM),
            all_new[1].reshape(SPAN, kv_heads, HEAD_DIM),
        ],
        axis=0,
    )
    slot_age = jnp.mod(jnp.arange(W, dtype=jnp.int32) - offset, W)
    in_window = (slot_age[None, :] < filled) & (slot_age[None, :] > own_step[:, None] + filled - W)
    causal = jnp.arange(SPAN, dtype=jnp.int32)[None, :] <= own_step[:, None]
    visible = jnp.concatenate([jnp.ones((own_rows, SINKS), dtype=bool), in_window, causal], axis=1)
    row_top, row_total, row_mix = attend_by_head(
        own_grouped, key_rows, value_rows, visible, score_scale
    )
    long_out = (
        (row_mix / row_total[..., None]).reshape(own_rows, q_heads * HEAD_DIM).astype(jnp.bfloat16)
    )
    head_count = lax.axis_size("head")
    arriving = dec_query.shape[0]
    query_parts = dec_query.reshape(arriving, 1, head_count, dec_query.shape[1] // head_count)
    new_parts = dec_new_kv.reshape(arriving, 2, head_count, dec_new_kv.shape[2] // head_count)
    query_mine, new_mine = (
        lax.all_to_all(query_parts, "head", split_axis=2, concat_axis=0, tiled=True),
        lax.all_to_all(new_parts, "head", split_axis=2, concat_axis=0, tiled=True),
    )
    query_width = query_mine.shape[3]
    key_width = new_mine.shape[3]
    every_dec_q, every_dec_new = (
        lax.all_gather(query_mine.reshape(-1, query_width), "blk", axis=0, tiled=True),
        lax.all_gather(new_mine.reshape(-1, 2 * key_width), "blk", axis=0, tiled=True),
    )
    own_count = dec_cache.shape[1]
    owners = blk_index * own_count + jnp.arange(own_count, dtype=jnp.int32)
    chooser = (arrival_order[None, :] == owners[:, None]).astype(jnp.bfloat16)
    own_dec_q = jnp.dot(chooser, every_dec_q, preferred_element_type=jnp.float32).astype(
        jnp.bfloat16
    )
    own_new = (
        jnp.dot(chooser, every_dec_new, preferred_element_type=jnp.float32)
        .astype(jnp.bfloat16)
        .reshape(own_count, 2, key_width)
    )
    dec_q = rotate(
        own_dec_q.reshape(own_count, q_heads, HEAD_DIM).astype(jnp.float32), dec_len
    ).astype(jnp.bfloat16)
    dec_q = dec_q.reshape(own_count, kv_heads, group_size, HEAD_DIM)
    dec_key = rotate(
        own_new[:, 0].reshape(own_count, kv_heads, HEAD_DIM).astype(jnp.float32), dec_len
    ).astype(jnp.bfloat16)
    new_value = own_new[:, 1].reshape(own_count, kv_heads, HEAD_DIM)
    cache_slots = dec_cache.shape[2]
    cache_keys = dec_cache[0].reshape(own_count, cache_slots, kv_heads, HEAD_DIM)
    cache_values = dec_cache[1].reshape(own_count, cache_slots, kv_heads, HEAD_DIM)
    cache_scores = (
        jnp.einsum("nkgd,nmkd->nkgm", dec_q, cache_keys, preferred_element_type=jnp.float32)
        * score_scale
    )
    slot_ids = jnp.arange(cache_slots, dtype=jnp.int32)
    live_slots = slot_ids[None, :] < dec_len[:, None]
    cache_scores = jnp.where(live_slots[:, None, None, :], cache_scores, MASKED_SCORE)
    own_score = (
        jnp.einsum("nkgd,nkd->nkg", dec_q, dec_key, preferred_element_type=jnp.float32)
        * score_scale
    )
    dec_top = jnp.maximum(jnp.max(cache_scores, axis=-1), own_score)
    cache_weights = jnp.exp(cache_scores - dec_top[..., None])
    own_weight = jnp.exp(own_score - dec_top)
    dec_total = jnp.sum(cache_weights, axis=-1) + own_weight
    dec_mix = jnp.einsum(
        "nkgm,nmkd->nkgd",
        cache_weights.astype(jnp.bfloat16),
        cache_values,
        preferred_element_type=jnp.float32,
    )
    dec_mix = (
        dec_mix
        + own_weight.astype(jnp.bfloat16).astype(jnp.float32)[..., None]
        * new_value.astype(jnp.float32)[:, :, None, :]
    )
    dec_out = (
        (dec_mix / dec_total[..., None]).reshape(own_count, q_heads * HEAD_DIM).astype(jnp.bfloat16)
    )
    return (long_out, dec_out)


def solution(mesh):
    in_specs = (
        P("blk", "head"),
        P(None, "blk", "head"),
        P(None, None, None, "head"),
        P(None, "blk", "head"),
        P(),
        P(),
        P(("blk", "head"), None),
        P(("blk", "head"), None, None),
        P(None, "blk", None, "head"),
        P("blk"),
        P(),
    )
    out_specs = (P("blk", "head"), P("blk", "head"))
    return jax.shard_map(shards, mesh=mesh, in_specs=in_specs, out_specs=out_specs, check_vma=False)
```

profile of v0, /device:TPU:0, one launch (start us, length us, event | category | flops | bytes accessed | tf_op | source)
XLA Modules:
  0.0 207.1 jit_solution(9990801721509212565)
XLA Ops:
  0.7 1.5 copy.59
  2.2 3.0 %collective-permute-start = (bf16[2,1024,256]{1,2,0:T(8,128)(2,1)S(1)}, bf16[2,1024,256]{1,2,0:T(8,128)(2,1)}, u32[]{:S(2)}, u32[]{:S(2)}) collective-permute-start(bf16[2,1024,256]{1,2,0:T(8,128)(2,1)S(1)} %copy.59), channel_id=1, source_target_pairs={{0,4},{4,0},{8,12},{12,8},{16,20},{20,16},{24,28},{28,24},{1,5},{5... | collective-permute-start | bytes 3145736 | tf_op jit(solution)/shard_map/ppermute | solution.py:29
  9.8 3.8 %all-to-all-start.1 = ((bf16[1,2,4,256]{3,1,0,2:T(2,128)(2,1)}), bf16[1,2,4,256]{3,1,0,2:T(2,128)(2,1)}, u32[]{:S(2)}, u32[]{:S(2)}) async-start(bf16[1,2,4,256]{3,1,0,2:T(2,128)(2,1)} %bitcast.27), calls=%async_computation.1 | async-start | bytes 8192 | tf_op jit(solution)/shard_map/all_to_all | solution.py:167
  18.7 1.8 fusion.61
  22.2 2.4 %compare_and_fusion = pred[128,4096]{0,1:T(8,128)(4,1)} fusion(s32[128]{0:T(128)S(1)} %copy-done.18, s32[4096]{0:T(1024)S(1)} %add_select_fusion, pred[4096]{0:T(1024)(128)(4,1)S(1)} %copy-done.14), kind=kLoop, calls=%fused_computation.35 | loop fusion | flops 1048576 | bytes 545280 | tf_op jit(solution)/shard_map/and | solution.py:152
  25.1 1.4 copy.58
  26.5 1.4 copy.65
  28.0 1.4 copy.83
  29.3 1.3 copy.82
  31.2 1.4 reduce
  33.2 6.9 %concatenate.47 = pred[128,4612]{0,1:T(8,128)(4,1)} concatenate(pred[128,4]{0,1:T(4,128)(4,1)S(1)} %broadcast_in_dim.45, pred[128,4096]{0,1:T(8,128)(4,1)S(1)} %copy-done.2, pred[128,512]{0,1:T(8,128)(4,1)} %iota_compare_fusion), dimensions={1} | concatenate | bytes 1180672 | tf_op jit(solution)/shard_map/concatenate | solution.py:154
  40.1 3.3 %all-to-all-start = ((bf16[4,2,512]{2,1,0:T(2,128)(2,1)}), bf16[4,2,512]{2,1,0:T(2,128)(2,1)S(1)}, u32[]{:S(2)}, u32[]{:S(2)}) async-start(bf16[4,2,512]{2,1,0:T(2,128)(2,1)} %reshape.247), calls=%async_computation | async-start | bytes 16384 | tf_op jit(solution)/shard_map/all_to_all | solution.py:166
  44.1 31.2 %all-gather.1 = bf16[8,4,512]{2,1,0:T(4,128)(2,1)S(1)} all-gather(bf16[1,4,512]{2,1,0:T(4,128)(2,1)S(1)} %reshape.240), channel_id=1, replica_groups=mesh['blk'=8,'head'=4] {'blk'}, dimensions={0}, use_global_device_ids=true | all-gather | bytes 36864 | tf_op jit(solution)/shard_map/all_gather | solution.py:173
  76.3 30.9 %all-gather = bf16[1,1,32,1024]{3,1,0,2:T(2,128)(2,1)S(1)} all-gather(bf16[1,1,4,1024]{3,1,0,2:T(2,128)(2,1)S(1)} %bitcast.102), channel_id=2, replica_groups=mesh['blk'=8,'head'=4] {'blk'}, dimensions={2}, use_global_device_ids=true | all-gather | bytes 73728 | tf_op jit(solution)/shard_map/all_gather | solution.py:172
  107.4 1.4 broadcast_select_fusion.3
  108.9 1.6 pad_maximum_fusion.1
  112.3 2.1 %collective-permute-start.3 = (bf16[2,256,256]{1,2,0:T(8,128)(2,1)S(1)}, bf16[2,256,256]{1,2,0:T(8,128)(2,1)}, u32[]{:S(2)}, u32[]{:S(2)}) collective-permute-start(bf16[2,256,256]{1,2,0:T(8,128)(2,1)S(1)} %pad_maximum_fusion.3), channel_id=1, source_target_pairs={{0,8},{8,0},{4,12},{12,4},{16,24},{24,16},{20,28},{28,20},{1,9},{9... | collective-permute-start | bytes 786440 | tf_op jit(solution)/shard_map/ppermute | solution.py:29
  115.4 36.1 %collective-permute-done.3 = bf16[2,256,256]{1,2,0:T(8,128)(2,1)} collective-permute-done((bf16[2,256,256]{1,2,0:T(8,128)(2,1)S(1)}, bf16[2,256,256]{1,2,0:T(8,128)(2,1)}, u32[]{:S(2)}, u32[]{:S(2)}) %collective-permute-start.3) | collective-permute-done | bytes 262176 | tf_op jit(solution)/shard_map/ppermute | solution.py:29
  152.6 2.7 %broadcast_select_fusion = (bf16[2,2048,256]{1,2,0:T(8,128)(2,1)S(1)}, bf16[2,2048,256]{1,2,0:T(8,128)(2,1)S(1)}) fusion(bf16[2,2048,256]{1,2,0:T(8,128)(2,1)} %collective-permute-done.1, pred[]{:T(512)S(6)} %eq.25, bf16[2,1024,256]{1,2,0:T(8,128)(2,1)S(1)} %get-tuple-element.86, bf16[2,1024,256]{1,2,0:T(8,128)(2,1)S(1)} %get-tuple-element.85), kind=kLoop, calls=%fused_computation.33 | loop fusion | flops 6291456 | bytes 8388609 | tf_op jit(solution)/shard_map/jit(_where)/select_n | solution.py:79
  155.3 1.5 pad_maximum_fusion
  156.8 4.1 %concatenate.56 = bf16[4612,2,128]{0,2,1:T(8,128)(2,1)} concatenate(bf16[4,2,128]{0,2,1:T(8,128)(2,1)S(1)} %bitcast.99, bf16[4096,2,128]{0,2,1:T(8,128)(2,1)S(1)} %bitcast.88, bf16[512,2,128]{0,2,1:T(8,128)(2,1)S(1)} %bitcast.93), dimensions={0} | concatenate | bytes 4722688 | tf_op jit(solution)/shard_map/concatenate | solution.py:135
  160.9 3.9 %copy.66 = bf16[2,4612,128]{2,1,0:T(8,128)(2,1)S(1)} copy(bf16[2,4612,128]{1,2,0:T(8,128)(2,1)} %bitcast.85) | data formatting | bytes 4722688 | tf_op jit(solution)/shard_map/while | solution.py:69
  164.7 5.8 %concatenate.57 = bf16[4612,2,128]{0,2,1:T(8,128)(2,1)} concatenate(bf16[4,2,128]{0,2,1:T(8,128)(2,1)S(1)} %bitcast.100, bf16[4096,2,128]{0,2,1:T(8,128)(2,1)} %bitcast.87, bf16[512,2,128]{0,2,1:T(8,128)(2,1)S(1)} %bitcast.92), dimensions={0} | concatenate | bytes 4722688 | tf_op jit(solution)/shard_map/concatenate | solution.py:143
  170.5 4.4 %copy.67 = bf16[2,4612,128]{2,1,0:T(8,128)(2,1)} copy(bf16[2,4612,128]{1,2,0:T(8,128)(2,1)} %bitcast.86) | data formatting | bytes 4722688 | tf_op jit(solution)/shard_map/while | solution.py:69
  174.9 29.9 %while.12 = (s32[]{:T(128)}, f32[2,128,4]{1,2,0:T(4,128)S(1)}, f32[2,128,4,128]{3,1,2,0:T(8,128)}, pred[128,4612]{0,1:T(8,128)(4,1)S(1)}, bf16[2,128,4,128]{3,1,...) while((s32[]{:T(128)}, f32[2,128,4]{1,2,0:T(4,128)S(1)}, ...), condition=%wide.region_3.4_spmd, body=%wide.region_0.3_spmd.sunk | while | flops 1225542144 | bytes 55367348 | solution.py:69
  174.9 1.4 fusion.78
  176.3 6.6 %fusion.79 = (f32[128,4]{0,1:T(4,128)S(1)}, f32[128,4,4612]{0,2,1:T(8,128)}) fusion(pred[128,4612]{0,1:T(8,128)(4,1)S(1)} %get-tuple-element.185, f32[128,4,4612]{0,2,1:T(8,128)S(1)} %fusion.78), kind=kOutput, calls=%fused_computation.6.clone.1 | output fusion | flops 11811331 | bytes 19483136 | tf_op jit(solution)/shard_map/while/body/eval_jaxpr/sub | solution.py:59
  182.9 6.0 %fusion.80 = f32[2,128,4,128]{3,1,2,0:T(8,128)S(1)} fusion(f32[2,128,4,128]{3,1,2,0:T(8,128)S(1)} %copy-done.7, s32[]{:T(128)S(6)} %copy.103, bf16[2,4612,128]{2,1,0:T(8,128)(2,1)S(1)} %copy-done.1, f32[128,4,4612]{0,2,1:T(8,128)} %get-tuple-element.165, pred[128,4612]{0,1:T(8,128)(4,1)S(1)} %get-tuple-element.185), kind=kOutput, calls=%fused_computation.19.clone.1 | convolution fusion | flops 609226752 | bytes 11481088 | tf_op jit(solution)/shard_map/while/body/eval_jaxpr/ngm,md->ngd/dot_general | solution.py:61
  189.8 1.4 fusion.78
  191.3 6.6 %fusion.79 = (f32[128,4]{0,1:T(4,128)S(1)}, f32[128,4,4612]{0,2,1:T(8,128)}) fusion(pred[128,4612]{0,1:T(8,128)(4,1)S(1)} %get-tuple-element.185, f32[128,4,4612]{0,2,1:T(8,128)S(1)} %fusion.78), kind=kOutput, calls=%fused_computation.6.clone.1 | output fusion | flops 11811331 | bytes 19483136 | tf_op jit(solution)/shard_map/while/body/eval_jaxpr/sub | solution.py:59
  197.9 6.0 %fusion.80 = f32[2,128,4,128]{3,1,2,0:T(8,128)S(1)} fusion(f32[2,128,4,128]{3,1,2,0:T(8,128)S(1)} %copy-done.7, s32[]{:T(128)S(6)} %copy.103, bf16[2,4612,128]{2,1,0:T(8,128)(2,1)S(1)} %copy-done.1, f32[128,4,4612]{0,2,1:T(8,128)} %get-tuple-element.165, pred[128,4612]{0,1:T(8,128)(4,1)S(1)} %get-tuple-element.185), kind=kOutput, calls=%fused_computation.19.clone.1 | convolution fusion | flops 609226752 | bytes 11481088 | tf_op jit(solution)/shard_map/while/body/eval_jaxpr/ngm,md->ngd/dot_general | solution.py:61
  204.7 1.2 fusion.40
  (125 shorter events, 20.9 us)
Async XLA Ops:
  0.6 5.7 %copy-start.22 = (s32[2]{0:T(128)S(1)}, s32[2]{0:T(128)}, u32[]{:S(2)}) copy-start(s32[2]{0:T(128)} %param.17) | copy-start | bytes 28
  0.6 12.9 %copy-start.23 = (s32[2]{0:T(128)S(1)}, s32[2]{0:T(128)}, u32[]{:S(2)}) copy-start(s32[2]{0:T(128)} %param.18) | copy-start | bytes 28
  0.7 15.4 %copy-start.21 = (s32[4]{0:T(128)S(1)}, s32[4]{0:T(128)}, u32[]{:S(2)}) copy-start(s32[4]{0:T(128)} %param.22) | copy-start | bytes 52
  0.7 16.7 %copy-start.11 = (bf16[128,1024]{1,0:T(8,128)(2,1)S(1)}, bf16[128,1024]{1,0:T(8,128)(2,1)}, u32[]{:S(2)}) copy-start(bf16[128,1024]{1,0:T(8,128)(2,1)} %param.13) | copy-start | bytes 786436
  2.2 105.2 %collective-permute-start = (bf16[2,1024,256]{1,2,0:T(8,128)(2,1)S(1)}, bf16[2,1024,256]{1,2,0:T(8,128)(2,1)}, u32[]{:S(2)}, u32[]{:S(2)}) collective-permute-start(bf16[2,1024,256]{1,2,0:T(8,128)(2,1)S(1)} %copy.59), channel_id=1, source_target_pairs={{0,4},{4,0},{8,12},{12,8},{16,20},{20,16},{24,28},{28,24},{1,5},{5... | collective-permute-start | bytes 3145736 | tf_op jit(solution)/shard_map/ppermute | solution.py:29
  5.2 13.4 %copy-start.16 = (f32[64]{0:T(128)}, f32[64]{0:T(128)S(1)}, u32[]{:S(2)}) copy-start(f32[64]{0:T(128)S(1)} %negate_power_fusion) | copy-start | bytes 772
  9.7 101.6 %collective-permute-start.2 = (bf16[2,128,256]{1,2,0:T(8,128)(2,1)}, bf16[2,128,256]{1,2,0:T(8,128)(2,1)}, u32[]{:S(2)}, u32[]{:S(2)}) collective-permute-start(bf16[2,128,256]{1,2,0:T(8,128)(2,1)} %pad_maximum_fusion.4), channel_id=1, source_target_pairs={{0,4},{4,0},{8,12},{12,8},{16,20},{20,16},{24,28},{28,24},{1,5},{5... | collective-permute-start | bytes 393224 | tf_op jit(solution)/shard_map/ppermute | solution.py:29
  9.8 30.3 %all-to-all-start.1 = ((bf16[1,2,4,256]{3,1,0,2:T(2,128)(2,1)}), bf16[1,2,4,256]{3,1,0,2:T(2,128)(2,1)}, u32[]{:S(2)}, u32[]{:S(2)}) async-start(bf16[1,2,4,256]{3,1,0,2:T(2,128)(2,1)} %bitcast.27), calls=%async_computation.1 | async-start | bytes 8192 | tf_op jit(solution)/shard_map/all_to_all | solution.py:167
  18.7 1.8 copy-start.17
  18.7 2.5 %copy-start.3 = (f32[128,8,64]{2,1,0:T(8,128)S(1)}, f32[128,8,64]{2,1,0:T(8,128)}, u32[]{:S(2)}) copy-start(f32[128,8,64]{2,1,0:T(8,128)} %get-tuple-element.93) | copy-start | bytes 786436
  18.7 2.5 %copy-start.4 = (f32[128,8,64]{2,1,0:T(8,128)S(1)}, f32[128,8,64]{2,1,0:T(8,128)}, u32[]{:S(2)}) copy-start(f32[128,8,64]{2,1,0:T(8,128)} %get-tuple-element.94) | copy-start | bytes 786436
  18.7 2.9 %copy-start.20 = (bf16[2,2,4,256]{3,2,1,0:T(4,128)(2,1)S(1)}, bf16[2,2,4,256]{3,2,1,0:T(4,128)(2,1)}, u32[]{:S(2)}) copy-start(bf16[2,2,4,256]{3,2,1,0:T(4,128)(2,1)} %param.15) | copy-start | bytes 24580
  18.7 3.5 %copy-start.14 = (pred[4096]{0:T(1024)(128)(4,1)S(1)}, pred[4096]{0:T(1024)(128)(4,1)}, u32[]{:S(2)}) copy-start(pred[4096]{0:T(1024)(128)(4,1)} %broadcast_compare_fusion) | copy-start | bytes 12292
  18.7 3.5 %copy-start.18 = (s32[128]{0:T(128)S(1)}, s32[128]{0:T(128)}, u32[]{:S(2)}) copy-start(s32[128]{0:T(128)} %get-tuple-element.118) | copy-start | bytes 1540
  28.0 47.3 %copy-start.24 = (s32[32]{0:T(128)S(1)}, s32[32]{0:T(128)}, u32[]{:S(2)}) copy-start(s32[32]{0:T(128)} %param.23) | copy-start | bytes 388
  28.0 47.6 %copy-start.12 = (f32[4,64]{1,0:T(4,128)S(1)}, f32[4,64]{1,0:T(4,128)}, u32[]{:S(2)}) copy-start(f32[4,64]{1,0:T(4,128)} %get-tuple-element.111) | copy-start | bytes 3076
  28.0 47.6 %copy-start.13 = (f32[4,64]{1,0:T(4,128)S(1)}, f32[4,64]{1,0:T(4,128)}, u32[]{:S(2)}) copy-start(f32[4,64]{1,0:T(4,128)} %get-tuple-element.112) | copy-start | bytes 3076
  29.3 3.9 %copy-start.2 = (pred[128,4096]{0,1:T(8,128)(4,1)S(1)}, pred[128,4096]{0,1:T(8,128)(4,1)}, u32[]{:S(2)}) copy-start(pred[128,4096]{0,1:T(8,128)(4,1)} %compare_and_fusion) | copy-start | bytes 1572868
  29.3 46.0 %copy-start.26 = (s32[4]{0:T(128)S(1)}, s32[4]{0:T(128)}, u32[]{:S(2)}) copy-start(s32[4]{0:T(128)} %iota_add_fusion) | copy-start | bytes 52
  29.3 77.9 %copy-start.25 = (s32[32]{0:T(128)S(1)}, s32[32]{0:T(128)}, u32[]{:S(2)}) copy-start(s32[32]{0:T(128)} %param.23) | copy-start | bytes 388
  40.1 36.2 %all-to-all-start = ((bf16[4,2,512]{2,1,0:T(2,128)(2,1)}), bf16[4,2,512]{2,1,0:T(2,128)(2,1)S(1)}, u32[]{:S(2)}, u32[]{:S(2)}) async-start(bf16[4,2,512]{2,1,0:T(2,128)(2,1)} %reshape.247), calls=%async_computation | async-start | bytes 16384 | tf_op jit(solution)/shard_map/all_to_all | solution.py:166
  108.8 1.9 copy-start
  108.8 1.9 copy-start.15
  108.8 5.5 %copy-start.5 = (bf16[1,4,512,256]{2,3,1,0:T(8,128)(2,1)S(1)}, bf16[1,4,512,256]{2,3,1,0:T(8,128)(2,1)}, u32[]{:S(2)}) copy-start(bf16[1,4,512,256]{2,3,1,0:T(8,128)(2,1)} %copy.83) | copy-start | bytes 3145732
  110.4 42.2 %collective-permute-start.1 = (bf16[2,2048,256]{1,2,0:T(8,128)(2,1)}, bf16[2,2048,256]{1,2,0:T(8,128)(2,1)}, u32[]{:S(2)}, u32[]{:S(2)}) collective-permute-start(bf16[2,2048,256]{1,2,0:T(8,128)(2,1)} %pad_maximum_fusion.1), channel_id=1, source_target_pairs={{0,8},{8,0},{4,12},{12,4},{16,24},{24,16},{20,28},{28,20},{1,9},{9... | collective-permute-start | bytes 6291464 | tf_op jit(solution)/shard_map/ppermute | solution.py:29
  112.3 39.2 %collective-permute-start.3 = (bf16[2,256,256]{1,2,0:T(8,128)(2,1)S(1)}, bf16[2,256,256]{1,2,0:T(8,128)(2,1)}, u32[]{:S(2)}, u32[]{:S(2)}) collective-permute-start(bf16[2,256,256]{1,2,0:T(8,128)(2,1)S(1)} %pad_maximum_fusion.3), channel_id=1, source_target_pairs={{0,8},{8,0},{4,12},{12,4},{16,24},{24,16},{20,28},{28,20},{1,9},{9... | collective-permute-start | bytes 786440 | tf_op jit(solution)/shard_map/ppermute | solution.py:29
  160.9 3.9 %copy-start.10 = (bf16[1,1,4,256]{2,3,1,0:T(8,128)(2,1)S(1)}, bf16[1,1,4,256]{2,3,1,0:T(8,128)(2,1)}, u32[]{:S(2)}) copy-start(bf16[1,1,4,256]{2,3,1,0:T(8,128)(2,1)} %copy.65) | copy-start | bytes 6148
  170.5 4.4 %copy-start.6 = (pred[128,4612]{0,1:T(8,128)(4,1)S(1)}, pred[128,4612]{0,1:T(8,128)(4,1)}, u32[]{:S(2)}) copy-start(pred[128,4612]{0,1:T(8,128)(4,1)} %concatenate.47) | copy-start | bytes 1771012
  176.3 6.6 %copy-start.1 = (bf16[2,4612,128]{2,1,0:T(8,128)(2,1)S(1)}, bf16[2,4612,128]{2,1,0:T(8,128)(2,1)}, u32[]{:S(2)}) copy-start(bf16[2,4612,128]{2,1,0:T(8,128)(2,1)} %get-tuple-element.188) | copy-start | bytes 7084036 | tf_op jit(solution)/shard_map/while
  176.3 6.6 %copy-start.7 = (f32[2,128,4,128]{3,1,2,0:T(8,128)S(1)}, f32[2,128,4,128]{3,1,2,0:T(8,128)}, u32[]{:S(2)}) copy-start(f32[2,128,4,128]{3,1,2,0:T(8,128)} %get-tuple-element.176) | copy-start | bytes 1572868 | tf_op jit(solution)/shard_map/while
  191.2 6.6 %copy-start.1 = (bf16[2,4612,128]{2,1,0:T(8,128)(2,1)S(1)}, bf16[2,4612,128]{2,1,0:T(8,128)(2,1)}, u32[]{:S(2)}) copy-start(bf16[2,4612,128]{2,1,0:T(8,128)(2,1)} %get-tuple-element.188) | copy-start | bytes 7084036 | tf_op jit(solution)/shard_map/while
  191.2 6.6 %copy-start.7 = (f32[2,128,4,128]{3,1,2,0:T(8,128)S(1)}, f32[2,128,4,128]{3,1,2,0:T(8,128)}, u32[]{:S(2)}) copy-start(f32[2,128,4,128]{3,1,2,0:T(8,128)} %get-tuple-element.176) | copy-start | bytes 1572868 | tf_op jit(solution)/shard_map/while
  (4 other events, 4.9 us)
where the time goes:
time: 208 us; the launch traced here: 207 us
  blocking collectives  62.1 us (30%)
  local copies, waits for them, and re-layouts  42.5 us (20%)
  other arithmetic  36.1 us (17%)
  waiting for transfers between devices  36.1 us (17%)
  matrix products  16.3 us (8%)
  starting transfers between devices  12.2 us (6%)
    ppermute x4, waiting for transfers between devices, partner(): return lax.ppermute(block, axis, route)  36.1 us
    all_gather x1, blocking collectives, shards(): lax.all_gather(new_mine.reshape(-1, 2 * key_width), 'blk', axis=0, tiled=...  31.2 us
    all_gather x1, blocking collectives, shards(): lax.all_gather(query_mine.reshape(-1, query_width), 'blk', axis=0, tiled=...  30.9 us
    sub x2, other arithmetic, one_head(): scores - head_top[..., None]  13.2 us
    dot_general x2, matrix products, one_head(): jnp.einsum('ngm,md->ngd', weights.astype(jnp.bfloat16), head_values, pref...  12.1 us
    while x2, local copies, waits for them, and re-layouts, attend_by_head(): lax.map(one_head, (jnp.moveaxis(queries, 1, 0), jnp.moveaxis(key_rows, 1,...  8.24 us
    concatenate x1, local copies, waits for them, and re-layouts, shards(): jnp.concatenate([jnp.ones((own_rows, SINKS), dtype=bool), in_window, caus...  6.88 us
    unnamed x59, local copies, waits for them, and re-layouts  6.39 us
  transfers between devices with their start and end apart: 6, of which 1 were waited for; matrix products, arithmetic and copies ran while one was open for 19% of the time, Pallas kernels for 0%

commit v1 on v0

v1 whole, which is shorter than its diff:
```python
import functools
import math

import jax
import jax.numpy as jnp
from jax import lax
from jax.experimental import pallas as pl
from jax.experimental.pallas import tpu as pltpu
from jax.sharding import PartitionSpec as P

D = 128
W = 4096
SINKS = 4
SPAN = 512
PAD_PARTS = 16
HIDDEN = -1e30
LOG2_SCALE = math.log2(math.e) / math.sqrt(D)
VMEM = pltpu.CompilerParams(vmem_limit_bytes=24 * 1024 * 1024)


def turn(x, cosine, sine):
    return x * cosine + pltpu.roll(x, D // 2, 1) * sine


def split_three(x):
    high = x.astype(jnp.bfloat16)
    rest = x - high.astype(jnp.float32)
    middle = rest.astype(jnp.bfloat16)
    low = (rest - middle.astype(jnp.float32)).astype(jnp.bfloat16)
    return high, middle, low


def angle_tables(length, first_step, frequency):
    half = D // 2
    line = lax.broadcasted_iota(jnp.int32, (half, D), 0)
    lane = lax.broadcasted_iota(jnp.int32, (half, D), 1)
    low = lane < half
    position = length + first_step + line + jnp.where(low, 0, half)
    angle = position.astype(jnp.float32) * frequency
    cosine, sine = jnp.cos(angle), jnp.sin(angle)
    cosine_r, sine_r = pltpu.roll(cosine, half, 1), pltpu.roll(sine, half, 1)
    cosines = [jnp.where(low, cosine, cosine_r), jnp.where(low, cosine_r, cosine)]
    sines = [jnp.where(low, -sine, sine_r), jnp.where(low, -sine_r, sine)]
    return jnp.concatenate(cosines, axis=0), jnp.concatenate(sines, axis=0)


def whereabouts(rows):
    members = SPAN // rows
    blk = lax.axis_index("blk")
    return blk // members, lax.rem(blk, members)


def spread_kernel(query, new_kv, *pieces):
    head_at = lax.axis_index("head")
    width = query.shape[1] // len(pieces)
    kv_width = new_kv.shape[2] // len(pieces)

    def lines(ref, size, at):
        found = ref[:, pl.ds(pl.multiple_of(at * size, D), size)].astype(jnp.float32)
        return [
            found[line : line + 1, low : low + D]
            for line in range(found.shape[0])
            for low in range(0, size, D)
        ]

    for distance, piece in enumerate(pieces):
        at = head_at ^ distance
        found = lines(query, width, at) + lines(new_kv.at[0], kv_width, at)
        found.append(jnp.zeros((PAD_PARTS - len(found), D), jnp.float32))
        piece[...] = jnp.concatenate(found, axis=0).astype(piece.dtype)


def prepare_kernel(
    lengths, new_kv, sinks, values, frequency, near_keys, values_t, cosines, sines, pad
):
    rows = new_kv.shape[1]
    slots = values.shape[1]
    request, place = whereabouts(rows)
    for part in range(cosines.shape[0]):
        first_step = (place ^ part) * rows
        for low in range(0, rows, D):
            lines = slice(low, low + D)
            cosines[part, lines], sines[part, lines] = angle_tables(
                lengths[request], first_step + low, frequency[...]
            )
    for head in range(new_kv.shape[2] // D):
        lanes = slice(head * D, (head + 1) * D)
        key = turn(new_kv[0, :, lanes].astype(jnp.float32), cosines[0], sines[0])
        near_keys[:rows, lanes] = key.astype(jnp.bfloat16)
    for kind in range(2):
        pad[...] = jnp.zeros_like(pad)
        pad[:SINKS, :] = sinks[kind, request].astype(jnp.float32)
        if kind == 0:
            near_keys[rows:, :] = pad[...].astype(jnp.bfloat16)
        else:
            values_t[:, slots + rows :] = pad[...].T.astype(jnp.bfloat16)
    values_t[:, :slots] = values[0].T
    values_t[:, slots : slots + rows] = new_kv[1].T


def attend_kernel(
    part, own, lengths, offsets, query, keys, near_keys, values_t, cosine, sine, out, scores, weights
):
    rows = query.shape[0]
    slots = keys.shape[1]
    kv_heads = keys.shape[2] // D
    group = query.shape[1] // D // kv_heads
    request, place = whereabouts(rows)
    offset, first_slot = offsets[request], place * slots
    filled = jnp.minimum(lengths[request] - SINKS, W)
    first_step = (place ^ part) * rows
    step = first_step + lax.broadcasted_iota(jnp.int32, (D, rows), 1)
    index = lax.broadcasted_iota(jnp.int32, (D, rows), 0)
    masks = []
    for low in range(0, slots, D):
        age = (first_slot + low - offset + index) & (W - 1)
        limit = jnp.where(age < filled, age - filled + W, -1)
        masks.append(jnp.where(limit > step, 0.0, HIDDEN))
    for low in range(0, rows, D):
        masks.append(jnp.where(place * rows + low + index <= step, 0.0, HIDDEN))
    if own:
        masks.append(jnp.where(index < SINKS, 0.0, HIDDEN))
    total = len(masks) * D
    logs = []
    for kv in range(kv_heads):
        lanes = slice(kv * D, (kv + 1) * D)
        turned = []
        for head in range(kv * group, (kv + 1) * group):
            x = query[:, head * D : (head + 1) * D].astype(jnp.float32)
            turned.append(turn(x, cosine[0], sine[0]).astype(jnp.bfloat16))
        block = jnp.concatenate(turned, axis=0)
        top = None
        for number, mask in enumerate(masks):
            low = number * D
            if low < slots:
                chunk = keys[0, low : low + D, lanes]
            else:
                chunk = near_keys[low - slots : low - slots + D, lanes]
            s = lax.dot_general(
                chunk, block, (((1,), (1,)), ((), ())), preferred_element_type=jnp.float32
            )
            s = s + jnp.concatenate([mask] * group, axis=1)
            scores[low : low + D, :] = s
            peak = jnp.max(s.reshape(D // 8, 8, group * rows), axis=0)
            top = peak if top is None else jnp.maximum(top, peak)
        top = jnp.max(top, axis=0, keepdims=True)
        mass = jnp.zeros((8, group * rows), jnp.float32)
        for low in range(0, total, D):
            w = jnp.exp2((scores[low : low + D, :] - top) * LOG2_SCALE)
            mass = mass + jnp.sum(w.reshape(D // 8, 8, group * rows), axis=0)
            weights[low : low + D, :] = w.astype(jnp.bfloat16)
        mass = jnp.sum(mass, axis=0, keepdims=True)
        mix = jnp.dot(
            values_t[lanes, :total], weights[:total, :], preferred_element_type=jnp.float32
        )
        mix = mix * (1.0 / mass)
        log = top * LOG2_SCALE + jnp.log2(mass)
        for j in range(group):
            head = kv * group + j
            out[head * D : (head + 1) * D, :] = mix[:, j * rows : (j + 1) * rows].astype(out.dtype)
            logs.append(log[:, j * rows : (j + 1) * rows])
    log = jnp.concatenate(logs, axis=0)
    heads = len(logs)
    if own:
        out[heads * D :, :] = log
    else:
        pieces = [p.astype(jnp.float32) for p in split_three(log)]
        pieces.append(jnp.zeros_like(log))
        out[heads * D :, :] = jnp.concatenate(pieces, axis=0).astype(out.dtype)


def combine_kernel(own, first, second, third, out):
    rows = out.shape[0]
    heads = out.shape[1] // D
    logs = [own[heads * D :, :]]
    for other in (first, second, third):
        p = other[heads * D :, :].astype(jnp.float32)
        logs.append(p[:heads] + p[heads : 2 * heads] + p[2 * heads : 3 * heads])
    top = functools.reduce(jnp.maximum, logs)
    shares = [jnp.exp2(log - top) for log in logs]
    scale = 1.0 / sum(shares)
    shares = [share * scale for share in shares]
    for head in range(heads):
        lines = slice(head * D, (head + 1) * D)
        mix = own[lines, :] * shares[0][head : head + 1, :]
        for other, share in zip((first, second, third), shares[1:]):
            mix = mix + other[lines, :].astype(jnp.float32) * share[head : head + 1, :]
        out[:, lines] = mix.T.astype(out.dtype)


def decode_kernel(lengths, arrivals, *refs):
    near, (cache, frequency, out, mixed) = refs[: len(refs) - 4], refs[len(refs) - 4 :]
    count = cache.shape[1]
    slots = cache.shape[2]
    kv_heads = cache.shape[3] // D
    heads = out.shape[1] // D
    group = heads // kv_heads
    blk, head_at = lax.axis_index("blk"), lax.axis_index("head")
    head_count = lax.axis_size("head")
    members = len(near)

    def look(i, found):
        owner = arrivals[i] - blk * count
        return tuple(jnp.where(owner == n, i, was) for n, was in enumerate(found))

    found = lax.fori_loop(
        0, arrivals.shape[0], look, (jnp.int32(0),) * count, unroll=8
    )
    head_of = lax.broadcasted_iota(jnp.int32, (heads, D), 0) // group
    for n in range(count):
        away = (found[n] // head_count) ^ blk
        line = (away // members) * head_count + (lax.rem(found[n], head_count) ^ head_at)
        lines = pl.ds(pl.multiple_of(line * PAD_PARTS, PAD_PARTS), PAD_PARTS)
        x = near[0][lines, :]
        for part in range(1, members):
            x = jnp.where(lax.rem(away, members) == part, near[part][lines, :], x)
        x = x.astype(jnp.float32)
        angle = lengths[n].astype(jnp.float32) * frequency[...]
        lane = lax.broadcasted_iota(jnp.int32, angle.shape, 1)
        sine = jnp.sin(angle)
        turned = turn(x, jnp.cos(angle), jnp.where(lane < D // 2, -sine, sine))
        turned = turned.astype(jnp.bfloat16).astype(jnp.float32)
        q = turned[:heads]
        wide = [jnp.where(head_of == kv, q, 0.0) for kv in range(kv_heads)]
        wide = jnp.concatenate(wide, axis=1).astype(jnp.bfloat16)
        new_key = jnp.zeros((heads, D), jnp.float32)
        new_value = jnp.zeros((heads, D), jnp.float32)
        for kv in range(kv_heads):
            key = turned[heads + kv : heads + kv + 1]
            value = x[heads + kv_heads + kv : heads + kv_heads + kv + 1]
            new_key = jnp.where(head_of == kv, key, new_key)
            new_value = jnp.where(head_of == kv, value, new_value)
        s = lax.dot_general(
            wide, cache[0, n], (((1,), (1,)), ((), ())), preferred_element_type=jnp.float32
        )
        slot = lax.broadcasted_iota(jnp.int32, (heads, slots), 1)
        s = jnp.where(slot < lengths[n], s, HIDDEN)
        own_s = jnp.sum(q * new_key, axis=1, keepdims=True)
        top = jnp.maximum(jnp.max(s, axis=1, keepdims=True), own_s)
        w = jnp.exp2((s - top) * LOG2_SCALE)
        own_w = jnp.exp2((own_s - top) * LOG2_SCALE)
        mass = jnp.sum(w, axis=1, keepdims=True) + own_w
        mix = jnp.dot(w.astype(jnp.bfloat16), cache[1, n], preferred_element_type=jnp.float32)
        picked = own_w.astype(jnp.bfloat16).astype(jnp.float32) * new_value
        for kv in range(kv_heads):
            picked = picked + jnp.where(head_of == kv, mix[:, kv * D : (kv + 1) * D], 0.0)
        picked = picked / mass
        for head in range(heads):
            mixed[n : n + 1, head * D : (head + 1) * D] = picked[head : head + 1, :]
    out[...] = mixed[...].astype(out.dtype)


def whole(array):
    return pl.BlockSpec(array.shape, lambda i, rank=array.ndim: (0,) * rank)


def exchange(block, axis, distance):
    count = lax.axis_size(axis)
    return lax.ppermute(block, axis, [(i, i ^ distance) for i in range(count)])


SCALARS = pl.BlockSpec(memory_space=pltpu.SMEM)


def shards(
    long_query,
    long_new_kv,
    sink_kv,
    window,
    long_len,
    long_offset,
    dec_query,
    dec_new_kv,
    dec_cache,
    dec_len,
    arrival_order,
):
    blk_count, head_count = lax.axis_size("blk"), lax.axis_size("head")
    rows, features = long_query.shape
    heads = features // D
    kv_width = long_new_kv.shape[2]
    kv_heads = kv_width // D
    group = heads // kv_heads
    slots = window.shape[1]
    members = SPAN // rows
    own_count = dec_cache.shape[1]

    queries = [long_query] + [exchange(long_query, "blk", part) for part in range(1, members)]

    half = jnp.arange(D, dtype=jnp.int32) % (D // 2)
    frequency = (10000.0 ** (-(half.astype(jnp.float32) * 2.0 / D))).reshape(1, D)

    def call(kernel, out_shape, operands, specs, scratch):
        return pl.pallas_call(
            kernel,
            grid=(1,),
            in_specs=specs,
            out_specs=jax.tree.map(whole, out_shape),
            out_shape=out_shape,
            scratch_shapes=scratch,
            compiler_params=VMEM,
        )(*operands)

    pieces = call(
        spread_kernel,
        (jax.ShapeDtypeStruct((PAD_PARTS, D), jnp.bfloat16),) * head_count,
        (dec_query, dec_new_kv),
        [whole(dec_query), whole(dec_new_kv)],
        [],
    )
    arrived = jnp.concatenate(
        [exchange(piece, "head", r) if r else piece for r, piece in enumerate(pieces)], axis=0
    )
    distance = members
    while distance < blk_count:
        arrived = jnp.concatenate([arrived, exchange(arrived, "blk", distance)], axis=0)
        distance *= 2
    near = [arrived] + [exchange(arrived, "blk", part) for part in range(1, members)]

    table = lambda part: pl.BlockSpec((1, rows, D), lambda i: (part, 0, 0))
    near_keys, values_t, cosines, sines = call(
        prepare_kernel,
        (
            jax.ShapeDtypeStruct((rows + D, kv_width), jnp.bfloat16),
            jax.ShapeDtypeStruct((kv_width, slots + rows + D), jnp.bfloat16),
            jax.ShapeDtypeStruct((members, rows, D), jnp.float32),
            jax.ShapeDtypeStruct((members, rows, D), jnp.float32),
        ),
        (long_len, long_new_kv, sink_kv, window, frequency),
        [
            SCALARS,
            whole(long_new_kv),
            whole(sink_kv),
            pl.BlockSpec((1, slots, kv_width), lambda i: (1, 0, 0)),
            whole(frequency),
        ],
        [pltpu.VMEM((D, kv_width), jnp.float32)],
    )

    def attend(part):
        own = part == 0
        total = slots + rows + D
        if own:
            out = jax.ShapeDtypeStruct((features + heads, rows), jnp.float32)
        else:
            out = jax.ShapeDtypeStruct((features + 4 * heads, rows), jnp.bfloat16)
        return call(
            functools.partial(attend_kernel, part, own),
            out,
            (long_len, long_offset, queries[part], window, near_keys, values_t, cosines, sines),
            [
                SCALARS,
                SCALARS,
                whole(queries[part]),
                pl.BlockSpec((1, slots, kv_width), lambda i: (0, 0, 0)),
                whole(near_keys),
                whole(values_t),
                table(part),
                table(part),
            ],
            [
                pltpu.VMEM((total, group * rows), jnp.float32),
                pltpu.VMEM((total, group * rows), jnp.bfloat16),
            ],
        )

    mine = attend(0)
    others = [exchange(attend(part), "blk", part) for part in range(1, members)]
    long_out = call(
        combine_kernel,
        jax.ShapeDtypeStruct((rows, features), jnp.bfloat16),
        (mine, *others),
        [whole(mine)] + [whole(other) for other in others],
        [],
    )
    dec_out = call(
        decode_kernel,
        jax.ShapeDtypeStruct((own_count, features), jnp.bfloat16),
        (dec_len, arrival_order, *near, dec_cache, frequency),
        [SCALARS, SCALARS] + [whole(a) for a in (*near, dec_cache, frequency)],
        [
            pltpu.VMEM((own_count, features), jnp.float32),
        ],
    )
    return (long_out, dec_out)


def solution(mesh):
    in_specs = (
        P("blk", "head"),
        P(None, "blk", "head"),
        P(None, None, None, "head"),
        P(None, "blk", "head"),
        P(),
        P(),
        P(("blk", "head"), None),
        P(("blk", "head"), None, None),
        P(None, "blk", None, "head"),
        P("blk"),
        P(),
    )
    out_specs = (P("blk", "head"), P("blk", "head"))
    return jax.shard_map(shards, mesh=mesh, in_specs=in_specs, out_specs=out_specs, check_vma=False)
```

time: 208 us -> 47.4 us (0.23)
  blocking collectives: 62.1 us -> 0 us
  other arithmetic: 36.1 us -> 0.01 us
  local copies, waits for them, and re-layouts: 42.5 us -> 6.82 us
  waiting for transfers between devices: 36.1 us -> 4.68 us
  Pallas kernels: 0 us -> 16.4 us
  matrix products: 16.3 us -> 0 us
  starting transfers between devices: 12.2 us -> 18.3 us
    all_gather x2 -> x0, blocking collectives: 62.1 us -> none  [the longest x1 31.2 us: shards(): lax.all_gather(new_mine.reshape(-1, 2 * key_width), 'blk', axis=0, tiled=...]
    ppermute x4 -> x13, waiting for transfers between devices: 36.1 us -> 4.68 us  [exchange(): return lax.ppermute(block, axis, [(i, i ^ distance) for i in range(count)])]
    concatenate x3 -> x1, local copies, waits for them, and re-layouts: 16.7 us -> 0.01 us  [shards(): jnp.concatenate([arrived, exchange(arrived, 'blk', distance)], axis=0)]
    pallas_call x0 -> x8, Pallas kernels: none -> 16.4 us  [call(): pl.pallas_call(kernel, grid=(1,), in_specs=specs, out_specs=jax.tree.map(...]
    dot_general x9 -> x0, matrix products: 16.3 us -> none  [the longest x2 12.1 us: one_head(): jnp.einsum('ngm,md->ngd', weights.astype(jnp.bfloat16), head_values, pref...]
    ppermute x4 -> x13, starting transfers between devices: 5.14 us -> 18.3 us  [exchange(): return lax.ppermute(block, axis, [(i, i ^ distance) for i in range(count)])]
    sub x2 -> x0, other arithmetic: 13.2 us -> none  [one_head(): scores - head_top[..., None]]
    while x14 -> x0, local copies, waits for them, and re-layouts: 9.87 us -> none  [the longest x2 8.24 us: attend_by_head(): lax.map(one_head, (jnp.moveaxis(queries, 1, 0), jnp.moveaxis(key_rows, 1,...]
  transfers between devices with their start and end apart: 6 -> 13, of which waited for: 1 -> 1; matrix products, arithmetic and copies ran while one was open for 19% -> 0% of each run, Pallas kernels for 0% -> 33%
where the time goes in v1:
time: 47.4 us; the launch traced here: 47 us
  starting transfers between devices  18.3 us (39%)
  Pallas kernels  16.4 us (35%)
  local copies, waits for them, and re-layouts  6.82 us (14%)
  waiting for transfers between devices  4.68 us (10%)
  between operations  0.8 us (2%)
    ppermute x13, starting transfers between devices, exchange(): return lax.ppermute(block, axis, [(i, i ^ distance) for i in range(count)])  18.3 us
    pallas_call x8, Pallas kernels, call(): pl.pallas_call(kernel, grid=(1,), in_specs=specs, out_specs=jax.tree.map(...  16.4 us
    unnamed x30, local copies, waits for them, and re-layouts  6.81 us
    ppermute x13, waiting for transfers between devices, exchange(): return lax.ppermute(block, axis, [(i, i ^ distance) for i in range(count)])  4.68 us
  transfers between devices with their start and end apart: 13, of which 1 were waited for; matrix products, arithmetic and copies ran while one was open for 0% of the time, Pallas kernels for 33%

profile of v1, /device:TPU:0, one launch (start us, length us, event | category | flops | bytes accessed | tf_op | source)
XLA Modules:
  0.0 47.0 jit_solution(4853626374754226260)
XLA Ops:
  0.6 4.0 %collective-permute-start.4 = (bf16[128,1024]{1,0:T(8,128)(2,1)}, bf16[128,1024]{1,0:T(8,128)(2,1)S(1)}, u32[]{:S(2)}, u32[]{:S(2)}) collective-permute-start(bf16[128,1024]{1,0:T(8,128)(2,1)} %query.2), channel_id=1, source_target_pairs={{0,12},{4,8},{8,4},{12,0},{16,28},{20,24},{24,20},{28,16},{1,13},{... | collective-permute-start | bytes 786440 | tf_op jit(solution)/shard_map/ppermute | solution.py:259
  4.6 0.4 collective-permute-start.2
  5.1 0.7 %copy-done.5 = bf16[1,4096]{1,0:T(2,128)(2,1)S(1)} copy-done((bf16[1,4096]{1,0:T(2,128)(2,1)S(1)}, bf16[1,4096]{1,0:T(2,128)(2,1)}, u32[]{:S(2)}) %copy-start.5) | copy-done | bytes 8216
  5.8 0.7 %copy-done.10 = bf16[1,2,1024]{2,1,0:T(2,128)(2,1)S(1)} copy-done((bf16[1,2,1024]{2,1,0:T(2,128)(2,1)S(1)}, bf16[1,2,1024]{2,1,0:T(2,128)(2,1)}, u32[]{:S(2)}) %copy-start.10) | copy-done | bytes 4120
  6.5 0.1 collective-permute-start.6
  6.6 1.6 %collective-permute-start.7 = (bf16[16,128]{1,0:T(8,128)(2,1)S(1)}, bf16[16,128]{1,0:T(8,128)(2,1)S(1)}, u32[]{:S(2)}, u32[]{:S(2)}) collective-permute-start(bf16[16,128]{1,0:T(8,128)(2,1)S(1)} %get-tuple-element.16), channel_id=1, source_target_pairs={{0,2},{1,3},{2,0},{3,1},{4,6},{5,7},{6,4},{7,5},{8,10},{9,11},{10,... | collective-permute-start | bytes 12296 | tf_op jit(solution)/shard_map/ppermute | solution.py:259
  8.2 0.3 collective-permute-start.8
  8.5 1.2 %copy-done = bf16[2,1024,256]{2,1,0:T(8,128)(2,1)S(1)} copy-done((bf16[2,1024,256]{2,1,0:T(8,128)(2,1)S(1)}, bf16[2,1024,256]{2,1,0:T(8,128)(2,1)}, u32[]{:S(2)}) %copy-start) | copy-done | bytes 1048600
  9.7 0.9 %copy-done.4 = bf16[2,128,256]{2,1,0:T(8,128)(2,1)S(1)} copy-done((bf16[2,128,256]{2,1,0:T(8,128)(2,1)S(1)}, bf16[2,128,256]{2,1,0:T(8,128)(2,1)}, u32[]{:S(2)}) %copy-start.4) | copy-done | bytes 131096
  10.6 0.7 %copy-done.6 = s32[2]{0:T(128)S(1)} copy-done((s32[2]{0:T(128)S(1)}, s32[2]{0:T(128)}, u32[]{:S(2)}) %copy-start.6) | copy-done | bytes 32
  11.3 0.7 %copy-done.7 = bf16[2,2,4,256]{3,2,1,0:T(4,128)(2,1)S(1)} copy-done((bf16[2,2,4,256]{3,2,1,0:T(4,128)(2,1)S(1)}, bf16[2,2,4,256]{3,2,1,0:T(4,128)(2,1)}, u32[]{:S(2)}) %copy-start.7) | copy-done | bytes 8216
  12.0 1.4 %shard_map.122 = (bf16[256,256]{1,0:T(8,128)(2,1)S(1)}, bf16[256,1280]{1,0:T(8,128)(2,1)S(1)}, f32[4,128,128]{2,1,0:T(8,128)S(1)}, f32[4,128,128]{2,1,0:T(8,128)S(1)}) custom-call(s32[2]{0:T(128)S(1)} %copy-done.6, bf16[2,128,256]{2,1,0:T(8,128)(2,1)S(1)} %copy-done.4, bf16[2,2,4,256]{3,2,1,0:T(4,128)(2,1)S(1)} %copy-done.7, ...), custom_call_target="tpu_custom_call" | custom-call | tf_op jit(solution)/shard_map/pallas_call | solution.py:294
  13.3 0.4 collective-permute-start
  13.7 2.9 %collective-permute-start.9 = (bf16[64,128]{1,0:T(8,128)(2,1)S(1)}, bf16[64,128]{1,0:T(8,128)(2,1)S(1)}, u32[]{:S(2)}, u32[]{:S(2)}) collective-permute-start(bf16[64,128]{1,0:T(8,128)(2,1)S(1)} %pad_maximum_fusion), channel_id=1, source_target_pairs={{0,16},{4,20},{8,24},{12,28},{16,0},{20,4},{24,8},{28,12},{1,17},{... | collective-permute-start | bytes 49160 | tf_op jit(solution)/shard_map/ppermute | solution.py:259
  16.6 1.2 %copy-done.1 = bf16[2,1024,256]{2,1,0:T(8,128)(2,1)S(1)} copy-done((bf16[2,1024,256]{2,1,0:T(8,128)(2,1)S(1)}, bf16[2,1024,256]{2,1,0:T(8,128)(2,1)}, u32[]{:S(2)}) %copy-start.1) | copy-done | bytes 1048600
  17.8 0.7 %copy-done.8 = s32[2]{0:T(128)S(1)} copy-done((s32[2]{0:T(128)S(1)}, s32[2]{0:T(128)}, u32[]{:S(2)}) %copy-start.8) | copy-done | bytes 32
  18.5 2.8 %shard_map.126 = bf16[1056,128]{1,0:T(8,128)(2,1)S(1)} custom-call(s32[2]{0:T(128)S(1)} %copy-done.6, s32[2]{0:T(128)S(1)} %copy-done.8, bf16[128,1024]{1,0:T(8,128)(2,1)S(1)} %collective-permute-done.4.query, bf16[2,1024,256]{2,1,0:T(8,128)(2,1)S(1)} %copy-done.1, bf16[256,256]{1,0:T(8,128)(2,1)S(1)} %get-tuple-element.10.near_keys, ...), custom_call_target="tpu_custom_call" | custom-call | tf_op jit(solution)/shard_map/pallas_call | solution.py:294
  21.3 2.6 %collective-permute-start.5 = (bf16[1056,128]{1,0:T(8,128)(2,1)S(1)}, bf16[1056,128]{1,0:T(8,128)(2,1)S(1)}, u32[]{:S(2)}, u32[]{:S(2)}) collective-permute-start(bf16[1056,128]{1,0:T(8,128)(2,1)S(1)} %shard_map.126), channel_id=1, source_target_pairs={{0,12},{4,8},{8,4},{12,0},{16,28},{20,24},{24,20},{28,16},{1,13},{... | collective-permute-start | bytes 811016 | tf_op jit(solution)/shard_map/ppermute | solution.py:259
  23.9 2.8 %shard_map.125 = bf16[1056,128]{1,0:T(8,128)(2,1)S(1)} custom-call(s32[2]{0:T(128)S(1)} %copy-done.6, s32[2]{0:T(128)S(1)} %copy-done.8, bf16[128,1024]{1,0:T(8,128)(2,1)S(1)} %collective-permute-done.2.query, bf16[2,1024,256]{2,1,0:T(8,128)(2,1)S(1)} %copy-done.1, bf16[256,256]{1,0:T(8,128)(2,1)S(1)} %get-tuple-element.10.near_keys, ...), custom_call_target="tpu_custom_call" | custom-call | tf_op jit(solution)/shard_map/pallas_call | solution.py:294
  26.7 0.0 copy-start.9
  26.7 0.5 %collective-permute-start.3 = (bf16[1056,128]{1,0:T(8,128)(2,1)S(1)}, bf16[1056,128]{1,0:T(8,128)(2,1)S(1)}, u32[]{:S(2)}, u32[]{:S(2)}) collective-permute-start(bf16[1056,128]{1,0:T(8,128)(2,1)S(1)} %shard_map.125), channel_id=1, source_target_pairs={{0,8},{4,12},{8,0},{12,4},{16,24},{20,28},{24,16},{28,20},{1,9},{5... | collective-permute-start | bytes 811016 | tf_op jit(solution)/shard_map/ppermute | solution.py:259
  27.2 2.8 %shard_map.124 = bf16[1056,128]{1,0:T(8,128)(2,1)S(1)} custom-call(s32[2]{0:T(128)S(1)} %copy-done.6, s32[2]{0:T(128)S(1)} %copy-done.8, bf16[128,1024]{1,0:T(8,128)(2,1)S(1)} %collective-permute-done.query, bf16[2,1024,256]{2,1,0:T(8,128)(2,1)S(1)} %copy-done.1, bf16[256,256]{1,0:T(8,128)(2,1)S(1)} %get-tuple-element.10.near_keys, ...), custom_call_target="tpu_custom_call" | custom-call | tf_op jit(solution)/shard_map/pallas_call | solution.py:294
  30.0 0.0 copy-start.11
  30.0 0.0 copy-start.12
  30.0 0.6 %collective-permute-start.1 = (bf16[1056,128]{1,0:T(8,128)(2,1)S(1)}, bf16[1056,128]{1,0:T(8,128)(2,1)S(1)}, u32[]{:S(2)}, u32[]{:S(2)}) collective-permute-start(bf16[1056,128]{1,0:T(8,128)(2,1)S(1)} %shard_map.124), channel_id=1, source_target_pairs={{0,4},{4,0},{8,12},{12,8},{16,20},{20,16},{24,28},{28,24},{1,5},{5... | collective-permute-start | bytes 811016 | tf_op jit(solution)/shard_map/ppermute | solution.py:259
  30.7 1.5 %collective-permute-start.10 = (bf16[128,128]{1,0:T(8,128)(2,1)S(1)}, bf16[128,128]{1,0:T(8,128)(2,1)S(1)}, u32[]{:S(2)}, u32[]{:S(2)}) collective-permute-start(bf16[128,128]{1,0:T(8,128)(2,1)S(1)} %constant_dynamic-update-slice_fusion.refs_0_), channel_id=1, source_target_pairs={{0,4},{4,0},{8,12},{12,8},{16,20},{20,16},{24,28},{28,24},{1,5},{5... | collective-permute-start | bytes 98312 | tf_op jit(solution)/shard_map/ppermute | solution.py:259
  32.2 1.6 %collective-permute-start.11 = (bf16[128,128]{1,0:T(8,128)(2,1)S(1)}, bf16[128,128]{1,0:T(8,128)(2,1)S(1)}, u32[]{:S(2)}, u32[]{:S(2)}) collective-permute-start(bf16[128,128]{1,0:T(8,128)(2,1)S(1)} %constant_dynamic-update-slice_fusion.refs_0_), channel_id=1, source_target_pairs={{0,8},{4,12},{8,0},{12,4},{16,24},{20,28},{24,16},{28,20},{1,9},{5... | collective-permute-start | bytes 98312 | tf_op jit(solution)/shard_map/ppermute | solution.py:259
  33.8 4.6 %collective-permute-done.10.refs_1_ = bf16[128,128]{1,0:T(8,128)(2,1)S(1)} collective-permute-done((bf16[128,128]{1,0:T(8,128)(2,1)S(1)}, bf16[128,128]{1,0:T(8,128)(2,1)S(1)}, u32[]{:S(2)}, u32[]{:S(2)}) %collective-permute-start.10) | collective-permute-done | bytes 32800 | tf_op jit(solution)/shard_map/ppermute | solution.py:259
  38.4 1.9 %collective-permute-start.12 = (bf16[128,128]{1,0:T(8,128)(2,1)S(1)}, bf16[128,128]{1,0:T(8,128)(2,1)S(1)}, u32[]{:S(2)}, u32[]{:S(2)}) collective-permute-start(bf16[128,128]{1,0:T(8,128)(2,1)S(1)} %constant_dynamic-update-slice_fusion.refs_0_), channel_id=1, source_target_pairs={{0,12},{4,8},{8,4},{12,0},{16,28},{20,24},{24,20},{28,16},{1,13},{... | collective-permute-start | bytes 98312 | tf_op jit(solution)/shard_map/ppermute | solution.py:259
  40.3 3.0 %shard_map.123.own = f32[1032,128]{1,0:T(8,128)S(1)} custom-call(s32[2]{0:T(128)S(1)} %copy-done.6, s32[2]{0:T(128)S(1)} %copy-done.9, bf16[128,1024]{1,0:T(8,128)(2,1)S(1)} %copy-done.3, bf16[2,1024,256]{2,1,0:T(8,128)(2,1)S(1)} %copy-done.1, bf16[256,256]{1,0:T(8,128)(2,1)S(1)} %get-tuple-element.10.near_keys, ...), custom_call_target="tpu_custom_call" | custom-call | tf_op jit(solution)/shard_map/pallas_call | solution.py:294
  43.3 2.7 %shard_map.129 = bf16[4,1024]{1,0:T(4,128)(2,1)} custom-call(s32[4]{0:T(128)S(1)} %copy-done.11, s32[32]{0:T(128)S(1)} %copy-done.12, bf16[128,128]{1,0:T(8,128)(2,1)S(1)} %constant_dynamic-update-slice_fusion.refs_0_, bf16[128,128]{1,0:T(8,128)(2,1)S(1)} %collective-permute-done.10.refs_1_, bf16[128,128]{1,0:T(8,128)(2,1)S(1)} %collective-permute-done.11.refs_2_, ...), custom_call_target="tpu_custom_call" | custom-call | tf_op jit(solution)/shard_map/pallas_call | solution.py:294
  46.0 1.0 %shard_map.127 = bf16[128,1024]{1,0:T(8,128)(2,1)} custom-call(f32[1032,128]{1,0:T(8,128)S(1)} %shard_map.123.own, bf16[1056,128]{1,0:T(8,128)(2,1)S(1)} %collective-permute-done.1.first, bf16[1056,128]{1,0:T(8,128)(2,1)S(1)} %collective-permute-done.3.second, bf16[1056,128]{1,0:T(8,128)(2,1)S(1)} %collective-permute-done.5.third), custom_call_target="tpu_custom_call" | custom-call | tf_op jit(solution)/shard_map/pallas_call | solution.py:294
  (35 shorter events, 0.1 us)
Async XLA Ops:
  0.6 16.0 %collective-permute-start.4 = (bf16[128,1024]{1,0:T(8,128)(2,1)}, bf16[128,1024]{1,0:T(8,128)(2,1)S(1)}, u32[]{:S(2)}, u32[]{:S(2)}) collective-permute-start(bf16[128,1024]{1,0:T(8,128)(2,1)} %query.2), channel_id=1, source_target_pairs={{0,12},{4,8},{8,4},{12,0},{16,28},{20,24},{24,20},{28,16},{1,13},{... | collective-permute-start | bytes 786440 | tf_op jit(solution)/shard_map/ppermute | solution.py:259
  4.6 19.2 %collective-permute-start.2 = (bf16[128,1024]{1,0:T(8,128)(2,1)}, bf16[128,1024]{1,0:T(8,128)(2,1)S(1)}, u32[]{:S(2)}, u32[]{:S(2)}) collective-permute-start(bf16[128,1024]{1,0:T(8,128)(2,1)} %query.2), channel_id=1, source_target_pairs={{0,8},{4,12},{8,0},{12,4},{16,24},{20,28},{24,16},{28,20},{1,9},{5... | collective-permute-start | bytes 786440 | tf_op jit(solution)/shard_map/ppermute | solution.py:259
  5.1 0.7 %copy-start.5 = (bf16[1,4096]{1,0:T(2,128)(2,1)S(1)}, bf16[1,4096]{1,0:T(2,128)(2,1)}, u32[]{:S(2)}) copy-start(bf16[1,4096]{1,0:T(2,128)(2,1)} %query.3) | copy-start | bytes 24580
  5.8 0.7 %copy-start.10 = (bf16[1,2,1024]{2,1,0:T(2,128)(2,1)S(1)}, bf16[1,2,1024]{2,1,0:T(2,128)(2,1)}, u32[]{:S(2)}) copy-start(bf16[1,2,1024]{2,1,0:T(2,128)(2,1)} %new_kv.3) | copy-start | bytes 12292
  6.5 6.8 %collective-permute-start.6 = (bf16[16,128]{1,0:T(8,128)(2,1)S(1)}, bf16[16,128]{1,0:T(8,128)(2,1)S(1)}, u32[]{:S(2)}, u32[]{:S(2)}) collective-permute-start(bf16[16,128]{1,0:T(8,128)(2,1)S(1)} %get-tuple-element.15), channel_id=1, source_target_pairs={{0,1},{1,0},{2,3},{3,2},{4,5},{5,4},{6,7},{7,6},{8,9},{9,8},{10,11... | collective-permute-start | bytes 12296 | tf_op jit(solution)/shard_map/ppermute | solution.py:259
  6.6 7.1 %collective-permute-start.7 = (bf16[16,128]{1,0:T(8,128)(2,1)S(1)}, bf16[16,128]{1,0:T(8,128)(2,1)S(1)}, u32[]{:S(2)}, u32[]{:S(2)}) collective-permute-start(bf16[16,128]{1,0:T(8,128)(2,1)S(1)} %get-tuple-element.16), channel_id=1, source_target_pairs={{0,2},{1,3},{2,0},{3,1},{4,6},{5,7},{6,4},{7,5},{8,10},{9,11},{10,... | collective-permute-start | bytes 12296 | tf_op jit(solution)/shard_map/ppermute | solution.py:259
  8.2 5.5 %collective-permute-start.8 = (bf16[16,128]{1,0:T(8,128)(2,1)S(1)}, bf16[16,128]{1,0:T(8,128)(2,1)S(1)}, u32[]{:S(2)}, u32[]{:S(2)}) collective-permute-start(bf16[16,128]{1,0:T(8,128)(2,1)S(1)} %get-tuple-element.17), channel_id=1, source_target_pairs={{0,3},{1,2},{2,1},{3,0},{4,7},{5,6},{6,5},{7,4},{8,11},{9,10},{10,... | collective-permute-start | bytes 12296 | tf_op jit(solution)/shard_map/ppermute | solution.py:259
  8.5 1.2 %copy-start = (bf16[2,1024,256]{2,1,0:T(8,128)(2,1)S(1)}, bf16[2,1024,256]{2,1,0:T(8,128)(2,1)}, u32[]{:S(2)}) copy-start(bf16[2,1024,256]{2,1,0:T(8,128)(2,1)} %keys.7) | copy-start | bytes 3145732
  9.7 0.9 %copy-start.4 = (bf16[2,128,256]{2,1,0:T(8,128)(2,1)S(1)}, bf16[2,128,256]{2,1,0:T(8,128)(2,1)}, u32[]{:S(2)}) copy-start(bf16[2,128,256]{2,1,0:T(8,128)(2,1)} %new_kv.2) | copy-start | bytes 393220
  10.6 0.7 %copy-start.6 = (s32[2]{0:T(128)S(1)}, s32[2]{0:T(128)}, u32[]{:S(2)}) copy-start(s32[2]{0:T(128)} %lengths.10) | copy-start | bytes 28
  11.3 0.7 %copy-start.7 = (bf16[2,2,4,256]{3,2,1,0:T(4,128)(2,1)S(1)}, bf16[2,2,4,256]{3,2,1,0:T(4,128)(2,1)}, u32[]{:S(2)}) copy-start(bf16[2,2,4,256]{3,2,1,0:T(4,128)(2,1)} %sinks.1) | copy-start | bytes 24580
  13.3 13.9 %collective-permute-start = (bf16[128,1024]{1,0:T(8,128)(2,1)}, bf16[128,1024]{1,0:T(8,128)(2,1)S(1)}, u32[]{:S(2)}, u32[]{:S(2)}) collective-permute-start(bf16[128,1024]{1,0:T(8,128)(2,1)} %query.2), channel_id=1, source_target_pairs={{0,4},{4,0},{8,12},{12,8},{16,20},{20,16},{24,28},{28,24},{1,5},{5... | collective-permute-start | bytes 786440 | tf_op jit(solution)/shard_map/ppermute | solution.py:259
  13.7 16.9 %collective-permute-start.9 = (bf16[64,128]{1,0:T(8,128)(2,1)S(1)}, bf16[64,128]{1,0:T(8,128)(2,1)S(1)}, u32[]{:S(2)}, u32[]{:S(2)}) collective-permute-start(bf16[64,128]{1,0:T(8,128)(2,1)S(1)} %pad_maximum_fusion), channel_id=1, source_target_pairs={{0,16},{4,20},{8,24},{12,28},{16,0},{20,4},{24,8},{28,12},{1,17},{... | collective-permute-start | bytes 49160 | tf_op jit(solution)/shard_map/ppermute | solution.py:259
  16.6 1.2 %copy-start.1 = (bf16[2,1024,256]{2,1,0:T(8,128)(2,1)S(1)}, bf16[2,1024,256]{2,1,0:T(8,128)(2,1)}, u32[]{:S(2)}) copy-start(bf16[2,1024,256]{2,1,0:T(8,128)(2,1)} %keys.7) | copy-start | bytes 3145732
  17.8 0.7 %copy-start.8 = (s32[2]{0:T(128)S(1)}, s32[2]{0:T(128)}, u32[]{:S(2)}) copy-start(s32[2]{0:T(128)} %offsets.7) | copy-start | bytes 28
  21.3 24.7 %collective-permute-start.5 = (bf16[1056,128]{1,0:T(8,128)(2,1)S(1)}, bf16[1056,128]{1,0:T(8,128)(2,1)S(1)}, u32[]{:S(2)}, u32[]{:S(2)}) collective-permute-start(bf16[1056,128]{1,0:T(8,128)(2,1)S(1)} %shard_map.126), channel_id=1, source_target_pairs={{0,12},{4,8},{8,4},{12,0},{16,28},{20,24},{24,20},{28,16},{1,13},{... | collective-permute-start | bytes 811016 | tf_op jit(solution)/shard_map/ppermute | solution.py:259
  26.7 13.6 %copy-start.3 = (bf16[128,1024]{1,0:T(8,128)(2,1)S(1)}, bf16[128,1024]{1,0:T(8,128)(2,1)}, u32[]{:S(2)}) copy-start(bf16[128,1024]{1,0:T(8,128)(2,1)} %query.2) | copy-start | bytes 786436
  26.7 13.6 %copy-start.9 = (s32[2]{0:T(128)S(1)}, s32[2]{0:T(128)}, u32[]{:S(2)}) copy-start(s32[2]{0:T(128)} %offsets.7) | copy-start | bytes 28
  26.7 19.3 %collective-permute-start.3 = (bf16[1056,128]{1,0:T(8,128)(2,1)S(1)}, bf16[1056,128]{1,0:T(8,128)(2,1)S(1)}, u32[]{:S(2)}, u32[]{:S(2)}) collective-permute-start(bf16[1056,128]{1,0:T(8,128)(2,1)S(1)} %shard_map.125), channel_id=1, source_target_pairs={{0,8},{4,12},{8,0},{12,4},{16,24},{20,28},{24,16},{28,20},{1,9},{5... | collective-permute-start | bytes 811016 | tf_op jit(solution)/shard_map/ppermute | solution.py:259
  30.0 13.3 %copy-start.2 = (bf16[2,4,512,256]{3,2,1,0:T(8,128)(2,1)S(1)}, bf16[2,4,512,256]{3,2,1,0:T(8,128)(2,1)}, u32[]{:S(2)}) copy-start(bf16[2,4,512,256]{3,2,1,0:T(8,128)(2,1)} %refs_4_.1) | copy-start | bytes 6291460
  30.0 13.3 %copy-start.11 = (s32[4]{0:T(128)S(1)}, s32[4]{0:T(128)}, u32[]{:S(2)}) copy-start(s32[4]{0:T(128)} %lengths.11) | copy-start | bytes 52
  30.0 13.3 %copy-start.12 = (s32[32]{0:T(128)S(1)}, s32[32]{0:T(128)}, u32[]{:S(2)}) copy-start(s32[32]{0:T(128)} %arrivals.1) | copy-start | bytes 388
  30.0 16.0 %collective-permute-start.1 = (bf16[1056,128]{1,0:T(8,128)(2,1)S(1)}, bf16[1056,128]{1,0:T(8,128)(2,1)S(1)}, u32[]{:S(2)}, u32[]{:S(2)}) collective-permute-start(bf16[1056,128]{1,0:T(8,128)(2,1)S(1)} %shard_map.124), channel_id=1, source_target_pairs={{0,4},{4,0},{8,12},{12,8},{16,20},{20,16},{24,28},{28,24},{1,5},{5... | collective-permute-start | bytes 811016 | tf_op jit(solution)/shard_map/ppermute | solution.py:259
  30.7 7.8 %collective-permute-start.10 = (bf16[128,128]{1,0:T(8,128)(2,1)S(1)}, bf16[128,128]{1,0:T(8,128)(2,1)S(1)}, u32[]{:S(2)}, u32[]{:S(2)}) collective-permute-start(bf16[128,128]{1,0:T(8,128)(2,1)S(1)} %constant_dynamic-update-slice_fusion.refs_0_), channel_id=1, source_target_pairs={{0,4},{4,0},{8,12},{12,8},{16,20},{20,16},{24,28},{28,24},{1,5},{5... | collective-permute-start | bytes 98312 | tf_op jit(solution)/shard_map/ppermute | solution.py:259
  32.2 11.1 %collective-permute-start.11 = (bf16[128,128]{1,0:T(8,128)(2,1)S(1)}, bf16[128,128]{1,0:T(8,128)(2,1)S(1)}, u32[]{:S(2)}, u32[]{:S(2)}) collective-permute-start(bf16[128,128]{1,0:T(8,128)(2,1)S(1)} %constant_dynamic-update-slice_fusion.refs_0_), channel_id=1, source_target_pairs={{0,8},{4,12},{8,0},{12,4},{16,24},{20,28},{24,16},{28,20},{1,9},{5... | collective-permute-start | bytes 98312 | tf_op jit(solution)/shard_map/ppermute | solution.py:259
  38.4 4.9 %collective-permute-start.12 = (bf16[128,128]{1,0:T(8,128)(2,1)S(1)}, bf16[128,128]{1,0:T(8,128)(2,1)S(1)}, u32[]{:S(2)}, u32[]{:S(2)}) collective-permute-start(bf16[128,128]{1,0:T(8,128)(2,1)S(1)} %constant_dynamic-update-slice_fusion.refs_0_), channel_id=1, source_target_pairs={{0,12},{4,8},{8,4},{12,0},{16,28},{20,24},{24,20},{28,16},{1,13},{... | collective-permute-start | bytes 98312 | tf_op jit(solution)/shard_map/ppermute | solution.py:259

commit v2 on v1

--- a/solution.py
+++ b/solution.py
@@ -50,7 +50,19 @@
     return blk // members, lax.rem(blk, members)
 
 
-def spread_kernel(query, new_kv, *pieces):
+def fetch(*pairs):
+    copies = [pltpu.make_async_copy(*pair) for pair in pairs]
+    for copy in copies:
+        copy.start()
+    return copies
+
+
+def spread_kernel(query_far, new_kv_far, *refs):
+    pieces, (query, new_kv, arrived) = refs[:-3], refs[-3:]
+    for copy in fetch(
+        (query_far, query, arrived.at[0]), (new_kv_far, new_kv, arrived.at[1])
+    ):
+        copy.wait()
     head_at = lax.axis_index("head")
     width = query.shape[1] // len(pieces)
     kv_width = new_kv.shape[2] // len(pieces)
@@ -71,71 +83,98 @@
 
 
 def prepare_kernel(
-    lengths, new_kv, sinks, values, frequency, near_keys, values_t, cosines, sines, pad
+    lengths_far,
+    offsets_far,
+    new_kv_far,
+    sinks_far,
+    window_far,
+    frequency,
+    keys,
+    values_t,
+    cosines,
+    sines,
+    biases,
+    lengths,
+    offsets,
+    new_kv,
+    sinks,
+    values,
+    pad,
+    arrived,
 ):
     rows = new_kv.shape[1]
-    slots = values.shape[1]
+    slots = values.shape[0]
     request, place = whereabouts(rows)
+    scalars = fetch(
+        (lengths_far, lengths, arrived.at[0]),
+        (offsets_far, offsets, arrived.at[1]),
+    )
+    arrays = fetch(
+        (new_kv_far, new_kv, arrived.at[2]),
+        (sinks_far.at[:, request], sinks, arrived.at[3]),
+        (window_far.at[1], values, arrived.at[4]),
+        (window_far.at[0], keys.at[:slots], arrived.at[5]),
+    )
+    for copy in scalars:
+        copy.wait()
+    length, offset = lengths[request], offsets[request]
+    filled = jnp.minimum(length - SINKS, W)
     for part in range(cosines.shape[0]):
         first_step = (place ^ part) * rows
         for low in range(0, rows, D):
             lines = slice(low, low + D)
             cosines[part, lines], sines[part, lines] = angle_tables(
-                lengths[request], first_step + low, frequency[...]
+                length, first_step + low, frequency[...]
             )
+    index = lax.broadcasted_iota(jnp.int32, (D, rows), 0)
+    step = lax.broadcasted_iota(jnp.int32, (D, rows), 1)
+    for low in range(0, slots, D):
+        age = (place * slots + low - offset + index) & (W - 1)
+        limit = jnp.where(age < filled, age - filled + W, -1)
+        for part in range(biases.shape[0]):
+            seen = limit > (place ^ part) * rows + step
+            biases[part, low : low + D] = jnp.where(seen, 0.0, HIDDEN)
+    for low in range(0, rows, D):
+        for part in range(biases.shape[0]):
+            seen = place * rows + low + index <= (place ^ part) * rows + step
+            biases[part, slots + low : slots + low + D] = jnp.where(seen, 0.0, HIDDEN)
+    for part in range(biases.shape[0]):
+        seen = index < (SINKS if part == 0 else 0)
+        biases[part, slots + rows :] = jnp.where(seen, 0.0, HIDDEN)
+    for copy in arrays:
+        copy.wait()
     for head in range(new_kv.shape[2] // D):
         lanes = slice(head * D, (head + 1) * D)
         key = turn(new_kv[0, :, lanes].astype(jnp.float32), cosines[0], sines[0])
-        near_keys[:rows, lanes] = key.astype(jnp.bfloat16)
+        keys[slots : slots + rows, lanes] = key.astype(jnp.bfloat16)
     for kind in range(2):
         pad[...] = jnp.zeros_like(pad)
-        pad[:SINKS, :] = sinks[kind, request].astype(jnp.float32)
+        pad[:SINKS, :] = sinks[kind].astype(jnp.float32)
         if kind == 0:
-            near_keys[rows:, :] = pad[...].astype(jnp.bfloat16)
+            keys[slots + rows :, :] = pad[...].astype(jnp.bfloat16)
         else:
             values_t[:, slots + rows :] = pad[...].T.astype(jnp.bfloat16)
-    values_t[:, :slots] = values[0].T
+    values_t[:, :slots] = values[...].T
     values_t[:, slots : slots + rows] = new_kv[1].T
 
 
-def attend_kernel(
-    part, own, lengths, offsets, query, keys, near_keys, values_t, cosine, sine, out, scores, weights
-):
+def attend_kernel(part, own, query, keys, values_t, cosine, sine, bias, out, scores, weights):
     rows = query.shape[0]
-    slots = keys.shape[1]
-    kv_heads = keys.shape[2] // D
+    kv_heads = keys.shape[1] // D
     group = query.shape[1] // D // kv_heads
-    request, place = whereabouts(rows)
-    offset, first_slot = offsets[request], place * slots
-    filled = jnp.minimum(lengths[request] - SINKS, W)
-    first_step = (place ^ part) * rows
-    step = first_step + lax.broadcasted_iota(jnp.int32, (D, rows), 1)
-    index = lax.broadcasted_iota(jnp.int32, (D, rows), 0)
-    masks = []
-    for low in range(0, slots, D):
-        age = (first_slot + low - offset + index) & (W - 1)
-        limit = jnp.where(age < filled, age - filled + W, -1)
-        masks.append(jnp.where(limit > step, 0.0, HIDDEN))
-    for low in range(0, rows, D):
-        masks.append(jnp.where(place * rows + low + index <= step, 0.0, HIDDEN))
-    if own:
-        masks.append(jnp.where(index < SINKS, 0.0, HIDDEN))
-    total = len(masks) * D
+    total = keys.shape[0] if own else keys.shape[0] - D
     logs = []
     for kv in range(kv_heads):
         lanes = slice(kv * D, (kv + 1) * D)
         turned = []
         for head in range(kv * group, (kv + 1) * group):
             x = query[:, head * D : (head + 1) * D].astype(jnp.float32)
-            turned.append(turn(x, cosine[0], sine[0]).astype(jnp.bfloat16))
+            turned.append(turn(x, cosine[part], sine[part]).astype(jnp.bfloat16))
         block = jnp.concatenate(turned, axis=0)
         top = None
-        for number, mask in enumerate(masks):
-            low = number * D
-            if low < slots:
-                chunk = keys[0, low : low + D, lanes]
-            else:
-                chunk = near_keys[low - slots : low - slots + D, lanes]
+        for low in range(0, total, D):
+            chunk = keys[low : low + D, lanes]
+            mask = bias[part, low : low + D]
             s = lax.dot_general(
                 chunk, block, (((1,), (1,)), ((), ())), preferred_element_type=jnp.float32
             )
@@ -250,13 +289,15 @@
     out[...] = mixed[...].astype(out.dtype)
 
 
-def whole(array):
-    return pl.BlockSpec(array.shape, lambda i, rank=array.ndim: (0,) * rank)
-
-
 def exchange(block, axis, distance):
     count = lax.axis_size(axis)
     return lax.ppermute(block, axis, [(i, i ^ distance) for i in range(count)])
+
+
+NEAR = pl.BlockSpec(memory_space=pltpu.VMEM)
+FAR = pl.BlockSpec(memory_space=pltpu.MemorySpace.HBM)
+def stay(*arrays):
+    return [pltpu.with_memory_space_constraint(a, pltpu.MemorySpace.HBM) for a in arrays]
 
 
 SCALARS = pl.BlockSpec(memory_space=pltpu.SMEM)
@@ -293,9 +334,8 @@
     def call(kernel, out_shape, operands, specs, scratch):
         return pl.pallas_call(
             kernel,
-            grid=(1,),
             in_specs=specs,
-            out_specs=jax.tree.map(whole, out_shape),
+            out_specs=jax.tree.map(lambda _: NEAR, out_shape),
             out_shape=out_shape,
             scratch_shapes=scratch,
             compiler_params=VMEM,
@@ -304,9 +344,13 @@
     pieces = call(
         spread_kernel,
         (jax.ShapeDtypeStruct((PAD_PARTS, D), jnp.bfloat16),) * head_count,
-        (dec_query, dec_new_kv),
-        [whole(dec_query), whole(dec_new_kv)],
-        [],
+        stay(dec_query, dec_new_kv),
+        [FAR, FAR],
+        [
+            pltpu.VMEM(dec_query.shape, jnp.bfloat16),
+            pltpu.VMEM(dec_new_kv.shape, jnp.bfloat16),
+            pltpu.SemaphoreType.DMA((2,)),
+        ],
     )
     arrived = jnp.concatenate(
         [exchange(piece, "head", r) if r else piece for r, piece in enumerate(pieces)], axis=0
@@ -317,29 +361,31 @@
         distance *= 2
     near = [arrived] + [exchange(arrived, "blk", part) for part in range(1, members)]
 
-    table = lambda part: pl.BlockSpec((1, rows, D), lambda i: (part, 0, 0))
-    near_keys, values_t, cosines, sines = call(
+    total = slots + rows + D
+    shared = call(
         prepare_kernel,
         (
-            jax.ShapeDtypeStruct((rows + D, kv_width), jnp.bfloat16),
-            jax.ShapeDtypeStruct((kv_width, slots + rows + D), jnp.bfloat16),
+            jax.ShapeDtypeStruct((total, kv_width), jnp.bfloat16),
+            jax.ShapeDtypeStruct((kv_width, total), jnp.bfloat16),
             jax.ShapeDtypeStruct((members, rows, D), jnp.float32),
             jax.ShapeDtypeStruct((members, rows, D), jnp.float32),
+            jax.ShapeDtypeStruct((members, total, rows), jnp.float32),
         ),
-        (long_len, long_new_kv, sink_kv, window, frequency),
+        (*stay(long_len, long_offset, long_new_kv, sink_kv, window), frequency),
+        [FAR] * 5 + [NEAR],
         [
-            SCALARS,
-            whole(long_new_kv),
-            whole(sink_kv),
-            pl.BlockSpec((1, slots, kv_width), lambda i: (1, 0, 0)),
-            whole(frequency),
+            pltpu.SMEM(long_len.shape, jnp.int32),
+            pltpu.SMEM(long_offset.shape, jnp.int32),
+            pltpu.VMEM(long_new_kv.shape, jnp.bfloat16),
+            pltpu.VMEM((2, *sink_kv.shape[2:]), jnp.bfloat16),
+            pltpu.VMEM(window.shape[1:], jnp.bfloat16),
+            pltpu.VMEM((D, kv_width), jnp.float32),
+            pltpu.SemaphoreType.DMA((6,)),
         ],
-        [pltpu.VMEM((D, kv_width), jnp.float32)],
     )
 
     def attend(part):
         own = part == 0
-        total = slots + rows + D
         if own:
             out = jax.ShapeDtypeStruct((features + heads, rows), jnp.float32)
         else:
@@ -347,17 +393,8 @@
         return call(
             functools.partial(attend_kernel, part, own),
             out,
-            (long_len, long_offset, queries[part], window, near_keys, values_t, cosines, sines),
-            [
-                SCALARS,
-                SCALARS,
-                whole(queries[part]),
-                pl.BlockSpec((1, slots, kv_width), lambda i: (0, 0, 0)),
-                whole(near_keys),
-                whole(values_t),
-                table(part),
-                table(part),
-            ],
+            (queries[part], *shared),
+            [NEAR] * 6,
             [
                 pltpu.VMEM((total, group * rows), jnp.float32),
                 pltpu.VMEM((total, group * rows), jnp.bfloat16),
@@ -370,14 +407,14 @@
         combine_kernel,
         jax.ShapeDtypeStruct((rows, features), jnp.bfloat16),
         (mine, *others),
-        [whole(mine)] + [whole(other) for other in others],
+        [NEAR] * (1 + len(others)),
         [],
     )
     dec_out = call(
         decode_kernel,
         jax.ShapeDtypeStruct((own_count, features), jnp.bfloat16),
         (dec_len, arrival_order, *near, dec_cache, frequency),
-        [SCALARS, SCALARS] + [whole(a) for a in (*near, dec_cache, frequency)],
+        [SCALARS, SCALARS] + [NEAR] * (len(near) + 2),
         [
             pltpu.VMEM((own_count, features), jnp.float32),
         ],

time: 47.4 us -> 41.4 us (0.87)
  the two profiles are of different devices: /device:TPU:0 before, /device:TPU:20 now
where the time goes in v2:
time: 41.4 us; the launch traced here: 41.1 us
  starting transfers between devices  15.8 us (38%)
  Pallas kernels  15.6 us (38%)
  waiting for transfers between devices  8.88 us (21%)
  between operations  0.77 us (2%)
    ppermute x13, starting transfers between devices, exchange(): return lax.ppermute(block, axis, [(i, i ^ distance) for i in range(count)])  15.8 us
    pallas_call x8, Pallas kernels, call(): pl.pallas_call(kernel, in_specs=specs, out_specs=jax.tree.map(lambda _: N...  15.6 us
    ppermute x13, waiting for transfers between devices, exchange(): return lax.ppermute(block, axis, [(i, i ^ distance) for i in range(count)])  8.88 us
  transfers between devices with their start and end apart: 13, of which 5 were waited for; matrix products, arithmetic and copies ran while one was open for 0% of the time, Pallas kernels for 35%

profile of v2, /device:TPU:20, one launch (start us, length us, event | category | flops | bytes accessed | tf_op | source)
XLA Modules:
  0.0 41.1 jit_solution(1097861359634707054)
XLA Ops:
  0.6 2.6 %collective-permute-start.4 = (bf16[128,1024]{1,0:T(8,128)(2,1)}, bf16[128,1024]{1,0:T(8,128)(2,1)S(1)}, u32[]{:S(2)}, u32[]{:S(2)}) collective-permute-start(bf16[128,1024]{1,0:T(8,128)(2,1)} %query.1), channel_id=1, source_target_pairs={{0,12},{4,8},{8,4},{12,0},{16,28},{20,24},{24,20},{28,16},{1,13},{... | collective-permute-start | bytes 786440 | tf_op jit(solution)/shard_map/ppermute | solution.py:294
  3.2 0.4 %collective-permute-start.2 = (bf16[128,1024]{1,0:T(8,128)(2,1)}, bf16[128,1024]{1,0:T(8,128)(2,1)S(1)}, u32[]{:S(2)}, u32[]{:S(2)}) collective-permute-start(bf16[128,1024]{1,0:T(8,128)(2,1)} %query.1), channel_id=1, source_target_pairs={{0,8},{4,12},{8,0},{12,4},{16,24},{20,28},{24,16},{28,20},{1,9},{5... | collective-permute-start | bytes 786440 | tf_op jit(solution)/shard_map/ppermute | solution.py:294
  3.6 0.8 %shard_map.128 = (bf16[16,128]{1,0:T(8,128)(2,1)S(1)}, bf16[16,128]{1,0:T(8,128)(2,1)S(1)}, bf16[16,128]{1,0:T(8,128)(2,1)S(1)}, bf16[16,128]{1,0:T(8,128)(2,1)S(1)}) custom-call(bf16[1,4096]{1,0:T(2,128)(2,1)} %query_far.1, bf16[1,2,1024]{2,1,0:T(2,128)(2,1)} %new_kv_far.3), custom_call_target="tpu_custom_call" | custom-call | tf_op jit(solution)/shard_map/pallas_call | solution.py:335
  4.4 0.1 collective-permute-start.6
  4.5 0.6 %collective-permute-start.7 = (bf16[16,128]{1,0:T(8,128)(2,1)S(1)}, bf16[16,128]{1,0:T(8,128)(2,1)S(1)}, u32[]{:S(2)}, u32[]{:S(2)}) collective-permute-start(bf16[16,128]{1,0:T(8,128)(2,1)S(1)} %get-tuple-element.18), channel_id=1, source_target_pairs={{0,2},{1,3},{2,0},{3,1},{4,6},{5,7},{6,4},{7,5},{8,10},{9,11},{10,... | collective-permute-start | bytes 12296 | tf_op jit(solution)/shard_map/ppermute | solution.py:294
  5.1 1.3 %collective-permute-start.8 = (bf16[16,128]{1,0:T(8,128)(2,1)S(1)}, bf16[16,128]{1,0:T(8,128)(2,1)S(1)}, u32[]{:S(2)}, u32[]{:S(2)}) collective-permute-start(bf16[16,128]{1,0:T(8,128)(2,1)S(1)} %get-tuple-element.19), channel_id=1, source_target_pairs={{0,3},{1,2},{2,1},{3,0},{4,7},{5,6},{6,5},{7,4},{8,11},{9,10},{10,... | collective-permute-start | bytes 12296 | tf_op jit(solution)/shard_map/ppermute | solution.py:294
  6.4 1.9 %shard_map.122 = (bf16[1280,256]{1,0:T(8,128)(2,1)S(1)}, bf16[256,1280]{1,0:T(8,128)(2,1)S(1)}, f32[4,128,128]{2,1,0:T(8,128)S(1)}, f32[4,128,128]{2,1,0:T(8,128)S(1)}, f32[4,1280,128]{2,1,0:T(8,128)S(1)}) custom-call(s32[2]{0:T(128)} %lengths_far.1, s32[2]{0:T(128)} %offsets_far.1, bf16[2,128,256]{2,1,0:T(8,128)(2,1)} %new_kv_far.2, ...), custom_call_target="tpu_custom_call" | custom-call | tf_op jit(solution)/shard_map/pallas_call | solution.py:335
  8.3 0.0 collective-permute-done.6
  8.3 0.6 %collective-permute-start = (bf16[128,1024]{1,0:T(8,128)(2,1)}, bf16[128,1024]{1,0:T(8,128)(2,1)S(1)}, u32[]{:S(2)}, u32[]{:S(2)}) collective-permute-start(bf16[128,1024]{1,0:T(8,128)(2,1)} %query.1), channel_id=1, source_target_pairs={{0,4},{4,0},{8,12},{12,8},{16,20},{20,16},{24,28},{28,24},{1,5},{5... | collective-permute-start | bytes 786440 | tf_op jit(solution)/shard_map/ppermute | solution.py:294
  8.9 0.0 collective-permute-done.7
  8.9 0.4 collective-permute-start.9
  9.3 1.7 %collective-permute-done.4.query = bf16[128,1024]{1,0:T(8,128)(2,1)S(1)} collective-permute-done((bf16[128,1024]{1,0:T(8,128)(2,1)}, bf16[128,1024]{1,0:T(8,128)(2,1)S(1)}, u32[]{:S(2)}, u32[]{:S(2)}) %collective-permute-start.4) | collective-permute-done | bytes 262176 | tf_op jit(solution)/shard_map/ppermute | solution.py:294
  11.0 2.3 %shard_map.126 = bf16[1056,128]{1,0:T(8,128)(2,1)S(1)} custom-call(bf16[128,1024]{1,0:T(8,128)(2,1)S(1)} %collective-permute-done.4.query, bf16[1280,256]{1,0:T(8,128)(2,1)S(1)} %get-tuple-element.11.keys, bf16[256,1280]{1,0:T(8,128)(2,1)S(1)} %get-tuple-element.12.values_t, f32[4,128,128]{2,1,0:T(8,128)S(1)} %get-tuple-element.13.cosine, ...), custom_call_target="tpu_custom_call" | custom-call | tf_op jit(solution)/shard_map/pallas_call | solution.py:335
  13.3 2.6 %collective-permute-start.5 = (bf16[1056,128]{1,0:T(8,128)(2,1)S(1)}, bf16[1056,128]{1,0:T(8,128)(2,1)S(1)}, u32[]{:S(2)}, u32[]{:S(2)}) collective-permute-start(bf16[1056,128]{1,0:T(8,128)(2,1)S(1)} %shard_map.126), channel_id=1, source_target_pairs={{0,12},{4,8},{8,4},{12,0},{16,28},{20,24},{24,20},{28,16},{1,13},{... | collective-permute-start | bytes 811016 | tf_op jit(solution)/shard_map/ppermute | solution.py:294
  15.8 0.5 %collective-permute-done.2.query = bf16[128,1024]{1,0:T(8,128)(2,1)S(1)} collective-permute-done((bf16[128,1024]{1,0:T(8,128)(2,1)}, bf16[128,1024]{1,0:T(8,128)(2,1)S(1)}, u32[]{:S(2)}, u32[]{:S(2)}) %collective-permute-start.2) | collective-permute-done | bytes 262176 | tf_op jit(solution)/shard_map/ppermute | solution.py:294
  16.3 2.3 %shard_map.125 = bf16[1056,128]{1,0:T(8,128)(2,1)S(1)} custom-call(bf16[128,1024]{1,0:T(8,128)(2,1)S(1)} %collective-permute-done.2.query, bf16[1280,256]{1,0:T(8,128)(2,1)S(1)} %get-tuple-element.11.keys, bf16[256,1280]{1,0:T(8,128)(2,1)S(1)} %get-tuple-element.12.values_t, f32[4,128,128]{2,1,0:T(8,128)S(1)} %get-tuple-element.13.cosine, ...), custom_call_target="tpu_custom_call" | custom-call | tf_op jit(solution)/shard_map/pallas_call | solution.py:335
  18.6 0.0 copy-start.1
  18.6 2.0 %collective-permute-start.3 = (bf16[1056,128]{1,0:T(8,128)(2,1)S(1)}, bf16[1056,128]{1,0:T(8,128)(2,1)S(1)}, u32[]{:S(2)}, u32[]{:S(2)}) collective-permute-start(bf16[1056,128]{1,0:T(8,128)(2,1)S(1)} %shard_map.125), channel_id=1, source_target_pairs={{0,8},{4,12},{8,0},{12,4},{16,24},{20,28},{24,16},{28,20},{1,9},{5... | collective-permute-start | bytes 811016 | tf_op jit(solution)/shard_map/ppermute | solution.py:294
  20.6 1.6 %collective-permute-done.query = bf16[128,1024]{1,0:T(8,128)(2,1)S(1)} collective-permute-done((bf16[128,1024]{1,0:T(8,128)(2,1)}, bf16[128,1024]{1,0:T(8,128)(2,1)S(1)}, u32[]{:S(2)}, u32[]{:S(2)}) %collective-permute-start) | collective-permute-done | bytes 262176 | tf_op jit(solution)/shard_map/ppermute | solution.py:294
  22.2 2.3 %shard_map.124 = bf16[1056,128]{1,0:T(8,128)(2,1)S(1)} custom-call(bf16[128,1024]{1,0:T(8,128)(2,1)S(1)} %collective-permute-done.query, bf16[1280,256]{1,0:T(8,128)(2,1)S(1)} %get-tuple-element.11.keys, bf16[256,1280]{1,0:T(8,128)(2,1)S(1)} %get-tuple-element.12.values_t, f32[4,128,128]{2,1,0:T(8,128)S(1)} %get-tuple-element.13.cosine, ...), custom_call_target="tpu_custom_call" | custom-call | tf_op jit(solution)/shard_map/pallas_call | solution.py:335
  24.5 0.1 collective-permute-start.1
  24.6 0.0 copy-start
  24.6 0.0 copy-start.2
  24.6 0.0 copy-start.3
  24.6 2.1 %collective-permute-start.10 = (bf16[128,128]{1,0:T(8,128)(2,1)S(1)}, bf16[128,128]{1,0:T(8,128)(2,1)S(1)}, u32[]{:S(2)}, u32[]{:S(2)}) collective-permute-start(bf16[128,128]{1,0:T(8,128)(2,1)S(1)} %constant_dynamic-update-slice_fusion.refs_0_), channel_id=1, source_target_pairs={{0,4},{4,0},{8,12},{12,8},{16,20},{20,16},{24,28},{28,24},{1,5},{5... | collective-permute-start | bytes 98312 | tf_op jit(solution)/shard_map/ppermute | solution.py:294
  26.7 1.6 %collective-permute-start.11 = (bf16[128,128]{1,0:T(8,128)(2,1)S(1)}, bf16[128,128]{1,0:T(8,128)(2,1)S(1)}, u32[]{:S(2)}, u32[]{:S(2)}) collective-permute-start(bf16[128,128]{1,0:T(8,128)(2,1)S(1)} %constant_dynamic-update-slice_fusion.refs_0_), channel_id=1, source_target_pairs={{0,8},{4,12},{8,0},{12,4},{16,24},{20,28},{24,16},{28,20},{1,9},{5... | collective-permute-start | bytes 98312 | tf_op jit(solution)/shard_map/ppermute | solution.py:294
  28.2 4.4 %collective-permute-done.10.refs_1_ = bf16[128,128]{1,0:T(8,128)(2,1)S(1)} collective-permute-done((bf16[128,128]{1,0:T(8,128)(2,1)S(1)}, bf16[128,128]{1,0:T(8,128)(2,1)S(1)}, u32[]{:S(2)}, u32[]{:S(2)}) %collective-permute-start.10) | collective-permute-done | bytes 32800 | tf_op jit(solution)/shard_map/ppermute | solution.py:294
  32.6 1.6 %collective-permute-start.12 = (bf16[128,128]{1,0:T(8,128)(2,1)S(1)}, bf16[128,128]{1,0:T(8,128)(2,1)S(1)}, u32[]{:S(2)}, u32[]{:S(2)}) collective-permute-start(bf16[128,128]{1,0:T(8,128)(2,1)S(1)} %constant_dynamic-update-slice_fusion.refs_0_), channel_id=1, source_target_pairs={{0,12},{4,8},{8,4},{12,0},{16,28},{20,24},{24,20},{28,16},{1,13},{... | collective-permute-start | bytes 98312 | tf_op jit(solution)/shard_map/ppermute | solution.py:294
  34.2 2.4 %shard_map.123.own = f32[1032,128]{1,0:T(8,128)S(1)} custom-call(bf16[128,1024]{1,0:T(8,128)(2,1)S(1)} %copy-done.1, bf16[1280,256]{1,0:T(8,128)(2,1)S(1)} %get-tuple-element.11.keys, bf16[256,1280]{1,0:T(8,128)(2,1)S(1)} %get-tuple-element.12.values_t, f32[4,128,128]{2,1,0:T(8,128)S(1)} %get-tuple-element.13.cosine, ...), custom_call_target="tpu_custom_call" | custom-call | tf_op jit(solution)/shard_map/pallas_call | solution.py:335
  36.6 0.8 %collective-permute-done.12.refs_3_ = bf16[128,128]{1,0:T(8,128)(2,1)S(1)} collective-permute-done((bf16[128,128]{1,0:T(8,128)(2,1)S(1)}, bf16[128,128]{1,0:T(8,128)(2,1)S(1)}, u32[]{:S(2)}, u32[]{:S(2)}) %collective-permute-start.12) | collective-permute-done | bytes 32800 | tf_op jit(solution)/shard_map/ppermute | solution.py:294
  37.4 2.7 %shard_map.129 = bf16[4,1024]{1,0:T(4,128)(2,1)} custom-call(s32[4]{0:T(128)S(1)} %copy-done.2, s32[32]{0:T(128)S(1)} %copy-done.3, bf16[128,128]{1,0:T(8,128)(2,1)S(1)} %constant_dynamic-update-slice_fusion.refs_0_, bf16[128,128]{1,0:T(8,128)(2,1)S(1)} %collective-permute-done.10.refs_1_, bf16[128,128]{1,0:T(8,128)(2,1)S(1)} %collective-permute-done.11.refs_2_, ...), custom_call_target="tpu_custom_call" | custom-call | tf_op jit(solution)/shard_map/pallas_call | solution.py:335
  40.1 1.0 %shard_map.127 = bf16[128,1024]{1,0:T(8,128)(2,1)} custom-call(f32[1032,128]{1,0:T(8,128)S(1)} %shard_map.123.own, bf16[1056,128]{1,0:T(8,128)(2,1)S(1)} %collective-permute-done.1.first, bf16[1056,128]{1,0:T(8,128)(2,1)S(1)} %collective-permute-done.3.second, bf16[1056,128]{1,0:T(8,128)(2,1)S(1)} %collective-permute-done.5.third), custom_call_target="tpu_custom_call" | custom-call | tf_op jit(solution)/shard_map/pallas_call | solution.py:335
  (17 shorter events, 0.1 us)
Async XLA Ops:
  0.6 10.4 %collective-permute-start.4 = (bf16[128,1024]{1,0:T(8,128)(2,1)}, bf16[128,1024]{1,0:T(8,128)(2,1)S(1)}, u32[]{:S(2)}, u32[]{:S(2)}) collective-permute-start(bf16[128,1024]{1,0:T(8,128)(2,1)} %query.1), channel_id=1, source_target_pairs={{0,12},{4,8},{8,4},{12,0},{16,28},{20,24},{24,20},{28,16},{1,13},{... | collective-permute-start | bytes 786440 | tf_op jit(solution)/shard_map/ppermute | solution.py:294
  3.2 13.1 %collective-permute-start.2 = (bf16[128,1024]{1,0:T(8,128)(2,1)}, bf16[128,1024]{1,0:T(8,128)(2,1)S(1)}, u32[]{:S(2)}, u32[]{:S(2)}) collective-permute-start(bf16[128,1024]{1,0:T(8,128)(2,1)} %query.1), channel_id=1, source_target_pairs={{0,8},{4,12},{8,0},{12,4},{16,24},{20,28},{24,16},{28,20},{1,9},{5... | collective-permute-start | bytes 786440 | tf_op jit(solution)/shard_map/ppermute | solution.py:294
  4.4 3.9 %collective-permute-start.6 = (bf16[16,128]{1,0:T(8,128)(2,1)S(1)}, bf16[16,128]{1,0:T(8,128)(2,1)S(1)}, u32[]{:S(2)}, u32[]{:S(2)}) collective-permute-start(bf16[16,128]{1,0:T(8,128)(2,1)S(1)} %get-tuple-element.17), channel_id=1, source_target_pairs={{0,1},{1,0},{2,3},{3,2},{4,5},{5,4},{6,7},{7,6},{8,9},{9,8},{10,11... | collective-permute-start | bytes 12296 | tf_op jit(solution)/shard_map/ppermute | solution.py:294
  4.5 4.4 %collective-permute-start.7 = (bf16[16,128]{1,0:T(8,128)(2,1)S(1)}, bf16[16,128]{1,0:T(8,128)(2,1)S(1)}, u32[]{:S(2)}, u32[]{:S(2)}) collective-permute-start(bf16[16,128]{1,0:T(8,128)(2,1)S(1)} %get-tuple-element.18), channel_id=1, source_target_pairs={{0,2},{1,3},{2,0},{3,1},{4,6},{5,7},{6,4},{7,5},{8,10},{9,11},{10,... | collective-permute-start | bytes 12296 | tf_op jit(solution)/shard_map/ppermute | solution.py:294
  5.1 3.8 %collective-permute-start.8 = (bf16[16,128]{1,0:T(8,128)(2,1)S(1)}, bf16[16,128]{1,0:T(8,128)(2,1)S(1)}, u32[]{:S(2)}, u32[]{:S(2)}) collective-permute-start(bf16[16,128]{1,0:T(8,128)(2,1)S(1)} %get-tuple-element.19), channel_id=1, source_target_pairs={{0,3},{1,2},{2,1},{3,0},{4,7},{5,6},{6,5},{7,4},{8,11},{9,10},{10,... | collective-permute-start | bytes 12296 | tf_op jit(solution)/shard_map/ppermute | solution.py:294
  8.3 13.9 %collective-permute-start = (bf16[128,1024]{1,0:T(8,128)(2,1)}, bf16[128,1024]{1,0:T(8,128)(2,1)S(1)}, u32[]{:S(2)}, u32[]{:S(2)}) collective-permute-start(bf16[128,1024]{1,0:T(8,128)(2,1)} %query.1), channel_id=1, source_target_pairs={{0,4},{4,0},{8,12},{12,8},{16,20},{20,16},{24,28},{28,24},{1,5},{5... | collective-permute-start | bytes 786440 | tf_op jit(solution)/shard_map/ppermute | solution.py:294
  8.9 15.6 %collective-permute-start.9 = (bf16[64,128]{1,0:T(8,128)(2,1)S(1)}, bf16[64,128]{1,0:T(8,128)(2,1)S(1)}, u32[]{:S(2)}, u32[]{:S(2)}) collective-permute-start(bf16[64,128]{1,0:T(8,128)(2,1)S(1)} %pad_maximum_fusion), channel_id=1, source_target_pairs={{0,16},{4,20},{8,24},{12,28},{16,0},{20,4},{24,8},{28,12},{1,17},{... | collective-permute-start | bytes 49160 | tf_op jit(solution)/shard_map/ppermute | solution.py:294
  13.3 26.8 %collective-permute-start.5 = (bf16[1056,128]{1,0:T(8,128)(2,1)S(1)}, bf16[1056,128]{1,0:T(8,128)(2,1)S(1)}, u32[]{:S(2)}, u32[]{:S(2)}) collective-permute-start(bf16[1056,128]{1,0:T(8,128)(2,1)S(1)} %shard_map.126), channel_id=1, source_target_pairs={{0,12},{4,8},{8,4},{12,0},{16,28},{20,24},{24,20},{28,16},{1,13},{... | collective-permute-start | bytes 811016 | tf_op jit(solution)/shard_map/ppermute | solution.py:294
  18.6 15.6 %copy-start.1 = (bf16[128,1024]{1,0:T(8,128)(2,1)S(1)}, bf16[128,1024]{1,0:T(8,128)(2,1)}, u32[]{:S(2)}) copy-start(bf16[128,1024]{1,0:T(8,128)(2,1)} %query.1) | copy-start | bytes 786436
  18.6 21.5 %collective-permute-start.3 = (bf16[1056,128]{1,0:T(8,128)(2,1)S(1)}, bf16[1056,128]{1,0:T(8,128)(2,1)S(1)}, u32[]{:S(2)}, u32[]{:S(2)}) collective-permute-start(bf16[1056,128]{1,0:T(8,128)(2,1)S(1)} %shard_map.125), channel_id=1, source_target_pairs={{0,8},{4,12},{8,0},{12,4},{16,24},{20,28},{24,16},{28,20},{1,9},{5... | collective-permute-start | bytes 811016 | tf_op jit(solution)/shard_map/ppermute | solution.py:294
  24.5 15.6 %collective-permute-start.1 = (bf16[1056,128]{1,0:T(8,128)(2,1)S(1)}, bf16[1056,128]{1,0:T(8,128)(2,1)S(1)}, u32[]{:S(2)}, u32[]{:S(2)}) collective-permute-start(bf16[1056,128]{1,0:T(8,128)(2,1)S(1)} %shard_map.124), channel_id=1, source_target_pairs={{0,4},{4,0},{8,12},{12,8},{16,20},{20,16},{24,28},{28,24},{1,5},{5... | collective-permute-start | bytes 811016 | tf_op jit(solution)/shard_map/ppermute | solution.py:294
  24.6 12.8 %copy-start = (bf16[2,4,512,256]{3,2,1,0:T(8,128)(2,1)S(1)}, bf16[2,4,512,256]{3,2,1,0:T(8,128)(2,1)}, u32[]{:S(2)}) copy-start(bf16[2,4,512,256]{3,2,1,0:T(8,128)(2,1)} %refs_4_.1) | copy-start | bytes 6291460
  24.6 12.8 %copy-start.2 = (s32[4]{0:T(128)S(1)}, s32[4]{0:T(128)}, u32[]{:S(2)}) copy-start(s32[4]{0:T(128)} %lengths.1) | copy-start | bytes 52
  24.6 12.8 %copy-start.3 = (s32[32]{0:T(128)S(1)}, s32[32]{0:T(128)}, u32[]{:S(2)}) copy-start(s32[32]{0:T(128)} %arrivals.1) | copy-start | bytes 388
  24.6 8.0 %collective-permute-start.10 = (bf16[128,128]{1,0:T(8,128)(2,1)S(1)}, bf16[128,128]{1,0:T(8,128)(2,1)S(1)}, u32[]{:S(2)}, u32[]{:S(2)}) collective-permute-start(bf16[128,128]{1,0:T(8,128)(2,1)S(1)} %constant_dynamic-update-slice_fusion.refs_0_), channel_id=1, source_target_pairs={{0,4},{4,0},{8,12},{12,8},{16,20},{20,16},{24,28},{28,24},{1,5},{5... | collective-permute-start | bytes 98312 | tf_op jit(solution)/shard_map/ppermute | solution.py:294
  26.7 10.0 %collective-permute-start.11 = (bf16[128,128]{1,0:T(8,128)(2,1)S(1)}, bf16[128,128]{1,0:T(8,128)(2,1)S(1)}, u32[]{:S(2)}, u32[]{:S(2)}) collective-permute-start(bf16[128,128]{1,0:T(8,128)(2,1)S(1)} %constant_dynamic-update-slice_fusion.refs_0_), channel_id=1, source_target_pairs={{0,8},{4,12},{8,0},{12,4},{16,24},{20,28},{24,16},{28,20},{1,9},{5... | collective-permute-start | bytes 98312 | tf_op jit(solution)/shard_map/ppermute | solution.py:294
  32.6 4.8 %collective-permute-start.12 = (bf16[128,128]{1,0:T(8,128)(2,1)S(1)}, bf16[128,128]{1,0:T(8,128)(2,1)S(1)}, u32[]{:S(2)}, u32[]{:S(2)}) collective-permute-start(bf16[128,128]{1,0:T(8,128)(2,1)S(1)} %constant_dynamic-update-slice_fusion.refs_0_), channel_id=1, source_target_pairs={{0,12},{4,8},{8,4},{12,0},{16,28},{20,24},{24,20},{28,16},{1,13},{... | collective-permute-start | bytes 98312 | tf_op jit(solution)/shard_map/ppermute | solution.py:294

commit v3 on v2

--- a/solution.py
+++ b/solution.py
@@ -13,6 +13,7 @@
 SINKS = 4
 SPAN = 512
 PAD_PARTS = 16
+LOG_LINES = 4
 HIDDEN = -1e30
 LOG2_SCALE = math.log2(math.e) / math.sqrt(D)
 VMEM = pltpu.CompilerParams(vmem_limit_bytes=24 * 1024 * 1024)
@@ -88,14 +89,17 @@
     new_kv_far,
     sinks_far,
     window_far,
+    dec_lengths_far,
     frequency,
     keys,
     values_t,
     cosines,
     sines,
     biases,
+    dec_tables,
     lengths,
     offsets,
+    dec_lengths,
     new_kv,
     sinks,
     values,
@@ -108,6 +112,7 @@
     scalars = fetch(
         (lengths_far, lengths, arrived.at[0]),
         (offsets_far, offsets, arrived.at[1]),
+        (dec_lengths_far, dec_lengths, arrived.at[6]),
     )
     arrays = fetch(
         (new_kv_far, new_kv, arrived.at[2]),
@@ -126,6 +131,15 @@
             cosines[part, lines], sines[part, lines] = angle_tables(
                 length, first_step + low, frequency[...]
             )
+    line = lax.broadcasted_iota(jnp.int32, dec_tables.shape[1:], 0)
+    lane = lax.broadcasted_iota(jnp.int32, dec_tables.shape[1:], 1)
+    position = jnp.zeros(dec_tables.shape[1:], jnp.int32)
+    for n in range(dec_lengths.shape[0]):
+        position = jnp.where(line == n, dec_lengths[n], position)
+    angle = position.astype(jnp.float32) * frequency[...]
+    sine = jnp.sin(angle)
+    dec_tables[0] = jnp.cos(angle)
+    dec_tables[1] = jnp.where(lane < D // 2, -sine, sine)
     index = lax.broadcasted_iota(jnp.int32, (D, rows), 0)
     step = lax.broadcasted_iota(jnp.int32, (D, rows), 1)
     for low in range(0, slots, D):
@@ -158,7 +172,9 @@
     values_t[:, slots : slots + rows] = new_kv[1].T
 
 
-def attend_kernel(part, own, query, keys, values_t, cosine, sine, bias, out, scores, weights):
+def attend_kernel(part, query, keys, values_t, cosine, sine, bias, *refs):
+    own = part == 0
+    passengers, (out, scores, weights) = refs[:-3], refs[-3:]
     rows = query.shape[0]
     kv_heads = keys.shape[1] // D
     group = query.shape[1] // D // kv_heads
@@ -179,18 +195,18 @@
                 chunk, block, (((1,), (1,)), ((), ())), preferred_element_type=jnp.float32
             )
             s = s + jnp.concatenate([mask] * group, axis=1)
-            scores[low : low + D, :] = s
+            scores[kv, low : low + D, :] = s
             peak = jnp.max(s.reshape(D // 8, 8, group * rows), axis=0)
             top = peak if top is None else jnp.maximum(top, peak)
         top = jnp.max(top, axis=0, keepdims=True)
         mass = jnp.zeros((8, group * rows), jnp.float32)
         for low in range(0, total, D):
-            w = jnp.exp2((scores[low : low + D, :] - top) * LOG2_SCALE)
+            w = jnp.exp2((scores[kv, low : low + D, :] - top) * LOG2_SCALE)
             mass = mass + jnp.sum(w.reshape(D // 8, 8, group * rows), axis=0)
-            weights[low : low + D, :] = w.astype(jnp.bfloat16)
+            weights[kv, low : low + D, :] = w.astype(jnp.bfloat16)
         mass = jnp.sum(mass, axis=0, keepdims=True)
         mix = jnp.dot(
-            values_t[lanes, :total], weights[:total, :], preferred_element_type=jnp.float32
+            values_t[lanes, :total], weights[kv, :total, :], preferred_element_type=jnp.float32
         )
         mix = mix * (1.0 / mass)
         log = top * LOG2_SCALE + jnp.log2(mass)
@@ -205,15 +221,26 @@
     else:
         pieces = [p.astype(jnp.float32) for p in split_three(log)]
         pieces.append(jnp.zeros_like(log))
-        out[heads * D :, :] = jnp.concatenate(pieces, axis=0).astype(out.dtype)
-
-
-def combine_kernel(own, first, second, third, out):
-    rows = out.shape[0]
+        end = heads * D + LOG_LINES * heads
+        out[heads * D : end, :] = jnp.concatenate(pieces, axis=0).astype(out.dtype)
+        for block in passengers:
+            out[end : end + block.shape[0], :] = block[...]
+            end += block.shape[0]
+
+
+def append_kernel(block, *refs):
+    passengers, out = refs[:-1], refs[-1]
+    end = block.shape[0]
+    for passenger in passengers[::-1]:
+        out[end - passenger.shape[0] : end, :] = passenger[...]
+        end -= passenger.shape[0]
+
+
+def combine(own, first, second, third, out):
     heads = out.shape[1] // D
     logs = [own[heads * D :, :]]
     for other in (first, second, third):
-        p = other[heads * D :, :].astype(jnp.float32)
+        p = other[heads * D : (D + LOG_LINES) * heads, :].astype(jnp.float32)
         logs.append(p[:heads] + p[heads : 2 * heads] + p[2 * heads : 3 * heads])
     top = functools.reduce(jnp.maximum, logs)
     shares = [jnp.exp2(log - top) for log in logs]
@@ -227,8 +254,7 @@
         out[:, lines] = mix.T.astype(out.dtype)
 
 
-def decode_kernel(lengths, arrivals, *refs):
-    near, (cache, frequency, out, mixed) = refs[: len(refs) - 4], refs[len(refs) - 4 :]
+def decode(lengths, arrivals, near, cache, tables, out, mixed):
     count = cache.shape[1]
     slots = cache.shape[2]
     kv_heads = cache.shape[3] // D
@@ -237,27 +263,27 @@
     blk, head_at = lax.axis_index("blk"), lax.axis_index("head")
     head_count = lax.axis_size("head")
     members = len(near)
+    height = near[0].shape[0]
 
     def look(i, found):
         owner = arrivals[i] - blk * count
         return tuple(jnp.where(owner == n, i, was) for n, was in enumerate(found))
 
-    found = lax.fori_loop(
-        0, arrivals.shape[0], look, (jnp.int32(0),) * count, unroll=8
-    )
+    found = lax.fori_loop(0, arrivals.shape[0], look, (jnp.int32(0),) * count, unroll=8)
     head_of = lax.broadcasted_iota(jnp.int32, (heads, D), 0) // group
+    slot = lax.broadcasted_iota(jnp.int32, (heads, slots), 1)
+    scores, own_scores, new_values = [], [], []
     for n in range(count):
         away = (found[n] // head_count) ^ blk
         line = (away // members) * head_count + (lax.rem(found[n], head_count) ^ head_at)
-        lines = pl.ds(pl.multiple_of(line * PAD_PARTS, PAD_PARTS), PAD_PARTS)
-        x = near[0][lines, :]
-        for part in range(1, members):
-            x = jnp.where(lax.rem(away, members) == part, near[part][lines, :], x)
+        line = line * PAD_PARTS
+        x = None
+        for part, block in enumerate(near):
+            start = pl.multiple_of(block.shape[0] - height + line, PAD_PARTS)
+            y = block[pl.ds(start, PAD_PARTS), :]
+            x = y if x is None else jnp.where(lax.rem(away, members) == part, y, x)
         x = x.astype(jnp.float32)
-        angle = lengths[n].astype(jnp.float32) * frequency[...]
-        lane = lax.broadcasted_iota(jnp.int32, angle.shape, 1)
-        sine = jnp.sin(angle)
-        turned = turn(x, jnp.cos(angle), jnp.where(lane < D // 2, -sine, sine))
+        turned = turn(x, tables[0, n : n + 1, :], tables[1, n : n + 1, :])
         turned = turned.astype(jnp.bfloat16).astype(jnp.float32)
         q = turned[:heads]
         wide = [jnp.where(head_of == kv, q, 0.0) for kv in range(kv_heads)]
@@ -272,21 +298,44 @@
         s = lax.dot_general(
             wide, cache[0, n], (((1,), (1,)), ((), ())), preferred_element_type=jnp.float32
         )
-        slot = lax.broadcasted_iota(jnp.int32, (heads, slots), 1)
-        s = jnp.where(slot < lengths[n], s, HIDDEN)
-        own_s = jnp.sum(q * new_key, axis=1, keepdims=True)
-        top = jnp.maximum(jnp.max(s, axis=1, keepdims=True), own_s)
-        w = jnp.exp2((s - top) * LOG2_SCALE)
-        own_w = jnp.exp2((own_s - top) * LOG2_SCALE)
-        mass = jnp.sum(w, axis=1, keepdims=True) + own_w
-        mix = jnp.dot(w.astype(jnp.bfloat16), cache[1, n], preferred_element_type=jnp.float32)
-        picked = own_w.astype(jnp.bfloat16).astype(jnp.float32) * new_value
+        scores.append(jnp.where(slot < lengths[n], s, HIDDEN))
+        own_scores.append(q * new_key)
+        new_values.append(new_value)
+    s = jnp.concatenate(scores, axis=0)
+    own_s = jnp.sum(jnp.concatenate(own_scores, axis=0), axis=1, keepdims=True)
+    top = jnp.maximum(jnp.max(s, axis=1, keepdims=True), own_s)
+    w = jnp.exp2((s - top) * LOG2_SCALE)
+    own_w = jnp.exp2((own_s - top) * LOG2_SCALE)
+    scale = 1.0 / (jnp.sum(w, axis=1, keepdims=True) + own_w)
+    own_w = own_w.astype(jnp.bfloat16).astype(jnp.float32)
+    for n in range(count):
+        lines = slice(n * heads, (n + 1) * heads)
+        mix = jnp.dot(
+            w[lines].astype(jnp.bfloat16), cache[1, n], preferred_element_type=jnp.float32
+        )
+        picked = own_w[lines] * new_values[n]
         for kv in range(kv_heads):
             picked = picked + jnp.where(head_of == kv, mix[:, kv * D : (kv + 1) * D], 0.0)
-        picked = picked / mass
+        picked = picked * scale[lines]
         for head in range(heads):
             mixed[n : n + 1, head * D : (head + 1) * D] = picked[head : head + 1, :]
     out[...] = mixed[...].astype(out.dtype)
+
+
+def finish_kernel(
+    lengths, arrivals, own, first, second, third, *refs
+):
+    rows, (cache, tables, long_out, dec_out, mixed, held) = refs[:-6], refs[-6:]
+    low = 0
+    for block in rows:
+        held[low : low + block.shape[0], :] = block[...]
+        low += block.shape[0]
+    decode(lengths, arrivals, (held, first, second, third), cache, tables, dec_out, mixed)
+    combine(own, first, second, third, long_out)
+
+
+def after(block, *others):
+    return lax.optimization_barrier((block, *others))[0]
 
 
 def exchange(block, axis, distance):
@@ -326,18 +375,19 @@
     members = SPAN // rows
     own_count = dec_cache.shape[1]
 
-    queries = [long_query] + [exchange(long_query, "blk", part) for part in range(1, members)]
+    queries = {part: exchange(long_query, "blk", part) for part in range(1, members)}
 
     half = jnp.arange(D, dtype=jnp.int32) % (D // 2)
     frequency = (10000.0 ** (-(half.astype(jnp.float32) * 2.0 / D))).reshape(1, D)
 
-    def call(kernel, out_shape, operands, specs, scratch):
+    def call(kernel, out_shape, operands, specs, scratch, aliases={}):
         return pl.pallas_call(
             kernel,
             in_specs=specs,
             out_specs=jax.tree.map(lambda _: NEAR, out_shape),
             out_shape=out_shape,
             scratch_shapes=scratch,
+            input_output_aliases=aliases,
             compiler_params=VMEM,
         )(*operands)
 
@@ -355,12 +405,6 @@
     arrived = jnp.concatenate(
         [exchange(piece, "head", r) if r else piece for r, piece in enumerate(pieces)], axis=0
     )
-    distance = members
-    while distance < blk_count:
-        arrived = jnp.concatenate([arrived, exchange(arrived, "blk", distance)], axis=0)
-        distance *= 2
-    near = [arrived] + [exchange(arrived, "blk", part) for part in range(1, members)]
-
     total = slots + rows + D
     shared = call(
         prepare_kernel,
@@ -370,56 +414,79 @@
             jax.ShapeDtypeStruct((members, rows, D), jnp.float32),
             jax.ShapeDtypeStruct((members, rows, D), jnp.float32),
             jax.ShapeDtypeStruct((members, total, rows), jnp.float32),
+            jax.ShapeDtypeStruct((2, -(-own_count // 8) * 8, D), jnp.float32),
         ),
-        (*stay(long_len, long_offset, long_new_kv, sink_kv, window), frequency),
-        [FAR] * 5 + [NEAR],
+        (*stay(long_len, long_offset, long_new_kv, sink_kv, window, dec_len), frequency),
+        [FAR] * 6 + [NEAR],
         [
             pltpu.SMEM(long_len.shape, jnp.int32),
             pltpu.SMEM(long_offset.shape, jnp.int32),
+            pltpu.SMEM(dec_len.shape, jnp.int32),
             pltpu.VMEM(long_new_kv.shape, jnp.bfloat16),
             pltpu.VMEM((2, *sink_kv.shape[2:]), jnp.bfloat16),
             pltpu.VMEM(window.shape[1:], jnp.bfloat16),
             pltpu.VMEM((D, kv_width), jnp.float32),
-            pltpu.SemaphoreType.DMA((6,)),
+            pltpu.SemaphoreType.DMA((7,)),
         ],
     )
 
-    def attend(part):
-        own = part == 0
-        if own:
+    def attend(part, query, spare, *passenger):
+        if part == 0:
             out = jax.ShapeDtypeStruct((features + heads, rows), jnp.float32)
         else:
-            out = jax.ShapeDtypeStruct((features + 4 * heads, rows), jnp.bfloat16)
+            lines = features + LOG_LINES * heads + spare
+            lines += sum(p.shape[0] for p in passenger)
+            out = jax.ShapeDtypeStruct((lines, rows), jnp.bfloat16)
         return call(
-            functools.partial(attend_kernel, part, own),
+            functools.partial(attend_kernel, part),
             out,
-            (queries[part], *shared),
-            [NEAR] * 6,
+            (query, *shared[:5], *passenger),
+            [NEAR] * (6 + len(passenger)),
             [
-                pltpu.VMEM((total, group * rows), jnp.float32),
-                pltpu.VMEM((total, group * rows), jnp.bfloat16),
+                pltpu.VMEM((kv_heads, total, group * rows), jnp.float32),
+                pltpu.VMEM((kv_heads, total, group * rows), jnp.bfloat16),
             ],
         )
 
-    mine = attend(0)
-    others = [exchange(attend(part), "blk", part) for part in range(1, members)]
-    long_out = call(
-        combine_kernel,
-        jax.ShapeDtypeStruct((rows, features), jnp.bfloat16),
-        (mine, *others),
-        [NEAR] * (1 + len(others)),
-        [],
-    )
-    dec_out = call(
-        decode_kernel,
-        jax.ShapeDtypeStruct((own_count, features), jnp.bfloat16),
-        (dec_len, arrival_order, *near, dec_cache, frequency),
-        [SCALARS, SCALARS] + [NEAR] * (len(near) + 2),
+    arrived = after(arrived, shared[0])
+    blocks = [arrived]
+    while len(blocks) * arrived.shape[0] * members < arrival_order.shape[0] * PAD_PARTS:
+        full = blocks[0] if len(blocks) == 1 else jnp.concatenate(blocks, axis=0)
+        blocks = [full, exchange(full, "blk", members * full.shape[0] // arrived.shape[0])]
+    spare = sum(block.shape[0] for block in blocks)
+    mine = attend(0, long_query, 0)
+    backs = {}
+    for part in range(1, members):
+        if part == members - 1:
+            mix = attend(part, queries[part], spare)
+            mix = call(
+                append_kernel,
+                jax.ShapeDtypeStruct(mix.shape, mix.dtype),
+                (mix, *blocks),
+                [NEAR] * (1 + len(blocks)),
+                [],
+                {0: 0},
+            )
+        else:
+            mix = attend(part, queries[part], 0, *blocks)
+        backs[part] = exchange(mix, "blk", part)
+    first_back, second_back, third_back = [backs[part] for part in range(1, members)]
+    return call(
+        finish_kernel,
+        (
+            jax.ShapeDtypeStruct((rows, features), jnp.bfloat16),
+            jax.ShapeDtypeStruct((own_count, features), jnp.bfloat16),
+        ),
+        (
+            dec_len, arrival_order, mine, first_back, second_back, third_back,
+            *blocks, dec_cache, shared[5],
+        ),
+        [SCALARS, SCALARS] + [NEAR] * (6 + len(blocks)),
         [
             pltpu.VMEM((own_count, features), jnp.float32),
+            pltpu.VMEM((spare, D), jnp.bfloat16),
         ],
     )
-    return (long_out, dec_out)
 
 
 def solution(mesh):

time: 41.4 us -> 35.7 us (0.86)
  the two profiles are of different devices: /device:TPU:20 before, /device:TPU:0 now
where the time goes in v3:
time: 35.7 us; the launch traced here: 35.4 us
  starting transfers between devices  15.2 us (43%)
  Pallas kernels  14 us (39%)
  waiting for transfers between devices  5.41 us (15%)
  between operations  0.76 us (2%)
    ppermute x10, starting transfers between devices, exchange(): return lax.ppermute(block, axis, [(i, i ^ distance) for i in range(count)])  15.2 us
    pallas_call x8, Pallas kernels, call(): pl.pallas_call(kernel, in_specs=specs, out_specs=jax.tree.map(lambda _: N...  14 us
    ppermute x10, waiting for transfers between devices, exchange(): return lax.ppermute(block, axis, [(i, i ^ distance) for i in range(count)])  5.41 us
  transfers between devices with their start and end apart: 10, of which 4 were waited for; matrix products, arithmetic and copies ran while one was open for 0% of the time, Pallas kernels for 34%

profile of v3, /device:TPU:0, one launch (start us, length us, event | category | flops | bytes accessed | tf_op | source)
XLA Modules:
  0.0 35.4 jit_solution(53728974224622999)
XLA Ops:
  0.6 4.0 %collective-permute-start.8 = (bf16[128,1024]{1,0:T(8,128)(2,1)}, bf16[128,1024]{1,0:T(8,128)(2,1)S(1)}, u32[]{:S(2)}, u32[]{:S(2)}) collective-permute-start(bf16[128,1024]{1,0:T(8,128)(2,1)} %query.1), channel_id=1, source_target_pairs={{0,12},{4,8},{8,4},{12,0},{16,28},{20,24},{24,20},{28,16},{1,13},{... | collective-permute-start | bytes 786440 | tf_op jit(solution)/shard_map/ppermute | solution.py:343
  4.6 0.5 %collective-permute-start = (bf16[128,1024]{1,0:T(8,128)(2,1)}, bf16[128,1024]{1,0:T(8,128)(2,1)S(1)}, u32[]{:S(2)}, u32[]{:S(2)}) collective-permute-start(bf16[128,1024]{1,0:T(8,128)(2,1)} %query.1), channel_id=1, source_target_pairs={{0,4},{4,0},{8,12},{12,8},{16,20},{20,16},{24,28},{28,24},{1,5},{5... | collective-permute-start | bytes 786440 | tf_op jit(solution)/shard_map/ppermute | solution.py:343
  5.2 0.1 collective-permute-start.6
  5.3 0.8 %shard_map.124 = (bf16[16,128]{1,0:T(8,128)(2,1)S(1)}, bf16[16,128]{1,0:T(8,128)(2,1)S(1)}, bf16[16,128]{1,0:T(8,128)(2,1)S(1)}, bf16[16,128]{1,0:T(8,128)(2,1)S(1)}) custom-call(bf16[1,4096]{1,0:T(2,128)(2,1)} %query_far.1, bf16[1,2,1024]{2,1,0:T(2,128)(2,1)} %new_kv_far.3), custom_call_target="tpu_custom_call" | custom-call | tf_op jit(solution)/shard_map/pallas_call | solution.py:384
  6.1 0.1 collective-permute-start.1
  6.1 1.9 %collective-permute-start.2 = (bf16[16,128]{1,0:T(8,128)(2,1)S(1)}, bf16[16,128]{1,0:T(8,128)(2,1)S(1)}, u32[]{:S(2)}, u32[]{:S(2)}) collective-permute-start(bf16[16,128]{1,0:T(8,128)(2,1)S(1)} %get-tuple-element.20), channel_id=1, source_target_pairs={{0,2},{1,3},{2,0},{3,1},{4,6},{5,7},{6,4},{7,5},{8,10},{9,11},{10,... | collective-permute-start | bytes 12296 | tf_op jit(solution)/shard_map/ppermute | solution.py:343
  8.1 0.0 collective-permute-done.1
  8.1 0.9 %collective-permute-start.3 = (bf16[16,128]{1,0:T(8,128)(2,1)S(1)}, bf16[16,128]{1,0:T(8,128)(2,1)S(1)}, u32[]{:S(2)}, u32[]{:S(2)}) collective-permute-start(bf16[16,128]{1,0:T(8,128)(2,1)S(1)} %get-tuple-element.21), channel_id=1, source_target_pairs={{0,3},{1,2},{2,1},{3,0},{4,7},{5,6},{6,5},{7,4},{8,11},{9,10},{10,... | collective-permute-start | bytes 12296 | tf_op jit(solution)/shard_map/ppermute | solution.py:343
  8.9 1.9 %shard_map.122 = (bf16[1280,256]{1,0:T(8,128)(2,1)S(1)}, bf16[256,1280]{1,0:T(8,128)(2,1)S(1)}, f32[4,128,128]{2,1,0:T(8,128)S(1)}, f32[4,128,128]{2,1,0:T(8,128...) custom-call(s32[2]{0:T(128)} %lengths_far.1, s32[2]{0:T(128)} %offsets_far.1, ...), custom_call_target="tpu_custom_call" | custom-call | tf_op jit(solution)/shard_map/pallas_call | solution.py:384
  10.9 0.0 collective-permute-done.2
  10.9 0.2 collective-permute-done.3
  11.1 2.6 %collective-permute-start.4 = (bf16[64,128]{1,0:T(8,128)(2,1)S(1)}, bf16[64,128]{1,0:T(8,128)(2,1)S(1)}, u32[]{:S(2)}, u32[]{:S(2)}) collective-permute-start(bf16[64,128]{1,0:T(8,128)(2,1)S(1)} %pad_maximum_fusion.refs_0_), channel_id=1, source_target_pairs={{0,16},{4,20},{8,24},{12,28},{16,0},{20,4},{24,8},{28,12},{1,17},{... | collective-permute-start | bytes 49160 | tf_op jit(solution)/shard_map/ppermute | solution.py:343
  13.7 0.0 collective-permute-done.8.query
  13.7 2.3 %shard_map.127.block = bf16[1184,128]{1,0:T(8,128)(2,1)S(1)} custom-call(bf16[128,1024]{1,0:T(8,128)(2,1)S(1)} %collective-permute-done.8.query, bf16[1280,256]{1,0:T(8,128)(2,1)S(1)} %get-tuple-element.13.keys, bf16[256,1280]{1,0:T(8,128)(2,1)S(1)} %get-tuple-element.14.values_t, f32[4,128,128]{2,1,0:T(8,128)S(1)} %get-tuple-element.15.cosine, ...), custom_call_target="tpu_custom_call" | custom-call | tf_op jit(solution)/shard_map/pallas_call | solution.py:384
  16.0 0.5 %collective-permute-done.4.refs_1_ = bf16[64,128]{1,0:T(8,128)(2,1)S(1)} collective-permute-done((bf16[64,128]{1,0:T(8,128)(2,1)S(1)}, bf16[64,128]{1,0:T(8,128)(2,1)S(1)}, u32[]{:S(2)}, u32[]{:S(2)}) %collective-permute-start.4) | collective-permute-done | bytes 16416 | tf_op jit(solution)/shard_map/ppermute | solution.py:343
  16.4 3.5 %collective-permute-start.9 = (bf16[1184,128]{1,0:T(8,128)(2,1)S(1)}, bf16[1184,128]{1,0:T(8,128)(2,1)S(1)}, u32[]{:S(2)}, u32[]{:S(2)}) collective-permute-start(bf16[1184,128]{1,0:T(8,128)(2,1)S(1)} %shard_map.128), channel_id=1, source_target_pairs={{0,12},{4,8},{8,4},{12,0},{16,28},{20,24},{24,20},{28,16},{1,13},{... | collective-permute-start | bytes 909320 | tf_op jit(solution)/shard_map/ppermute | solution.py:343
  19.9 0.0 collective-permute-done.query
  19.9 2.3 %shard_map.125 = bf16[1184,128]{1,0:T(8,128)(2,1)S(1)} custom-call(bf16[128,1024]{1,0:T(8,128)(2,1)S(1)} %collective-permute-done.query, bf16[1280,256]{1,0:T(8,128)(2,1)S(1)} %get-tuple-element.13.keys, bf16[256,1280]{1,0:T(8,128)(2,1)S(1)} %get-tuple-element.14.values_t, f32[4,128,128]{2,1,0:T(8,128)S(1)} %get-tuple-element.15.cosine, ...), custom_call_target="tpu_custom_call" | custom-call | tf_op jit(solution)/shard_map/pallas_call | solution.py:384
  22.2 0.0 copy-start.1
  22.2 1.6 %collective-permute-start.5 = (bf16[1184,128]{1,0:T(8,128)(2,1)S(1)}, bf16[1184,128]{1,0:T(8,128)(2,1)S(1)}, u32[]{:S(2)}, u32[]{:S(2)}) collective-permute-start(bf16[1184,128]{1,0:T(8,128)(2,1)S(1)} %shard_map.125), channel_id=1, source_target_pairs={{0,4},{4,0},{8,12},{12,8},{16,20},{20,16},{24,28},{28,24},{1,5},{5... | collective-permute-start | bytes 909320 | tf_op jit(solution)/shard_map/ppermute | solution.py:343
  23.7 0.0 collective-permute-done.6.query
  23.7 2.3 %shard_map.126 = bf16[1184,128]{1,0:T(8,128)(2,1)S(1)} custom-call(bf16[128,1024]{1,0:T(8,128)(2,1)S(1)} %collective-permute-done.6.query, bf16[1280,256]{1,0:T(8,128)(2,1)S(1)} %get-tuple-element.13.keys, bf16[256,1280]{1,0:T(8,128)(2,1)S(1)} %get-tuple-element.14.values_t, f32[4,128,128]{2,1,0:T(8,128)S(1)} %get-tuple-element.15.cosine, ...), custom_call_target="tpu_custom_call" | custom-call | tf_op jit(solution)/shard_map/pallas_call | solution.py:384
  26.0 0.0 copy-start
  26.0 0.0 copy-start.2
  26.0 0.0 copy-start.3
  26.1 0.1 collective-permute-start.7
  26.1 0.0 copy-done.1
  26.1 2.4 %shard_map.123.own = f32[1032,128]{1,0:T(8,128)S(1)} custom-call(bf16[128,1024]{1,0:T(8,128)(2,1)S(1)} %copy-done.1, bf16[1280,256]{1,0:T(8,128)(2,1)S(1)} %get-tuple-element.13.keys, bf16[256,1280]{1,0:T(8,128)(2,1)S(1)} %get-tuple-element.14.values_t, f32[4,128,128]{2,1,0:T(8,128)S(1)} %get-tuple-element.15.cosine, ...), custom_call_target="tpu_custom_call" | custom-call | tf_op jit(solution)/shard_map/pallas_call | solution.py:384
  28.6 0.0 collective-permute-done.9.third
  28.6 4.1 %collective-permute-done.5.first = bf16[1184,128]{1,0:T(8,128)(2,1)S(1)} collective-permute-done((bf16[1184,128]{1,0:T(8,128)(2,1)S(1)}, bf16[1184,128]{1,0:T(8,128)(2,1)S(1)}, u32[]{:S(2)}, u32[]{:S(2)}) %collective-permute-start.5) | collective-permute-done | bytes 303136 | tf_op jit(solution)/shard_map/ppermute | solution.py:343
  32.7 0.6 %collective-permute-done.7.second = bf16[1184,128]{1,0:T(8,128)(2,1)S(1)} collective-permute-done((bf16[1184,128]{1,0:T(8,128)(2,1)S(1)}, bf16[1184,128]{1,0:T(8,128)(2,1)S(1)}, u32[]{:S(2)}, u32[]{:S(2)}) %collective-permute-start.7) | collective-permute-done | bytes 303136 | tf_op jit(solution)/shard_map/ppermute | solution.py:343
  33.3 2.1 %shard_map.129 = (bf16[128,1024]{1,0:T(8,128)(2,1)}, bf16[4,1024]{1,0:T(4,128)(2,1)}) custom-call(s32[4]{0:T(128)S(1)} %copy-done.2, s32[32]{0:T(128)S(1)} %copy-done.3, f32[1032,128]{1,0:T(8,128)S(1)} %shard_map.123.own, bf16[1184,128]{1,0:T(8,128)(2,1)S(1)} %collective-permute-done.5.first, bf16[1184,128]{1,0:T(8,128)(2,1)S(1)} %collective-permute-done.7.second, ...), custom_call_target="tpu_custom_call" | custom-call | tf_op jit(solution)/shard_map/pallas_call | solution.py:384
  (6 shorter events, 0.0 us)
Async XLA Ops:
  0.6 13.1 %collective-permute-start.8 = (bf16[128,1024]{1,0:T(8,128)(2,1)}, bf16[128,1024]{1,0:T(8,128)(2,1)S(1)}, u32[]{:S(2)}, u32[]{:S(2)}) collective-permute-start(bf16[128,1024]{1,0:T(8,128)(2,1)} %query.1), channel_id=1, source_target_pairs={{0,12},{4,8},{8,4},{12,0},{16,28},{20,24},{24,20},{28,16},{1,13},{... | collective-permute-start | bytes 786440 | tf_op jit(solution)/shard_map/ppermute | solution.py:343
  4.6 15.3 %collective-permute-start = (bf16[128,1024]{1,0:T(8,128)(2,1)}, bf16[128,1024]{1,0:T(8,128)(2,1)S(1)}, u32[]{:S(2)}, u32[]{:S(2)}) collective-permute-start(bf16[128,1024]{1,0:T(8,128)(2,1)} %query.1), channel_id=1, source_target_pairs={{0,4},{4,0},{8,12},{12,8},{16,20},{20,16},{24,28},{28,24},{1,5},{5... | collective-permute-start | bytes 786440 | tf_op jit(solution)/shard_map/ppermute | solution.py:343
  5.2 18.6 %collective-permute-start.6 = (bf16[128,1024]{1,0:T(8,128)(2,1)}, bf16[128,1024]{1,0:T(8,128)(2,1)S(1)}, u32[]{:S(2)}, u32[]{:S(2)}) collective-permute-start(bf16[128,1024]{1,0:T(8,128)(2,1)} %query.1), channel_id=1, source_target_pairs={{0,8},{4,12},{8,0},{12,4},{16,24},{20,28},{24,16},{28,20},{1,9},{5... | collective-permute-start | bytes 786440 | tf_op jit(solution)/shard_map/ppermute | solution.py:343
  6.1 2.0 %collective-permute-start.1 = (bf16[16,128]{1,0:T(8,128)(2,1)S(1)}, bf16[16,128]{1,0:T(8,128)(2,1)S(1)}, u32[]{:S(2)}, u32[]{:S(2)}) collective-permute-start(bf16[16,128]{1,0:T(8,128)(2,1)S(1)} %get-tuple-element.19), channel_id=1, source_target_pairs={{0,1},{1,0},{2,3},{3,2},{4,5},{5,4},{6,7},{7,6},{8,9},{9,8},{10,11... | collective-permute-start | bytes 12296 | tf_op jit(solution)/shard_map/ppermute | solution.py:343
  6.1 4.7 %collective-permute-start.2 = (bf16[16,128]{1,0:T(8,128)(2,1)S(1)}, bf16[16,128]{1,0:T(8,128)(2,1)S(1)}, u32[]{:S(2)}, u32[]{:S(2)}) collective-permute-start(bf16[16,128]{1,0:T(8,128)(2,1)S(1)} %get-tuple-element.20), channel_id=1, source_target_pairs={{0,2},{1,3},{2,0},{3,1},{4,6},{5,7},{6,4},{7,5},{8,10},{9,11},{10,... | collective-permute-start | bytes 12296 | tf_op jit(solution)/shard_map/ppermute | solution.py:343
  8.1 3.0 %collective-permute-start.3 = (bf16[16,128]{1,0:T(8,128)(2,1)S(1)}, bf16[16,128]{1,0:T(8,128)(2,1)S(1)}, u32[]{:S(2)}, u32[]{:S(2)}) collective-permute-start(bf16[16,128]{1,0:T(8,128)(2,1)S(1)} %get-tuple-element.21), channel_id=1, source_target_pairs={{0,3},{1,2},{2,1},{3,0},{4,7},{5,6},{6,5},{7,4},{8,11},{9,10},{10,... | collective-permute-start | bytes 12296 | tf_op jit(solution)/shard_map/ppermute | solution.py:343
  11.1 5.3 %collective-permute-start.4 = (bf16[64,128]{1,0:T(8,128)(2,1)S(1)}, bf16[64,128]{1,0:T(8,128)(2,1)S(1)}, u32[]{:S(2)}, u32[]{:S(2)}) collective-permute-start(bf16[64,128]{1,0:T(8,128)(2,1)S(1)} %pad_maximum_fusion.refs_0_), channel_id=1, source_target_pairs={{0,16},{4,20},{8,24},{12,28},{16,0},{20,4},{24,8},{28,12},{1,17},{... | collective-permute-start | bytes 49160 | tf_op jit(solution)/shard_map/ppermute | solution.py:343
  16.4 12.1 %collective-permute-start.9 = (bf16[1184,128]{1,0:T(8,128)(2,1)S(1)}, bf16[1184,128]{1,0:T(8,128)(2,1)S(1)}, u32[]{:S(2)}, u32[]{:S(2)}) collective-permute-start(bf16[1184,128]{1,0:T(8,128)(2,1)S(1)} %shard_map.128), channel_id=1, source_target_pairs={{0,12},{4,8},{8,4},{12,0},{16,28},{20,24},{24,20},{28,16},{1,13},{... | collective-permute-start | bytes 909320 | tf_op jit(solution)/shard_map/ppermute | solution.py:343
  22.2 4.0 %copy-start.1 = (bf16[128,1024]{1,0:T(8,128)(2,1)S(1)}, bf16[128,1024]{1,0:T(8,128)(2,1)}, u32[]{:S(2)}) copy-start(bf16[128,1024]{1,0:T(8,128)(2,1)} %query.1) | copy-start | bytes 786436
  22.2 10.5 %collective-permute-start.5 = (bf16[1184,128]{1,0:T(8,128)(2,1)S(1)}, bf16[1184,128]{1,0:T(8,128)(2,1)S(1)}, u32[]{:S(2)}, u32[]{:S(2)}) collective-permute-start(bf16[1184,128]{1,0:T(8,128)(2,1)S(1)} %shard_map.125), channel_id=1, source_target_pairs={{0,4},{4,0},{8,12},{12,8},{16,20},{20,16},{24,28},{28,24},{1,5},{5... | collective-permute-start | bytes 909320 | tf_op jit(solution)/shard_map/ppermute | solution.py:343
  26.0 7.3 %copy-start = (bf16[2,4,512,256]{3,2,1,0:T(8,128)(2,1)S(1)}, bf16[2,4,512,256]{3,2,1,0:T(8,128)(2,1)}, u32[]{:S(2)}) copy-start(bf16[2,4,512,256]{3,2,1,0:T(8,128)(2,1)} %refs_2_.1) | copy-start | bytes 6291460
  26.0 7.3 %copy-start.2 = (s32[4]{0:T(128)S(1)}, s32[4]{0:T(128)}, u32[]{:S(2)}) copy-start(s32[4]{0:T(128)} %lengths.1) | copy-start | bytes 52
  26.0 7.3 %copy-start.3 = (s32[32]{0:T(128)S(1)}, s32[32]{0:T(128)}, u32[]{:S(2)}) copy-start(s32[32]{0:T(128)} %arrivals.1) | copy-start | bytes 388
  26.1 7.3 %collective-permute-start.7 = (bf16[1184,128]{1,0:T(8,128)(2,1)S(1)}, bf16[1184,128]{1,0:T(8,128)(2,1)S(1)}, u32[]{:S(2)}, u32[]{:S(2)}) collective-permute-start(bf16[1184,128]{1,0:T(8,128)(2,1)S(1)} %shard_map.126), channel_id=1, source_target_pairs={{0,8},{4,12},{8,0},{12,4},{16,24},{20,28},{24,16},{28,20},{1,9},{5... | collective-permute-start | bytes 909320 | tf_op jit(solution)/shard_map/ppermute | solution.py:343

commit v4 on v3

--- a/solution.py
+++ b/solution.py
@@ -449,10 +449,11 @@
         )
 
     arrived = after(arrived, shared[0])
-    blocks = [arrived]
-    while len(blocks) * arrived.shape[0] * members < arrival_order.shape[0] * PAD_PARTS:
+    blocks, distance = [arrived], members
+    while distance < blk_count:
         full = blocks[0] if len(blocks) == 1 else jnp.concatenate(blocks, axis=0)
-        blocks = [full, exchange(full, "blk", members * full.shape[0] // arrived.shape[0])]
+        blocks = [full, exchange(full, "blk", distance)]
+        distance *= 2
     spare = sum(block.shape[0] for block in blocks)
     mine = attend(0, long_query, 0)
     backs = {}

time: 35.7 us -> 35.7 us (level)
  no operation moved by 1% of the time
where the time goes in v4:
time: 35.7 us; the launch traced here: 35.4 us
  starting transfers between devices  15.2 us (43%)
  Pallas kernels  14 us (39%)
  waiting for transfers between devices  5.41 us (15%)
  between operations  0.76 us (2%)
    ppermute x10, starting transfers between devices, exchange(): return lax.ppermute(block, axis, [(i, i ^ distance) for i in range(count)])  15.2 us
    pallas_call x8, Pallas kernels, call(): pl.pallas_call(kernel, in_specs=specs, out_specs=jax.tree.map(lambda _: N...  14 us
    ppermute x10, waiting for transfers between devices, exchange(): return lax.ppermute(block, axis, [(i, i ^ distance) for i in range(count)])  5.41 us
  transfers between devices with their start and end apart: 10, of which 4 were waited for; matrix products, arithmetic and copies ran while one was open for 0% of the time, Pallas kernels for 34%

profile of v4, /device:TPU:0, one launch (start us, length us, event | category | flops | bytes accessed | tf_op | source)
XLA Modules:
  0.0 35.4 jit_solution(53728974224622999)
XLA Ops:
  0.6 4.0 %collective-permute-start.8 = (bf16[128,1024]{1,0:T(8,128)(2,1)}, bf16[128,1024]{1,0:T(8,128)(2,1)S(1)}, u32[]{:S(2)}, u32[]{:S(2)}) collective-permute-start(bf16[128,1024]{1,0:T(8,128)(2,1)} %query.1), channel_id=1, source_target_pairs={{0,12},{4,8},{8,4},{12,0},{16,28},{20,24},{24,20},{28,16},{1,13},{... | collective-permute-start | bytes 786440 | tf_op jit(solution)/shard_map/ppermute | solution.py:343
  4.6 0.5 %collective-permute-start = (bf16[128,1024]{1,0:T(8,128)(2,1)}, bf16[128,1024]{1,0:T(8,128)(2,1)S(1)}, u32[]{:S(2)}, u32[]{:S(2)}) collective-permute-start(bf16[128,1024]{1,0:T(8,128)(2,1)} %query.1), channel_id=1, source_target_pairs={{0,4},{4,0},{8,12},{12,8},{16,20},{20,16},{24,28},{28,24},{1,5},{5... | collective-permute-start | bytes 786440 | tf_op jit(solution)/shard_map/ppermute | solution.py:343
  5.2 0.1 collective-permute-start.6
  5.3 0.8 %shard_map.124 = (bf16[16,128]{1,0:T(8,128)(2,1)S(1)}, bf16[16,128]{1,0:T(8,128)(2,1)S(1)}, bf16[16,128]{1,0:T(8,128)(2,1)S(1)}, bf16[16,128]{1,0:T(8,128)(2,1)S(1)}) custom-call(bf16[1,4096]{1,0:T(2,128)(2,1)} %query_far.1, bf16[1,2,1024]{2,1,0:T(2,128)(2,1)} %new_kv_far.3), custom_call_target="tpu_custom_call" | custom-call | tf_op jit(solution)/shard_map/pallas_call | solution.py:384
  6.1 0.1 collective-permute-start.1
  6.1 1.9 %collective-permute-start.2 = (bf16[16,128]{1,0:T(8,128)(2,1)S(1)}, bf16[16,128]{1,0:T(8,128)(2,1)S(1)}, u32[]{:S(2)}, u32[]{:S(2)}) collective-permute-start(bf16[16,128]{1,0:T(8,128)(2,1)S(1)} %get-tuple-element.20), channel_id=1, source_target_pairs={{0,2},{1,3},{2,0},{3,1},{4,6},{5,7},{6,4},{7,5},{8,10},{9,11},{10,... | collective-permute-start | bytes 12296 | tf_op jit(solution)/shard_map/ppermute | solution.py:343
  8.1 0.0 collective-permute-done.1
  8.1 0.9 %collective-permute-start.3 = (bf16[16,128]{1,0:T(8,128)(2,1)S(1)}, bf16[16,128]{1,0:T(8,128)(2,1)S(1)}, u32[]{:S(2)}, u32[]{:S(2)}) collective-permute-start(bf16[16,128]{1,0:T(8,128)(2,1)S(1)} %get-tuple-element.21), channel_id=1, source_target_pairs={{0,3},{1,2},{2,1},{3,0},{4,7},{5,6},{6,5},{7,4},{8,11},{9,10},{10,... | collective-permute-start | bytes 12296 | tf_op jit(solution)/shard_map/ppermute | solution.py:343
  8.9 1.9 %shard_map.122 = (bf16[1280,256]{1,0:T(8,128)(2,1)S(1)}, bf16[256,1280]{1,0:T(8,128)(2,1)S(1)}, f32[4,128,128]{2,1,0:T(8,128)S(1)}, f32[4,128,128]{2,1,0:T(8,128...) custom-call(s32[2]{0:T(128)} %lengths_far.1, s32[2]{0:T(128)} %offsets_far.1, ...), custom_call_target="tpu_custom_call" | custom-call | tf_op jit(solution)/shard_map/pallas_call | solution.py:384
  10.9 0.0 collective-permute-done.2
  10.9 0.2 collective-permute-done.3
  11.1 2.6 %collective-permute-start.4 = (bf16[64,128]{1,0:T(8,128)(2,1)S(1)}, bf16[64,128]{1,0:T(8,128)(2,1)S(1)}, u32[]{:S(2)}, u32[]{:S(2)}) collective-permute-start(bf16[64,128]{1,0:T(8,128)(2,1)S(1)} %pad_maximum_fusion.refs_0_), channel_id=1, source_target_pairs={{0,16},{4,20},{8,24},{12,28},{16,0},{20,4},{24,8},{28,12},{1,17},{... | collective-permute-start | bytes 49160 | tf_op jit(solution)/shard_map/ppermute | solution.py:343
  13.7 0.0 collective-permute-done.8.query
  13.7 2.3 %shard_map.127.block = bf16[1184,128]{1,0:T(8,128)(2,1)S(1)} custom-call(bf16[128,1024]{1,0:T(8,128)(2,1)S(1)} %collective-permute-done.8.query, bf16[1280,256]{1,0:T(8,128)(2,1)S(1)} %get-tuple-element.13.keys, bf16[256,1280]{1,0:T(8,128)(2,1)S(1)} %get-tuple-element.14.values_t, f32[4,128,128]{2,1,0:T(8,128)S(1)} %get-tuple-element.15.cosine, ...), custom_call_target="tpu_custom_call" | custom-call | tf_op jit(solution)/shard_map/pallas_call | solution.py:384
  16.0 0.5 %collective-permute-done.4.refs_1_ = bf16[64,128]{1,0:T(8,128)(2,1)S(1)} collective-permute-done((bf16[64,128]{1,0:T(8,128)(2,1)S(1)}, bf16[64,128]{1,0:T(8,128)(2,1)S(1)}, u32[]{:S(2)}, u32[]{:S(2)}) %collective-permute-start.4) | collective-permute-done | bytes 16416 | tf_op jit(solution)/shard_map/ppermute | solution.py:343
  16.4 3.5 %collective-permute-start.9 = (bf16[1184,128]{1,0:T(8,128)(2,1)S(1)}, bf16[1184,128]{1,0:T(8,128)(2,1)S(1)}, u32[]{:S(2)}, u32[]{:S(2)}) collective-permute-start(bf16[1184,128]{1,0:T(8,128)(2,1)S(1)} %shard_map.128), channel_id=1, source_target_pairs={{0,12},{4,8},{8,4},{12,0},{16,28},{20,24},{24,20},{28,16},{1,13},{... | collective-permute-start | bytes 909320 | tf_op jit(solution)/shard_map/ppermute | solution.py:343
  19.9 0.0 collective-permute-done.query
  19.9 2.3 %shard_map.125 = bf16[1184,128]{1,0:T(8,128)(2,1)S(1)} custom-call(bf16[128,1024]{1,0:T(8,128)(2,1)S(1)} %collective-permute-done.query, bf16[1280,256]{1,0:T(8,128)(2,1)S(1)} %get-tuple-element.13.keys, bf16[256,1280]{1,0:T(8,128)(2,1)S(1)} %get-tuple-element.14.values_t, f32[4,128,128]{2,1,0:T(8,128)S(1)} %get-tuple-element.15.cosine, ...), custom_call_target="tpu_custom_call" | custom-call | tf_op jit(solution)/shard_map/pallas_call | solution.py:384
  22.2 0.0 copy-start.1
  22.2 1.6 %collective-permute-start.5 = (bf16[1184,128]{1,0:T(8,128)(2,1)S(1)}, bf16[1184,128]{1,0:T(8,128)(2,1)S(1)}, u32[]{:S(2)}, u32[]{:S(2)}) collective-permute-start(bf16[1184,128]{1,0:T(8,128)(2,1)S(1)} %shard_map.125), channel_id=1, source_target_pairs={{0,4},{4,0},{8,12},{12,8},{16,20},{20,16},{24,28},{28,24},{1,5},{5... | collective-permute-start | bytes 909320 | tf_op jit(solution)/shard_map/ppermute | solution.py:343
  23.7 0.0 collective-permute-done.6.query
  23.7 2.3 %shard_map.126 = bf16[1184,128]{1,0:T(8,128)(2,1)S(1)} custom-call(bf16[128,1024]{1,0:T(8,128)(2,1)S(1)} %collective-permute-done.6.query, bf16[1280,256]{1,0:T(8,128)(2,1)S(1)} %get-tuple-element.13.keys, bf16[256,1280]{1,0:T(8,128)(2,1)S(1)} %get-tuple-element.14.values_t, f32[4,128,128]{2,1,0:T(8,128)S(1)} %get-tuple-element.15.cosine, ...), custom_call_target="tpu_custom_call" | custom-call | tf_op jit(solution)/shard_map/pallas_call | solution.py:384
  26.0 0.0 copy-start
  26.0 0.0 copy-start.2
  26.0 0.0 copy-start.3
  26.1 0.1 collective-permute-start.7
  26.1 2.4 %shard_map.123.own = f32[1032,128]{1,0:T(8,128)S(1)} custom-call(bf16[128,1024]{1,0:T(8,128)(2,1)S(1)} %copy-done.1, bf16[1280,256]{1,0:T(8,128)(2,1)S(1)} %get-tuple-element.13.keys, bf16[256,1280]{1,0:T(8,128)(2,1)S(1)} %get-tuple-element.14.values_t, f32[4,128,128]{2,1,0:T(8,128)S(1)} %get-tuple-element.15.cosine, ...), custom_call_target="tpu_custom_call" | custom-call | tf_op jit(solution)/shard_map/pallas_call | solution.py:384
  28.6 0.0 collective-permute-done.9.third
  28.6 4.1 %collective-permute-done.5.first = bf16[1184,128]{1,0:T(8,128)(2,1)S(1)} collective-permute-done((bf16[1184,128]{1,0:T(8,128)(2,1)S(1)}, bf16[1184,128]{1,0:T(8,128)(2,1)S(1)}, u32[]{:S(2)}, u32[]{:S(2)}) %collective-permute-start.5) | collective-permute-done | bytes 303136 | tf_op jit(solution)/shard_map/ppermute | solution.py:343
  32.7 0.6 %collective-permute-done.7.second = bf16[1184,128]{1,0:T(8,128)(2,1)S(1)} collective-permute-done((bf16[1184,128]{1,0:T(8,128)(2,1)S(1)}, bf16[1184,128]{1,0:T(8,128)(2,1)S(1)}, u32[]{:S(2)}, u32[]{:S(2)}) %collective-permute-start.7) | collective-permute-done | bytes 303136 | tf_op jit(solution)/shard_map/ppermute | solution.py:343
  33.3 0.0 copy-done
  33.3 2.1 %shard_map.129 = (bf16[128,1024]{1,0:T(8,128)(2,1)}, bf16[4,1024]{1,0:T(4,128)(2,1)}) custom-call(s32[4]{0:T(128)S(1)} %copy-done.2, s32[32]{0:T(128)S(1)} %copy-done.3, f32[1032,128]{1,0:T(8,128)S(1)} %shard_map.123.own, bf16[1184,128]{1,0:T(8,128)(2,1)S(1)} %collective-permute-done.5.first, bf16[1184,128]{1,0:T(8,128)(2,1)S(1)} %collective-permute-done.7.second, ...), custom_call_target="tpu_custom_call" | custom-call | tf_op jit(solution)/shard_map/pallas_call | solution.py:384
  (6 shorter events, 0.0 us)
Async XLA Ops:
  0.6 13.1 %collective-permute-start.8 = (bf16[128,1024]{1,0:T(8,128)(2,1)}, bf16[128,1024]{1,0:T(8,128)(2,1)S(1)}, u32[]{:S(2)}, u32[]{:S(2)}) collective-permute-start(bf16[128,1024]{1,0:T(8,128)(2,1)} %query.1), channel_id=1, source_target_pairs={{0,12},{4,8},{8,4},{12,0},{16,28},{20,24},{24,20},{28,16},{1,13},{... | collective-permute-start | bytes 786440 | tf_op jit(solution)/shard_map/ppermute | solution.py:343
  4.6 15.3 %collective-permute-start = (bf16[128,1024]{1,0:T(8,128)(2,1)}, bf16[128,1024]{1,0:T(8,128)(2,1)S(1)}, u32[]{:S(2)}, u32[]{:S(2)}) collective-permute-start(bf16[128,1024]{1,0:T(8,128)(2,1)} %query.1), channel_id=1, source_target_pairs={{0,4},{4,0},{8,12},{12,8},{16,20},{20,16},{24,28},{28,24},{1,5},{5... | collective-permute-start | bytes 786440 | tf_op jit(solution)/shard_map/ppermute | solution.py:343
  5.2 18.6 %collective-permute-start.6 = (bf16[128,1024]{1,0:T(8,128)(2,1)}, bf16[128,1024]{1,0:T(8,128)(2,1)S(1)}, u32[]{:S(2)}, u32[]{:S(2)}) collective-permute-start(bf16[128,1024]{1,0:T(8,128)(2,1)} %query.1), channel_id=1, source_target_pairs={{0,8},{4,12},{8,0},{12,4},{16,24},{20,28},{24,16},{28,20},{1,9},{5... | collective-permute-start | bytes 786440 | tf_op jit(solution)/shard_map/ppermute | solution.py:343
  6.1 2.0 %collective-permute-start.1 = (bf16[16,128]{1,0:T(8,128)(2,1)S(1)}, bf16[16,128]{1,0:T(8,128)(2,1)S(1)}, u32[]{:S(2)}, u32[]{:S(2)}) collective-permute-start(bf16[16,128]{1,0:T(8,128)(2,1)S(1)} %get-tuple-element.19), channel_id=1, source_target_pairs={{0,1},{1,0},{2,3},{3,2},{4,5},{5,4},{6,7},{7,6},{8,9},{9,8},{10,11... | collective-permute-start | bytes 12296 | tf_op jit(solution)/shard_map/ppermute | solution.py:343
  6.1 4.7 %collective-permute-start.2 = (bf16[16,128]{1,0:T(8,128)(2,1)S(1)}, bf16[16,128]{1,0:T(8,128)(2,1)S(1)}, u32[]{:S(2)}, u32[]{:S(2)}) collective-permute-start(bf16[16,128]{1,0:T(8,128)(2,1)S(1)} %get-tuple-element.20), channel_id=1, source_target_pairs={{0,2},{1,3},{2,0},{3,1},{4,6},{5,7},{6,4},{7,5},{8,10},{9,11},{10,... | collective-permute-start | bytes 12296 | tf_op jit(solution)/shard_map/ppermute | solution.py:343
  8.1 3.0 %collective-permute-start.3 = (bf16[16,128]{1,0:T(8,128)(2,1)S(1)}, bf16[16,128]{1,0:T(8,128)(2,1)S(1)}, u32[]{:S(2)}, u32[]{:S(2)}) collective-permute-start(bf16[16,128]{1,0:T(8,128)(2,1)S(1)} %get-tuple-element.21), channel_id=1, source_target_pairs={{0,3},{1,2},{2,1},{3,0},{4,7},{5,6},{6,5},{7,4},{8,11},{9,10},{10,... | collective-permute-start | bytes 12296 | tf_op jit(solution)/shard_map/ppermute | solution.py:343
  11.1 5.3 %collective-permute-start.4 = (bf16[64,128]{1,0:T(8,128)(2,1)S(1)}, bf16[64,128]{1,0:T(8,128)(2,1)S(1)}, u32[]{:S(2)}, u32[]{:S(2)}) collective-permute-start(bf16[64,128]{1,0:T(8,128)(2,1)S(1)} %pad_maximum_fusion.refs_0_), channel_id=1, source_target_pairs={{0,16},{4,20},{8,24},{12,28},{16,0},{20,4},{24,8},{28,12},{1,17},{... | collective-permute-start | bytes 49160 | tf_op jit(solution)/shard_map/ppermute | solution.py:343
  16.4 12.1 %collective-permute-start.9 = (bf16[1184,128]{1,0:T(8,128)(2,1)S(1)}, bf16[1184,128]{1,0:T(8,128)(2,1)S(1)}, u32[]{:S(2)}, u32[]{:S(2)}) collective-permute-start(bf16[1184,128]{1,0:T(8,128)(2,1)S(1)} %shard_map.128), channel_id=1, source_target_pairs={{0,12},{4,8},{8,4},{12,0},{16,28},{20,24},{24,20},{28,16},{1,13},{... | collective-permute-start | bytes 909320 | tf_op jit(solution)/shard_map/ppermute | solution.py:343
  22.2 4.0 %copy-start.1 = (bf16[128,1024]{1,0:T(8,128)(2,1)S(1)}, bf16[128,1024]{1,0:T(8,128)(2,1)}, u32[]{:S(2)}) copy-start(bf16[128,1024]{1,0:T(8,128)(2,1)} %query.1) | copy-start | bytes 786436
  22.2 10.5 %collective-permute-start.5 = (bf16[1184,128]{1,0:T(8,128)(2,1)S(1)}, bf16[1184,128]{1,0:T(8,128)(2,1)S(1)}, u32[]{:S(2)}, u32[]{:S(2)}) collective-permute-start(bf16[1184,128]{1,0:T(8,128)(2,1)S(1)} %shard_map.125), channel_id=1, source_target_pairs={{0,4},{4,0},{8,12},{12,8},{16,20},{20,16},{24,28},{28,24},{1,5},{5... | collective-permute-start | bytes 909320 | tf_op jit(solution)/shard_map/ppermute | solution.py:343
  26.0 7.3 %copy-start = (bf16[2,4,512,256]{3,2,1,0:T(8,128)(2,1)S(1)}, bf16[2,4,512,256]{3,2,1,0:T(8,128)(2,1)}, u32[]{:S(2)}) copy-start(bf16[2,4,512,256]{3,2,1,0:T(8,128)(2,1)} %refs_2_.1) | copy-start | bytes 6291460
  26.0 7.3 %copy-start.2 = (s32[4]{0:T(128)S(1)}, s32[4]{0:T(128)}, u32[]{:S(2)}) copy-start(s32[4]{0:T(128)} %lengths.1) | copy-start | bytes 52
  26.0 7.3 %copy-start.3 = (s32[32]{0:T(128)S(1)}, s32[32]{0:T(128)}, u32[]{:S(2)}) copy-start(s32[32]{0:T(128)} %arrivals.1) | copy-start | bytes 388
  26.1 7.3 %collective-permute-start.7 = (bf16[1184,128]{1,0:T(8,128)(2,1)S(1)}, bf16[1184,128]{1,0:T(8,128)(2,1)S(1)}, u32[]{:S(2)}, u32[]{:S(2)}) collective-permute-start(bf16[1184,128]{1,0:T(8,128)(2,1)S(1)} %shard_map.126), channel_id=1, source_target_pairs={{0,8},{4,12},{8,0},{12,4},{16,24},{20,28},{24,16},{28,20},{1,9},{5... | collective-permute-start | bytes 909320 | tf_op jit(solution)/shard_map/ppermute | solution.py:343

commit v5 on v4

--- a/solution.py
+++ b/solution.py
@@ -179,43 +179,63 @@
     kv_heads = keys.shape[1] // D
     group = query.shape[1] // D // kv_heads
     total = keys.shape[0] if own else keys.shape[0] - D
-    logs = []
-    for kv in range(kv_heads):
+    share = group
+    heads = kv_heads * group
+    units = heads // share
+    blocks, tops, masses, logs = {}, {}, {}, []
+
+    def score_unit(unit, low):
+        kv = unit
         lanes = slice(kv * D, (kv + 1) * D)
-        turned = []
-        for head in range(kv * group, (kv + 1) * group):
-            x = query[:, head * D : (head + 1) * D].astype(jnp.float32)
-            turned.append(turn(x, cosine[part], sine[part]).astype(jnp.bfloat16))
-        block = jnp.concatenate(turned, axis=0)
-        top = None
-        for low in range(0, total, D):
-            chunk = keys[low : low + D, lanes]
-            mask = bias[part, low : low + D]
-            s = lax.dot_general(
-                chunk, block, (((1,), (1,)), ((), ())), preferred_element_type=jnp.float32
-            )
-            s = s + jnp.concatenate([mask] * group, axis=1)
-            scores[kv, low : low + D, :] = s
-            peak = jnp.max(s.reshape(D // 8, 8, group * rows), axis=0)
-            top = peak if top is None else jnp.maximum(top, peak)
-        top = jnp.max(top, axis=0, keepdims=True)
-        mass = jnp.zeros((8, group * rows), jnp.float32)
-        for low in range(0, total, D):
-            w = jnp.exp2((scores[kv, low : low + D, :] - top) * LOG2_SCALE)
-            mass = mass + jnp.sum(w.reshape(D // 8, 8, group * rows), axis=0)
-            weights[kv, low : low + D, :] = w.astype(jnp.bfloat16)
-        mass = jnp.sum(mass, axis=0, keepdims=True)
+        if low == 0:
+            turned = []
+            for head in range(unit * share, (unit + 1) * share):
+                x = query[:, head * D : (head + 1) * D].astype(jnp.float32)
+                turned.append(turn(x, cosine[part], sine[part]).astype(jnp.bfloat16))
+            blocks[unit] = jnp.concatenate(turned, axis=0)
+        s = lax.dot_general(
+            keys[low : low + D, lanes],
+            blocks[unit],
+            (((1,), (1,)), ((), ())),
+            preferred_element_type=jnp.float32,
+        )
+        s = s + jnp.concatenate([bias[part, low : low + D]] * share, axis=1)
+        scores[unit, low : low + D, :] = s
+        peak = jnp.max(s.reshape(D // 8, 8, share * rows), axis=0)
+        tops[unit] = peak if low == 0 else jnp.maximum(tops[unit], peak)
+
+    def weigh_unit(unit, low):
+        if low == 0:
+            tops[unit] = jnp.max(tops[unit], axis=0, keepdims=True)
+        w = jnp.exp2((scores[unit, low : low + D, :] - tops[unit]) * LOG2_SCALE)
+        mass = jnp.sum(w.reshape(D // 8, 8, share * rows), axis=0)
+        masses[unit] = mass if low == 0 else masses[unit] + mass
+        weights[unit, low : low + D, :] = w.astype(jnp.bfloat16)
+
+    def finish_unit(unit):
+        kv = unit
+        mass = jnp.sum(masses[unit], axis=0, keepdims=True)
         mix = jnp.dot(
-            values_t[lanes, :total], weights[kv, :total, :], preferred_element_type=jnp.float32
+            values_t[kv * D : (kv + 1) * D, :total],
+            weights[unit, :total, :],
+            preferred_element_type=jnp.float32,
         )
         mix = mix * (1.0 / mass)
-        log = top * LOG2_SCALE + jnp.log2(mass)
-        for j in range(group):
-            head = kv * group + j
+        log = tops[unit] * LOG2_SCALE + jnp.log2(mass)
+        for j in range(share):
+            head = unit * share + j
             out[head * D : (head + 1) * D, :] = mix[:, j * rows : (j + 1) * rows].astype(out.dtype)
             logs.append(log[:, j * rows : (j + 1) * rows])
+
+    for step in range(units + 2):
+        if step >= 2:
+            finish_unit(step - 2)
+        for low in range(0, total, D):
+            if step < units:
+                score_unit(step, low)
+            if 1 <= step <= units:
+                weigh_unit(step - 1, low)
     log = jnp.concatenate(logs, axis=0)
-    heads = len(logs)
     if own:
         out[heads * D :, :] = log
     else:

time: 35.7 us -> 35.2 us (0.986)
  Pallas kernels: 14 us -> 13 us
  waiting for transfers between devices: 5.41 us -> 5.89 us
    pallas_call x8, Pallas kernels: 14 us -> 13 us  [call(): pl.pallas_call(kernel, in_specs=specs, out_specs=jax.tree.map(lambda _: N...]
    ppermute x10, waiting for transfers between devices: 5.41 us -> 5.89 us  [exchange(): return lax.ppermute(block, axis, [(i, i ^ distance) for i in range(count)])]
  transfers between devices with their start and end apart: 10 -> 10, of which waited for: 4 -> 4; matrix products, arithmetic and copies ran while one was open for 0% -> 0% of each run, Pallas kernels for 34% -> 31%
where the time goes in v5:
time: 35.2 us; the launch traced here: 34.9 us
  starting transfers between devices  15.2 us (43%)
  Pallas kernels  13 us (37%)
  waiting for transfers between devices  5.89 us (17%)
  between operations  0.76 us (2%)
    ppermute x10, starting transfers between devices, exchange(): return lax.ppermute(block, axis, [(i, i ^ distance) for i in range(count)])  15.2 us
    pallas_call x8, Pallas kernels, call(): pl.pallas_call(kernel, in_specs=specs, out_specs=jax.tree.map(lambda _: N...  13 us
    ppermute x10, waiting for transfers between devices, exchange(): return lax.ppermute(block, axis, [(i, i ^ distance) for i in range(count)])  5.89 us
  transfers between devices with their start and end apart: 10, of which 4 were waited for; matrix products, arithmetic and copies ran while one was open for 0% of the time, Pallas kernels for 31%

profile of v5, /device:TPU:0, one launch (start us, length us, event | category | flops | bytes accessed | tf_op | source)
XLA Modules:
  0.0 34.9 jit_solution(2843364106849047695)
XLA Ops:
  0.6 4.0 %collective-permute-start.8 = (bf16[128,1024]{1,0:T(8,128)(2,1)}, bf16[128,1024]{1,0:T(8,128)(2,1)S(1)}, u32[]{:S(2)}, u32[]{:S(2)}) collective-permute-start(bf16[128,1024]{1,0:T(8,128)(2,1)} %query.1), channel_id=1, source_target_pairs={{0,12},{4,8},{8,4},{12,0},{16,28},{20,24},{24,20},{28,16},{1,13},{... | collective-permute-start | bytes 786440 | tf_op jit(solution)/shard_map/ppermute | solution.py:363
  4.6 0.5 %collective-permute-start = (bf16[128,1024]{1,0:T(8,128)(2,1)}, bf16[128,1024]{1,0:T(8,128)(2,1)S(1)}, u32[]{:S(2)}, u32[]{:S(2)}) collective-permute-start(bf16[128,1024]{1,0:T(8,128)(2,1)} %query.1), channel_id=1, source_target_pairs={{0,4},{4,0},{8,12},{12,8},{16,20},{20,16},{24,28},{28,24},{1,5},{5... | collective-permute-start | bytes 786440 | tf_op jit(solution)/shard_map/ppermute | solution.py:363
  5.2 0.1 collective-permute-start.6
  5.3 0.8 %shard_map.124 = (bf16[16,128]{1,0:T(8,128)(2,1)S(1)}, bf16[16,128]{1,0:T(8,128)(2,1)S(1)}, bf16[16,128]{1,0:T(8,128)(2,1)S(1)}, bf16[16,128]{1,0:T(8,128)(2,1)S(1)}) custom-call(bf16[1,4096]{1,0:T(2,128)(2,1)} %query_far.1, bf16[1,2,1024]{2,1,0:T(2,128)(2,1)} %new_kv_far.3), custom_call_target="tpu_custom_call" | custom-call | tf_op jit(solution)/shard_map/pallas_call | solution.py:404
  6.1 0.1 collective-permute-start.1
  6.1 1.9 %collective-permute-start.2 = (bf16[16,128]{1,0:T(8,128)(2,1)S(1)}, bf16[16,128]{1,0:T(8,128)(2,1)S(1)}, u32[]{:S(2)}, u32[]{:S(2)}) collective-permute-start(bf16[16,128]{1,0:T(8,128)(2,1)S(1)} %get-tuple-element.20), channel_id=1, source_target_pairs={{0,2},{1,3},{2,0},{3,1},{4,6},{5,7},{6,4},{7,5},{8,10},{9,11},{10,... | collective-permute-start | bytes 12296 | tf_op jit(solution)/shard_map/ppermute | solution.py:363
  8.1 0.0 collective-permute-done.1
  8.1 0.9 %collective-permute-start.3 = (bf16[16,128]{1,0:T(8,128)(2,1)S(1)}, bf16[16,128]{1,0:T(8,128)(2,1)S(1)}, u32[]{:S(2)}, u32[]{:S(2)}) collective-permute-start(bf16[16,128]{1,0:T(8,128)(2,1)S(1)} %get-tuple-element.21), channel_id=1, source_target_pairs={{0,3},{1,2},{2,1},{3,0},{4,7},{5,6},{6,5},{7,4},{8,11},{9,10},{10,... | collective-permute-start | bytes 12296 | tf_op jit(solution)/shard_map/ppermute | solution.py:363
  8.9 1.9 %shard_map.122 = (bf16[1280,256]{1,0:T(8,128)(2,1)S(1)}, bf16[256,1280]{1,0:T(8,128)(2,1)S(1)}, f32[4,128,128]{2,1,0:T(8,128)S(1)}, f32[4,128,128]{2,1,0:T(8,128...) custom-call(s32[2]{0:T(128)} %lengths_far.1, s32[2]{0:T(128)} %offsets_far.1, ...), custom_call_target="tpu_custom_call" | custom-call | tf_op jit(solution)/shard_map/pallas_call | solution.py:404
  10.9 0.0 collective-permute-done.2
  10.9 0.2 collective-permute-done.3
  11.1 2.6 %collective-permute-start.4 = (bf16[64,128]{1,0:T(8,128)(2,1)S(1)}, bf16[64,128]{1,0:T(8,128)(2,1)S(1)}, u32[]{:S(2)}, u32[]{:S(2)}) collective-permute-start(bf16[64,128]{1,0:T(8,128)(2,1)S(1)} %pad_maximum_fusion.refs_0_), channel_id=1, source_target_pairs={{0,16},{4,20},{8,24},{12,28},{16,0},{20,4},{24,8},{28,12},{1,17},{... | collective-permute-start | bytes 49160 | tf_op jit(solution)/shard_map/ppermute | solution.py:363
  13.7 0.0 collective-permute-done.8.query
  13.7 2.0 %shard_map.127.block = bf16[1184,128]{1,0:T(8,128)(2,1)S(1)} custom-call(bf16[128,1024]{1,0:T(8,128)(2,1)S(1)} %collective-permute-done.8.query, bf16[1280,256]{1,0:T(8,128)(2,1)S(1)} %get-tuple-element.13.keys, bf16[256,1280]{1,0:T(8,128)(2,1)S(1)} %get-tuple-element.14.values_t, f32[4,128,128]{2,1,0:T(8,128)S(1)} %get-tuple-element.15.cosine, ...), custom_call_target="tpu_custom_call" | custom-call | tf_op jit(solution)/shard_map/pallas_call | solution.py:404
  15.7 0.7 %collective-permute-done.4.refs_1_ = bf16[64,128]{1,0:T(8,128)(2,1)S(1)} collective-permute-done((bf16[64,128]{1,0:T(8,128)(2,1)S(1)}, bf16[64,128]{1,0:T(8,128)(2,1)S(1)}, u32[]{:S(2)}, u32[]{:S(2)}) %collective-permute-start.4) | collective-permute-done | bytes 16416 | tf_op jit(solution)/shard_map/ppermute | solution.py:363
  16.4 3.5 %collective-permute-start.9 = (bf16[1184,128]{1,0:T(8,128)(2,1)S(1)}, bf16[1184,128]{1,0:T(8,128)(2,1)S(1)}, u32[]{:S(2)}, u32[]{:S(2)}) collective-permute-start(bf16[1184,128]{1,0:T(8,128)(2,1)S(1)} %shard_map.128), channel_id=1, source_target_pairs={{0,12},{4,8},{8,4},{12,0},{16,28},{20,24},{24,20},{28,16},{1,13},{... | collective-permute-start | bytes 909320 | tf_op jit(solution)/shard_map/ppermute | solution.py:363
  19.9 0.0 collective-permute-done.query
  19.9 2.0 %shard_map.125 = bf16[1184,128]{1,0:T(8,128)(2,1)S(1)} custom-call(bf16[128,1024]{1,0:T(8,128)(2,1)S(1)} %collective-permute-done.query, bf16[1280,256]{1,0:T(8,128)(2,1)S(1)} %get-tuple-element.13.keys, bf16[256,1280]{1,0:T(8,128)(2,1)S(1)} %get-tuple-element.14.values_t, f32[4,128,128]{2,1,0:T(8,128)S(1)} %get-tuple-element.15.cosine, ...), custom_call_target="tpu_custom_call" | custom-call | tf_op jit(solution)/shard_map/pallas_call | solution.py:404
  21.9 0.0 copy-start.1
  22.0 1.6 %collective-permute-start.5 = (bf16[1184,128]{1,0:T(8,128)(2,1)S(1)}, bf16[1184,128]{1,0:T(8,128)(2,1)S(1)}, u32[]{:S(2)}, u32[]{:S(2)}) collective-permute-start(bf16[1184,128]{1,0:T(8,128)(2,1)S(1)} %shard_map.125), channel_id=1, source_target_pairs={{0,4},{4,0},{8,12},{12,8},{16,20},{20,16},{24,28},{28,24},{1,5},{5... | collective-permute-start | bytes 909320 | tf_op jit(solution)/shard_map/ppermute | solution.py:363
  23.5 0.0 collective-permute-done.6.query
  23.5 2.0 %shard_map.126 = bf16[1184,128]{1,0:T(8,128)(2,1)S(1)} custom-call(bf16[128,1024]{1,0:T(8,128)(2,1)S(1)} %collective-permute-done.6.query, bf16[1280,256]{1,0:T(8,128)(2,1)S(1)} %get-tuple-element.13.keys, bf16[256,1280]{1,0:T(8,128)(2,1)S(1)} %get-tuple-element.14.values_t, f32[4,128,128]{2,1,0:T(8,128)S(1)} %get-tuple-element.15.cosine, ...), custom_call_target="tpu_custom_call" | custom-call | tf_op jit(solution)/shard_map/pallas_call | solution.py:404
  25.5 0.0 copy-start
  25.6 0.0 copy-start.2
  25.6 0.0 copy-start.3
  25.6 0.1 collective-permute-start.7
  25.7 2.2 %shard_map.123.own = f32[1032,128]{1,0:T(8,128)S(1)} custom-call(bf16[128,1024]{1,0:T(8,128)(2,1)S(1)} %copy-done.1, bf16[1280,256]{1,0:T(8,128)(2,1)S(1)} %get-tuple-element.13.keys, bf16[256,1280]{1,0:T(8,128)(2,1)S(1)} %get-tuple-element.14.values_t, f32[4,128,128]{2,1,0:T(8,128)S(1)} %get-tuple-element.15.cosine, ...), custom_call_target="tpu_custom_call" | custom-call | tf_op jit(solution)/shard_map/pallas_call | solution.py:404
  27.9 0.0 collective-permute-done.9.third
  27.9 4.6 %collective-permute-done.5.first = bf16[1184,128]{1,0:T(8,128)(2,1)S(1)} collective-permute-done((bf16[1184,128]{1,0:T(8,128)(2,1)S(1)}, bf16[1184,128]{1,0:T(8,128)(2,1)S(1)}, u32[]{:S(2)}, u32[]{:S(2)}) %collective-permute-start.5) | collective-permute-done | bytes 303136 | tf_op jit(solution)/shard_map/ppermute | solution.py:363
  32.5 0.4 %collective-permute-done.7.second = bf16[1184,128]{1,0:T(8,128)(2,1)S(1)} collective-permute-done((bf16[1184,128]{1,0:T(8,128)(2,1)S(1)}, bf16[1184,128]{1,0:T(8,128)(2,1)S(1)}, u32[]{:S(2)}, u32[]{:S(2)}) %collective-permute-start.7) | collective-permute-done | bytes 303136 | tf_op jit(solution)/shard_map/ppermute | solution.py:363
  32.8 0.0 copy-done
  32.9 2.1 %shard_map.129 = (bf16[128,1024]{1,0:T(8,128)(2,1)}, bf16[4,1024]{1,0:T(4,128)(2,1)}) custom-call(s32[4]{0:T(128)S(1)} %copy-done.2, s32[32]{0:T(128)S(1)} %copy-done.3, f32[1032,128]{1,0:T(8,128)S(1)} %shard_map.123.own, bf16[1184,128]{1,0:T(8,128)(2,1)S(1)} %collective-permute-done.5.first, bf16[1184,128]{1,0:T(8,128)(2,1)S(1)} %collective-permute-done.7.second, ...), custom_call_target="tpu_custom_call" | custom-call | tf_op jit(solution)/shard_map/pallas_call | solution.py:404
  (6 shorter events, 0.0 us)
Async XLA Ops:
  0.6 13.1 %collective-permute-start.8 = (bf16[128,1024]{1,0:T(8,128)(2,1)}, bf16[128,1024]{1,0:T(8,128)(2,1)S(1)}, u32[]{:S(2)}, u32[]{:S(2)}) collective-permute-start(bf16[128,1024]{1,0:T(8,128)(2,1)} %query.1), channel_id=1, source_target_pairs={{0,12},{4,8},{8,4},{12,0},{16,28},{20,24},{24,20},{28,16},{1,13},{... | collective-permute-start | bytes 786440 | tf_op jit(solution)/shard_map/ppermute | solution.py:363
  4.6 15.3 %collective-permute-start = (bf16[128,1024]{1,0:T(8,128)(2,1)}, bf16[128,1024]{1,0:T(8,128)(2,1)S(1)}, u32[]{:S(2)}, u32[]{:S(2)}) collective-permute-start(bf16[128,1024]{1,0:T(8,128)(2,1)} %query.1), channel_id=1, source_target_pairs={{0,4},{4,0},{8,12},{12,8},{16,20},{20,16},{24,28},{28,24},{1,5},{5... | collective-permute-start | bytes 786440 | tf_op jit(solution)/shard_map/ppermute | solution.py:363
  5.2 18.3 %collective-permute-start.6 = (bf16[128,1024]{1,0:T(8,128)(2,1)}, bf16[128,1024]{1,0:T(8,128)(2,1)S(1)}, u32[]{:S(2)}, u32[]{:S(2)}) collective-permute-start(bf16[128,1024]{1,0:T(8,128)(2,1)} %query.1), channel_id=1, source_target_pairs={{0,8},{4,12},{8,0},{12,4},{16,24},{20,28},{24,16},{28,20},{1,9},{5... | collective-permute-start | bytes 786440 | tf_op jit(solution)/shard_map/ppermute | solution.py:363
  6.1 2.0 %collective-permute-start.1 = (bf16[16,128]{1,0:T(8,128)(2,1)S(1)}, bf16[16,128]{1,0:T(8,128)(2,1)S(1)}, u32[]{:S(2)}, u32[]{:S(2)}) collective-permute-start(bf16[16,128]{1,0:T(8,128)(2,1)S(1)} %get-tuple-element.19), channel_id=1, source_target_pairs={{0,1},{1,0},{2,3},{3,2},{4,5},{5,4},{6,7},{7,6},{8,9},{9,8},{10,11... | collective-permute-start | bytes 12296 | tf_op jit(solution)/shard_map/ppermute | solution.py:363
  6.1 4.7 %collective-permute-start.2 = (bf16[16,128]{1,0:T(8,128)(2,1)S(1)}, bf16[16,128]{1,0:T(8,128)(2,1)S(1)}, u32[]{:S(2)}, u32[]{:S(2)}) collective-permute-start(bf16[16,128]{1,0:T(8,128)(2,1)S(1)} %get-tuple-element.20), channel_id=1, source_target_pairs={{0,2},{1,3},{2,0},{3,1},{4,6},{5,7},{6,4},{7,5},{8,10},{9,11},{10,... | collective-permute-start | bytes 12296 | tf_op jit(solution)/shard_map/ppermute | solution.py:363
  8.1 3.0 %collective-permute-start.3 = (bf16[16,128]{1,0:T(8,128)(2,1)S(1)}, bf16[16,128]{1,0:T(8,128)(2,1)S(1)}, u32[]{:S(2)}, u32[]{:S(2)}) collective-permute-start(bf16[16,128]{1,0:T(8,128)(2,1)S(1)} %get-tuple-element.21), channel_id=1, source_target_pairs={{0,3},{1,2},{2,1},{3,0},{4,7},{5,6},{6,5},{7,4},{8,11},{9,10},{10,... | collective-permute-start | bytes 12296 | tf_op jit(solution)/shard_map/ppermute | solution.py:363
  11.1 5.3 %collective-permute-start.4 = (bf16[64,128]{1,0:T(8,128)(2,1)S(1)}, bf16[64,128]{1,0:T(8,128)(2,1)S(1)}, u32[]{:S(2)}, u32[]{:S(2)}) collective-permute-start(bf16[64,128]{1,0:T(8,128)(2,1)S(1)} %pad_maximum_fusion.refs_0_), channel_id=1, source_target_pairs={{0,16},{4,20},{8,24},{12,28},{16,0},{20,4},{24,8},{28,12},{1,17},{... | collective-permute-start | bytes 49160 | tf_op jit(solution)/shard_map/ppermute | solution.py:363
  16.4 11.4 %collective-permute-start.9 = (bf16[1184,128]{1,0:T(8,128)(2,1)S(1)}, bf16[1184,128]{1,0:T(8,128)(2,1)S(1)}, u32[]{:S(2)}, u32[]{:S(2)}) collective-permute-start(bf16[1184,128]{1,0:T(8,128)(2,1)S(1)} %shard_map.128), channel_id=1, source_target_pairs={{0,12},{4,8},{8,4},{12,0},{16,28},{20,24},{24,20},{28,16},{1,13},{... | collective-permute-start | bytes 909320 | tf_op jit(solution)/shard_map/ppermute | solution.py:363
  21.9 3.7 %copy-start.1 = (bf16[128,1024]{1,0:T(8,128)(2,1)S(1)}, bf16[128,1024]{1,0:T(8,128)(2,1)}, u32[]{:S(2)}) copy-start(bf16[128,1024]{1,0:T(8,128)(2,1)} %query.1) | copy-start | bytes 786436
  22.0 10.5 %collective-permute-start.5 = (bf16[1184,128]{1,0:T(8,128)(2,1)S(1)}, bf16[1184,128]{1,0:T(8,128)(2,1)S(1)}, u32[]{:S(2)}, u32[]{:S(2)}) collective-permute-start(bf16[1184,128]{1,0:T(8,128)(2,1)S(1)} %shard_map.125), channel_id=1, source_target_pairs={{0,4},{4,0},{8,12},{12,8},{16,20},{20,16},{24,28},{28,24},{1,5},{5... | collective-permute-start | bytes 909320 | tf_op jit(solution)/shard_map/ppermute | solution.py:363
  25.5 7.3 %copy-start = (bf16[2,4,512,256]{3,2,1,0:T(8,128)(2,1)S(1)}, bf16[2,4,512,256]{3,2,1,0:T(8,128)(2,1)}, u32[]{:S(2)}) copy-start(bf16[2,4,512,256]{3,2,1,0:T(8,128)(2,1)} %refs_2_.1) | copy-start | bytes 6291460
  25.6 7.3 %copy-start.2 = (s32[4]{0:T(128)S(1)}, s32[4]{0:T(128)}, u32[]{:S(2)}) copy-start(s32[4]{0:T(128)} %lengths.1) | copy-start | bytes 52
  25.6 7.3 %copy-start.3 = (s32[32]{0:T(128)S(1)}, s32[32]{0:T(128)}, u32[]{:S(2)}) copy-start(s32[32]{0:T(128)} %arrivals.1) | copy-start | bytes 388
  25.6 7.3 %collective-permute-start.7 = (bf16[1184,128]{1,0:T(8,128)(2,1)S(1)}, bf16[1184,128]{1,0:T(8,128)(2,1)S(1)}, u32[]{:S(2)}, u32[]{:S(2)}) collective-permute-start(bf16[1184,128]{1,0:T(8,128)(2,1)S(1)} %shard_map.126), channel_id=1, source_target_pairs={{0,8},{4,12},{8,0},{12,4},{16,24},{20,28},{24,16},{28,20},{1,9},{5... | collective-permute-start | bytes 909320 | tf_op jit(solution)/shard_map/ppermute | solution.py:363

commit v6 on v5

--- a/solution.py
+++ b/solution.py
@@ -289,7 +289,7 @@
         owner = arrivals[i] - blk * count
         return tuple(jnp.where(owner == n, i, was) for n, was in enumerate(found))
 
-    found = lax.fori_loop(0, arrivals.shape[0], look, (jnp.int32(0),) * count, unroll=8)
+    found = lax.fori_loop(0, arrivals.shape[0], look, (jnp.int32(0),) * count, unroll=min(32, arrivals.shape[0]))
     head_of = lax.broadcasted_iota(jnp.int32, (heads, D), 0) // group
     slot = lax.broadcasted_iota(jnp.int32, (heads, slots), 1)
     scores, own_scores, new_values = [], [], []

time: 35.2 us -> 35.1 us (level)
  transfers between devices with their start and end apart: 10 -> 10, of which waited for: 4 -> 4; matrix products, arithmetic and copies ran while one was open for 0% -> 0% of each run, Pallas kernels for 31% -> 32%
where the time goes in v6:
time: 35.1 us; the launch traced here: 34.8 us
  starting transfers between devices  15.2 us (43%)
  Pallas kernels  13 us (37%)
  waiting for transfers between devices  5.89 us (17%)
  between operations  0.76 us (2%)
    ppermute x10, starting transfers between devices, exchange(): return lax.ppermute(block, axis, [(i, i ^ distance) for i in range(count)])  15.2 us
    pallas_call x8, Pallas kernels, call(): pl.pallas_call(kernel, in_specs=specs, out_specs=jax.tree.map(lambda _: N...  13 us
    ppermute x10, waiting for transfers between devices, exchange(): return lax.ppermute(block, axis, [(i, i ^ distance) for i in range(count)])  5.89 us
  transfers between devices with their start and end apart: 10, of which 4 were waited for; matrix products, arithmetic and copies ran while one was open for 0% of the time, Pallas kernels for 32%

profile of v6, /device:TPU:0, one launch (start us, length us, event | category | flops | bytes accessed | tf_op | source)
XLA Modules:
  0.0 34.8 jit_solution(5678978646411717576)
XLA Ops:
  0.6 4.0 %collective-permute-start.8 = (bf16[128,1024]{1,0:T(8,128)(2,1)}, bf16[128,1024]{1,0:T(8,128)(2,1)S(1)}, u32[]{:S(2)}, u32[]{:S(2)}) collective-permute-start(bf16[128,1024]{1,0:T(8,128)(2,1)} %query.1), channel_id=1, source_target_pairs={{0,12},{4,8},{8,4},{12,0},{16,28},{20,24},{24,20},{28,16},{1,13},{... | collective-permute-start | bytes 786440 | tf_op jit(solution)/shard_map/ppermute | solution.py:363
  4.6 0.5 %collective-permute-start = (bf16[128,1024]{1,0:T(8,128)(2,1)}, bf16[128,1024]{1,0:T(8,128)(2,1)S(1)}, u32[]{:S(2)}, u32[]{:S(2)}) collective-permute-start(bf16[128,1024]{1,0:T(8,128)(2,1)} %query.1), channel_id=1, source_target_pairs={{0,4},{4,0},{8,12},{12,8},{16,20},{20,16},{24,28},{28,24},{1,5},{5... | collective-permute-start | bytes 786440 | tf_op jit(solution)/shard_map/ppermute | solution.py:363
  5.2 0.1 collective-permute-start.6
  5.3 0.8 %shard_map.124 = (bf16[16,128]{1,0:T(8,128)(2,1)S(1)}, bf16[16,128]{1,0:T(8,128)(2,1)S(1)}, bf16[16,128]{1,0:T(8,128)(2,1)S(1)}, bf16[16,128]{1,0:T(8,128)(2,1)S(1)}) custom-call(bf16[1,4096]{1,0:T(2,128)(2,1)} %query_far.1, bf16[1,2,1024]{2,1,0:T(2,128)(2,1)} %new_kv_far.3), custom_call_target="tpu_custom_call" | custom-call | tf_op jit(solution)/shard_map/pallas_call | solution.py:404
  6.1 0.1 collective-permute-start.1
  6.1 1.9 %collective-permute-start.2 = (bf16[16,128]{1,0:T(8,128)(2,1)S(1)}, bf16[16,128]{1,0:T(8,128)(2,1)S(1)}, u32[]{:S(2)}, u32[]{:S(2)}) collective-permute-start(bf16[16,128]{1,0:T(8,128)(2,1)S(1)} %get-tuple-element.20), channel_id=1, source_target_pairs={{0,2},{1,3},{2,0},{3,1},{4,6},{5,7},{6,4},{7,5},{8,10},{9,11},{10,... | collective-permute-start | bytes 12296 | tf_op jit(solution)/shard_map/ppermute | solution.py:363
  8.1 0.0 collective-permute-done.1
  8.1 0.9 %collective-permute-start.3 = (bf16[16,128]{1,0:T(8,128)(2,1)S(1)}, bf16[16,128]{1,0:T(8,128)(2,1)S(1)}, u32[]{:S(2)}, u32[]{:S(2)}) collective-permute-start(bf16[16,128]{1,0:T(8,128)(2,1)S(1)} %get-tuple-element.21), channel_id=1, source_target_pairs={{0,3},{1,2},{2,1},{3,0},{4,7},{5,6},{6,5},{7,4},{8,11},{9,10},{10,... | collective-permute-start | bytes 12296 | tf_op jit(solution)/shard_map/ppermute | solution.py:363
  8.9 1.9 %shard_map.122 = (bf16[1280,256]{1,0:T(8,128)(2,1)S(1)}, bf16[256,1280]{1,0:T(8,128)(2,1)S(1)}, f32[4,128,128]{2,1,0:T(8,128)S(1)}, f32[4,128,128]{2,1,0:T(8,128...) custom-call(s32[2]{0:T(128)} %lengths_far.1, s32[2]{0:T(128)} %offsets_far.1, ...), custom_call_target="tpu_custom_call" | custom-call | tf_op jit(solution)/shard_map/pallas_call | solution.py:404
  10.9 0.0 collective-permute-done.2
  10.9 0.2 collective-permute-done.3
  11.1 2.6 %collective-permute-start.4 = (bf16[64,128]{1,0:T(8,128)(2,1)S(1)}, bf16[64,128]{1,0:T(8,128)(2,1)S(1)}, u32[]{:S(2)}, u32[]{:S(2)}) collective-permute-start(bf16[64,128]{1,0:T(8,128)(2,1)S(1)} %pad_maximum_fusion.refs_0_), channel_id=1, source_target_pairs={{0,16},{4,20},{8,24},{12,28},{16,0},{20,4},{24,8},{28,12},{1,17},{... | collective-permute-start | bytes 49160 | tf_op jit(solution)/shard_map/ppermute | solution.py:363
  13.7 0.0 collective-permute-done.8.query
  13.7 2.0 %shard_map.127.block = bf16[1184,128]{1,0:T(8,128)(2,1)S(1)} custom-call(bf16[128,1024]{1,0:T(8,128)(2,1)S(1)} %collective-permute-done.8.query, bf16[1280,256]{1,0:T(8,128)(2,1)S(1)} %get-tuple-element.13.keys, bf16[256,1280]{1,0:T(8,128)(2,1)S(1)} %get-tuple-element.14.values_t, f32[4,128,128]{2,1,0:T(8,128)S(1)} %get-tuple-element.15.cosine, ...), custom_call_target="tpu_custom_call" | custom-call | tf_op jit(solution)/shard_map/pallas_call | solution.py:404
  15.7 0.7 %collective-permute-done.4.refs_1_ = bf16[64,128]{1,0:T(8,128)(2,1)S(1)} collective-permute-done((bf16[64,128]{1,0:T(8,128)(2,1)S(1)}, bf16[64,128]{1,0:T(8,128)(2,1)S(1)}, u32[]{:S(2)}, u32[]{:S(2)}) %collective-permute-start.4) | collective-permute-done | bytes 16416 | tf_op jit(solution)/shard_map/ppermute | solution.py:363
  16.4 3.5 %collective-permute-start.9 = (bf16[1184,128]{1,0:T(8,128)(2,1)S(1)}, bf16[1184,128]{1,0:T(8,128)(2,1)S(1)}, u32[]{:S(2)}, u32[]{:S(2)}) collective-permute-start(bf16[1184,128]{1,0:T(8,128)(2,1)S(1)} %shard_map.128), channel_id=1, source_target_pairs={{0,12},{4,8},{8,4},{12,0},{16,28},{20,24},{24,20},{28,16},{1,13},{... | collective-permute-start | bytes 909320 | tf_op jit(solution)/shard_map/ppermute | solution.py:363
  19.9 0.0 collective-permute-done.query
  19.9 2.0 %shard_map.125 = bf16[1184,128]{1,0:T(8,128)(2,1)S(1)} custom-call(bf16[128,1024]{1,0:T(8,128)(2,1)S(1)} %collective-permute-done.query, bf16[1280,256]{1,0:T(8,128)(2,1)S(1)} %get-tuple-element.13.keys, bf16[256,1280]{1,0:T(8,128)(2,1)S(1)} %get-tuple-element.14.values_t, f32[4,128,128]{2,1,0:T(8,128)S(1)} %get-tuple-element.15.cosine, ...), custom_call_target="tpu_custom_call" | custom-call | tf_op jit(solution)/shard_map/pallas_call | solution.py:404
  21.9 0.0 copy-start.1
  22.0 1.6 %collective-permute-start.5 = (bf16[1184,128]{1,0:T(8,128)(2,1)S(1)}, bf16[1184,128]{1,0:T(8,128)(2,1)S(1)}, u32[]{:S(2)}, u32[]{:S(2)}) collective-permute-start(bf16[1184,128]{1,0:T(8,128)(2,1)S(1)} %shard_map.125), channel_id=1, source_target_pairs={{0,4},{4,0},{8,12},{12,8},{16,20},{20,16},{24,28},{28,24},{1,5},{5... | collective-permute-start | bytes 909320 | tf_op jit(solution)/shard_map/ppermute | solution.py:363
  23.5 0.0 collective-permute-done.6.query
  23.5 2.0 %shard_map.126 = bf16[1184,128]{1,0:T(8,128)(2,1)S(1)} custom-call(bf16[128,1024]{1,0:T(8,128)(2,1)S(1)} %collective-permute-done.6.query, bf16[1280,256]{1,0:T(8,128)(2,1)S(1)} %get-tuple-element.13.keys, bf16[256,1280]{1,0:T(8,128)(2,1)S(1)} %get-tuple-element.14.values_t, f32[4,128,128]{2,1,0:T(8,128)S(1)} %get-tuple-element.15.cosine, ...), custom_call_target="tpu_custom_call" | custom-call | tf_op jit(solution)/shard_map/pallas_call | solution.py:404
  25.5 0.0 copy-start
  25.6 0.0 copy-start.2
  25.6 0.0 copy-start.3
  25.6 0.1 collective-permute-start.7
  25.7 2.2 %shard_map.123.own = f32[1032,128]{1,0:T(8,128)S(1)} custom-call(bf16[128,1024]{1,0:T(8,128)(2,1)S(1)} %copy-done.1, bf16[1280,256]{1,0:T(8,128)(2,1)S(1)} %get-tuple-element.13.keys, bf16[256,1280]{1,0:T(8,128)(2,1)S(1)} %get-tuple-element.14.values_t, f32[4,128,128]{2,1,0:T(8,128)S(1)} %get-tuple-element.15.cosine, ...), custom_call_target="tpu_custom_call" | custom-call | tf_op jit(solution)/shard_map/pallas_call | solution.py:404
  27.9 0.0 collective-permute-done.9.third
  27.9 4.6 %collective-permute-done.5.first = bf16[1184,128]{1,0:T(8,128)(2,1)S(1)} collective-permute-done((bf16[1184,128]{1,0:T(8,128)(2,1)S(1)}, bf16[1184,128]{1,0:T(8,128)(2,1)S(1)}, u32[]{:S(2)}, u32[]{:S(2)}) %collective-permute-start.5) | collective-permute-done | bytes 303136 | tf_op jit(solution)/shard_map/ppermute | solution.py:363
  32.5 0.4 %collective-permute-done.7.second = bf16[1184,128]{1,0:T(8,128)(2,1)S(1)} collective-permute-done((bf16[1184,128]{1,0:T(8,128)(2,1)S(1)}, bf16[1184,128]{1,0:T(8,128)(2,1)S(1)}, u32[]{:S(2)}, u32[]{:S(2)}) %collective-permute-start.7) | collective-permute-done | bytes 303136 | tf_op jit(solution)/shard_map/ppermute | solution.py:363
  32.8 0.0 copy-done
  32.9 2.0 %shard_map.129 = (bf16[128,1024]{1,0:T(8,128)(2,1)}, bf16[4,1024]{1,0:T(4,128)(2,1)}) custom-call(s32[4]{0:T(128)S(1)} %copy-done.2, s32[32]{0:T(128)S(1)} %copy-done.3, f32[1032,128]{1,0:T(8,128)S(1)} %shard_map.123.own, bf16[1184,128]{1,0:T(8,128)(2,1)S(1)} %collective-permute-done.5.first, bf16[1184,128]{1,0:T(8,128)(2,1)S(1)} %collective-permute-done.7.second, ...), custom_call_target="tpu_custom_call" | custom-call | tf_op jit(solution)/shard_map/pallas_call | solution.py:404
  (6 shorter events, 0.0 us)
Async XLA Ops:
  0.6 13.1 %collective-permute-start.8 = (bf16[128,1024]{1,0:T(8,128)(2,1)}, bf16[128,1024]{1,0:T(8,128)(2,1)S(1)}, u32[]{:S(2)}, u32[]{:S(2)}) collective-permute-start(bf16[128,1024]{1,0:T(8,128)(2,1)} %query.1), channel_id=1, source_target_pairs={{0,12},{4,8},{8,4},{12,0},{16,28},{20,24},{24,20},{28,16},{1,13},{... | collective-permute-start | bytes 786440 | tf_op jit(solution)/shard_map/ppermute | solution.py:363
  4.6 15.3 %collective-permute-start = (bf16[128,1024]{1,0:T(8,128)(2,1)}, bf16[128,1024]{1,0:T(8,128)(2,1)S(1)}, u32[]{:S(2)}, u32[]{:S(2)}) collective-permute-start(bf16[128,1024]{1,0:T(8,128)(2,1)} %query.1), channel_id=1, source_target_pairs={{0,4},{4,0},{8,12},{12,8},{16,20},{20,16},{24,28},{28,24},{1,5},{5... | collective-permute-start | bytes 786440 | tf_op jit(solution)/shard_map/ppermute | solution.py:363
  5.2 18.3 %collective-permute-start.6 = (bf16[128,1024]{1,0:T(8,128)(2,1)}, bf16[128,1024]{1,0:T(8,128)(2,1)S(1)}, u32[]{:S(2)}, u32[]{:S(2)}) collective-permute-start(bf16[128,1024]{1,0:T(8,128)(2,1)} %query.1), channel_id=1, source_target_pairs={{0,8},{4,12},{8,0},{12,4},{16,24},{20,28},{24,16},{28,20},{1,9},{5... | collective-permute-start | bytes 786440 | tf_op jit(solution)/shard_map/ppermute | solution.py:363
  6.1 2.0 %collective-permute-start.1 = (bf16[16,128]{1,0:T(8,128)(2,1)S(1)}, bf16[16,128]{1,0:T(8,128)(2,1)S(1)}, u32[]{:S(2)}, u32[]{:S(2)}) collective-permute-start(bf16[16,128]{1,0:T(8,128)(2,1)S(1)} %get-tuple-element.19), channel_id=1, source_target_pairs={{0,1},{1,0},{2,3},{3,2},{4,5},{5,4},{6,7},{7,6},{8,9},{9,8},{10,11... | collective-permute-start | bytes 12296 | tf_op jit(solution)/shard_map/ppermute | solution.py:363
  6.1 4.7 %collective-permute-start.2 = (bf16[16,128]{1,0:T(8,128)(2,1)S(1)}, bf16[16,128]{1,0:T(8,128)(2,1)S(1)}, u32[]{:S(2)}, u32[]{:S(2)}) collective-permute-start(bf16[16,128]{1,0:T(8,128)(2,1)S(1)} %get-tuple-element.20), channel_id=1, source_target_pairs={{0,2},{1,3},{2,0},{3,1},{4,6},{5,7},{6,4},{7,5},{8,10},{9,11},{10,... | collective-permute-start | bytes 12296 | tf_op jit(solution)/shard_map/ppermute | solution.py:363
  8.1 3.0 %collective-permute-start.3 = (bf16[16,128]{1,0:T(8,128)(2,1)S(1)}, bf16[16,128]{1,0:T(8,128)(2,1)S(1)}, u32[]{:S(2)}, u32[]{:S(2)}) collective-permute-start(bf16[16,128]{1,0:T(8,128)(2,1)S(1)} %get-tuple-element.21), channel_id=1, source_target_pairs={{0,3},{1,2},{2,1},{3,0},{4,7},{5,6},{6,5},{7,4},{8,11},{9,10},{10,... | collective-permute-start | bytes 12296 | tf_op jit(solution)/shard_map/ppermute | solution.py:363
  11.1 5.3 %collective-permute-start.4 = (bf16[64,128]{1,0:T(8,128)(2,1)S(1)}, bf16[64,128]{1,0:T(8,128)(2,1)S(1)}, u32[]{:S(2)}, u32[]{:S(2)}) collective-permute-start(bf16[64,128]{1,0:T(8,128)(2,1)S(1)} %pad_maximum_fusion.refs_0_), channel_id=1, source_target_pairs={{0,16},{4,20},{8,24},{12,28},{16,0},{20,4},{24,8},{28,12},{1,17},{... | collective-permute-start | bytes 49160 | tf_op jit(solution)/shard_map/ppermute | solution.py:363
  16.4 11.4 %collective-permute-start.9 = (bf16[1184,128]{1,0:T(8,128)(2,1)S(1)}, bf16[1184,128]{1,0:T(8,128)(2,1)S(1)}, u32[]{:S(2)}, u32[]{:S(2)}) collective-permute-start(bf16[1184,128]{1,0:T(8,128)(2,1)S(1)} %shard_map.128), channel_id=1, source_target_pairs={{0,12},{4,8},{8,4},{12,0},{16,28},{20,24},{24,20},{28,16},{1,13},{... | collective-permute-start | bytes 909320 | tf_op jit(solution)/shard_map/ppermute | solution.py:363
  21.9 3.7 %copy-start.1 = (bf16[128,1024]{1,0:T(8,128)(2,1)S(1)}, bf16[128,1024]{1,0:T(8,128)(2,1)}, u32[]{:S(2)}) copy-start(bf16[128,1024]{1,0:T(8,128)(2,1)} %query.1) | copy-start | bytes 786436
  22.0 10.5 %collective-permute-start.5 = (bf16[1184,128]{1,0:T(8,128)(2,1)S(1)}, bf16[1184,128]{1,0:T(8,128)(2,1)S(1)}, u32[]{:S(2)}, u32[]{:S(2)}) collective-permute-start(bf16[1184,128]{1,0:T(8,128)(2,1)S(1)} %shard_map.125), channel_id=1, source_target_pairs={{0,4},{4,0},{8,12},{12,8},{16,20},{20,16},{24,28},{28,24},{1,5},{5... | collective-permute-start | bytes 909320 | tf_op jit(solution)/shard_map/ppermute | solution.py:363
  25.5 7.3 %copy-start = (bf16[2,4,512,256]{3,2,1,0:T(8,128)(2,1)S(1)}, bf16[2,4,512,256]{3,2,1,0:T(8,128)(2,1)}, u32[]{:S(2)}) copy-start(bf16[2,4,512,256]{3,2,1,0:T(8,128)(2,1)} %refs_2_.1) | copy-start | bytes 6291460
  25.6 7.3 %copy-start.2 = (s32[4]{0:T(128)S(1)}, s32[4]{0:T(128)}, u32[]{:S(2)}) copy-start(s32[4]{0:T(128)} %lengths.1) | copy-start | bytes 52
  25.6 7.3 %copy-start.3 = (s32[32]{0:T(128)S(1)}, s32[32]{0:T(128)}, u32[]{:S(2)}) copy-start(s32[32]{0:T(128)} %arrivals.1) | copy-start | bytes 388
  25.6 7.3 %collective-permute-start.7 = (bf16[1184,128]{1,0:T(8,128)(2,1)S(1)}, bf16[1184,128]{1,0:T(8,128)(2,1)S(1)}, u32[]{:S(2)}, u32[]{:S(2)}) collective-permute-start(bf16[1184,128]{1,0:T(8,128)(2,1)S(1)} %shard_map.126), channel_id=1, source_target_pairs={{0,8},{4,12},{8,0},{12,4},{16,24},{20,28},{24,16},{28,20},{1,9},{5... | collective-permute-start | bytes 909320 | tf_op jit(solution)/shard_map/ppermute | solution.py:363

commit v7 on v6

--- a/solution.py
+++ b/solution.py
@@ -271,7 +271,7 @@
         mix = own[lines, :] * shares[0][head : head + 1, :]
         for other, share in zip((first, second, third), shares[1:]):
             mix = mix + other[lines, :].astype(jnp.float32) * share[head : head + 1, :]
-        out[:, lines] = mix.T.astype(out.dtype)
+        out[:, lines] = mix.astype(out.dtype).T
 
 
 def decode(lengths, arrivals, near, cache, tables, out, mixed):

time: 35.1 us -> 35.1 us (level)
  no operation moved by 1% of the time
where the time goes in v7:
time: 35.1 us; the launch traced here: 34.8 us
  starting transfers between devices  15.2 us (43%)
  Pallas kernels  12.9 us (37%)
  waiting for transfers between devices  5.89 us (17%)
  between operations  0.76 us (2%)
    ppermute x10, starting transfers between devices, exchange(): return lax.ppermute(block, axis, [(i, i ^ distance) for i in range(count)])  15.2 us
    pallas_call x8, Pallas kernels, call(): pl.pallas_call(kernel, in_specs=specs, out_specs=jax.tree.map(lambda _: N...  12.9 us
    ppermute x10, waiting for transfers between devices, exchange(): return lax.ppermute(block, axis, [(i, i ^ distance) for i in range(count)])  5.89 us
  transfers between devices with their start and end apart: 10, of which 4 were waited for; matrix products, arithmetic and copies ran while one was open for 0% of the time, Pallas kernels for 32%

profile of v7, /device:TPU:0, one launch (start us, length us, event | category | flops | bytes accessed | tf_op | source)
XLA Modules:
  0.0 34.8 jit_solution(7815009935628760136)
XLA Ops:
  0.6 4.0 %collective-permute-start.8 = (bf16[128,1024]{1,0:T(8,128)(2,1)}, bf16[128,1024]{1,0:T(8,128)(2,1)S(1)}, u32[]{:S(2)}, u32[]{:S(2)}) collective-permute-start(bf16[128,1024]{1,0:T(8,128)(2,1)} %query.1), channel_id=1, source_target_pairs={{0,12},{4,8},{8,4},{12,0},{16,28},{20,24},{24,20},{28,16},{1,13},{... | collective-permute-start | bytes 786440 | tf_op jit(solution)/shard_map/ppermute | solution.py:363
  4.6 0.5 %collective-permute-start = (bf16[128,1024]{1,0:T(8,128)(2,1)}, bf16[128,1024]{1,0:T(8,128)(2,1)S(1)}, u32[]{:S(2)}, u32[]{:S(2)}) collective-permute-start(bf16[128,1024]{1,0:T(8,128)(2,1)} %query.1), channel_id=1, source_target_pairs={{0,4},{4,0},{8,12},{12,8},{16,20},{20,16},{24,28},{28,24},{1,5},{5... | collective-permute-start | bytes 786440 | tf_op jit(solution)/shard_map/ppermute | solution.py:363
  5.2 0.1 collective-permute-start.6
  5.3 0.8 %shard_map.124 = (bf16[16,128]{1,0:T(8,128)(2,1)S(1)}, bf16[16,128]{1,0:T(8,128)(2,1)S(1)}, bf16[16,128]{1,0:T(8,128)(2,1)S(1)}, bf16[16,128]{1,0:T(8,128)(2,1)S(1)}) custom-call(bf16[1,4096]{1,0:T(2,128)(2,1)} %query_far.1, bf16[1,2,1024]{2,1,0:T(2,128)(2,1)} %new_kv_far.3), custom_call_target="tpu_custom_call" | custom-call | tf_op jit(solution)/shard_map/pallas_call | solution.py:404
  6.1 0.1 collective-permute-start.1
  6.1 1.9 %collective-permute-start.2 = (bf16[16,128]{1,0:T(8,128)(2,1)S(1)}, bf16[16,128]{1,0:T(8,128)(2,1)S(1)}, u32[]{:S(2)}, u32[]{:S(2)}) collective-permute-start(bf16[16,128]{1,0:T(8,128)(2,1)S(1)} %get-tuple-element.20), channel_id=1, source_target_pairs={{0,2},{1,3},{2,0},{3,1},{4,6},{5,7},{6,4},{7,5},{8,10},{9,11},{10,... | collective-permute-start | bytes 12296 | tf_op jit(solution)/shard_map/ppermute | solution.py:363
  8.1 0.0 collective-permute-done.1
  8.1 0.9 %collective-permute-start.3 = (bf16[16,128]{1,0:T(8,128)(2,1)S(1)}, bf16[16,128]{1,0:T(8,128)(2,1)S(1)}, u32[]{:S(2)}, u32[]{:S(2)}) collective-permute-start(bf16[16,128]{1,0:T(8,128)(2,1)S(1)} %get-tuple-element.21), channel_id=1, source_target_pairs={{0,3},{1,2},{2,1},{3,0},{4,7},{5,6},{6,5},{7,4},{8,11},{9,10},{10,... | collective-permute-start | bytes 12296 | tf_op jit(solution)/shard_map/ppermute | solution.py:363
  8.9 1.9 %shard_map.122 = (bf16[1280,256]{1,0:T(8,128)(2,1)S(1)}, bf16[256,1280]{1,0:T(8,128)(2,1)S(1)}, f32[4,128,128]{2,1,0:T(8,128)S(1)}, f32[4,128,128]{2,1,0:T(8,128...) custom-call(s32[2]{0:T(128)} %lengths_far.1, s32[2]{0:T(128)} %offsets_far.1, ...), custom_call_target="tpu_custom_call" | custom-call | tf_op jit(solution)/shard_map/pallas_call | solution.py:404
  10.9 0.0 collective-permute-done.2
  10.9 0.2 collective-permute-done.3
  11.1 2.6 %collective-permute-start.4 = (bf16[64,128]{1,0:T(8,128)(2,1)S(1)}, bf16[64,128]{1,0:T(8,128)(2,1)S(1)}, u32[]{:S(2)}, u32[]{:S(2)}) collective-permute-start(bf16[64,128]{1,0:T(8,128)(2,1)S(1)} %pad_maximum_fusion.refs_0_), channel_id=1, source_target_pairs={{0,16},{4,20},{8,24},{12,28},{16,0},{20,4},{24,8},{28,12},{1,17},{... | collective-permute-start | bytes 49160 | tf_op jit(solution)/shard_map/ppermute | solution.py:363
  13.7 0.0 collective-permute-done.8.query
  13.7 2.0 %shard_map.127.block = bf16[1184,128]{1,0:T(8,128)(2,1)S(1)} custom-call(bf16[128,1024]{1,0:T(8,128)(2,1)S(1)} %collective-permute-done.8.query, bf16[1280,256]{1,0:T(8,128)(2,1)S(1)} %get-tuple-element.13.keys, bf16[256,1280]{1,0:T(8,128)(2,1)S(1)} %get-tuple-element.14.values_t, f32[4,128,128]{2,1,0:T(8,128)S(1)} %get-tuple-element.15.cosine, ...), custom_call_target="tpu_custom_call" | custom-call | tf_op jit(solution)/shard_map/pallas_call | solution.py:404
  15.7 0.7 %collective-permute-done.4.refs_1_ = bf16[64,128]{1,0:T(8,128)(2,1)S(1)} collective-permute-done((bf16[64,128]{1,0:T(8,128)(2,1)S(1)}, bf16[64,128]{1,0:T(8,128)(2,1)S(1)}, u32[]{:S(2)}, u32[]{:S(2)}) %collective-permute-start.4) | collective-permute-done | bytes 16416 | tf_op jit(solution)/shard_map/ppermute | solution.py:363
  16.4 3.5 %collective-permute-start.9 = (bf16[1184,128]{1,0:T(8,128)(2,1)S(1)}, bf16[1184,128]{1,0:T(8,128)(2,1)S(1)}, u32[]{:S(2)}, u32[]{:S(2)}) collective-permute-start(bf16[1184,128]{1,0:T(8,128)(2,1)S(1)} %shard_map.128), channel_id=1, source_target_pairs={{0,12},{4,8},{8,4},{12,0},{16,28},{20,24},{24,20},{28,16},{1,13},{... | collective-permute-start | bytes 909320 | tf_op jit(solution)/shard_map/ppermute | solution.py:363
  19.9 0.0 collective-permute-done.query
  19.9 2.0 %shard_map.125 = bf16[1184,128]{1,0:T(8,128)(2,1)S(1)} custom-call(bf16[128,1024]{1,0:T(8,128)(2,1)S(1)} %collective-permute-done.query, bf16[1280,256]{1,0:T(8,128)(2,1)S(1)} %get-tuple-element.13.keys, bf16[256,1280]{1,0:T(8,128)(2,1)S(1)} %get-tuple-element.14.values_t, f32[4,128,128]{2,1,0:T(8,128)S(1)} %get-tuple-element.15.cosine, ...), custom_call_target="tpu_custom_call" | custom-call | tf_op jit(solution)/shard_map/pallas_call | solution.py:404
  21.9 0.0 copy-start.1
  22.0 1.6 %collective-permute-start.5 = (bf16[1184,128]{1,0:T(8,128)(2,1)S(1)}, bf16[1184,128]{1,0:T(8,128)(2,1)S(1)}, u32[]{:S(2)}, u32[]{:S(2)}) collective-permute-start(bf16[1184,128]{1,0:T(8,128)(2,1)S(1)} %shard_map.125), channel_id=1, source_target_pairs={{0,4},{4,0},{8,12},{12,8},{16,20},{20,16},{24,28},{28,24},{1,5},{5... | collective-permute-start | bytes 909320 | tf_op jit(solution)/shard_map/ppermute | solution.py:363
  23.5 0.0 collective-permute-done.6.query
  23.5 2.0 %shard_map.126 = bf16[1184,128]{1,0:T(8,128)(2,1)S(1)} custom-call(bf16[128,1024]{1,0:T(8,128)(2,1)S(1)} %collective-permute-done.6.query, bf16[1280,256]{1,0:T(8,128)(2,1)S(1)} %get-tuple-element.13.keys, bf16[256,1280]{1,0:T(8,128)(2,1)S(1)} %get-tuple-element.14.values_t, f32[4,128,128]{2,1,0:T(8,128)S(1)} %get-tuple-element.15.cosine, ...), custom_call_target="tpu_custom_call" | custom-call | tf_op jit(solution)/shard_map/pallas_call | solution.py:404
  25.5 0.0 copy-start
  25.6 0.0 copy-start.2
  25.6 0.0 copy-start.3
  25.6 0.1 collective-permute-start.7
  25.7 2.2 %shard_map.123.own = f32[1032,128]{1,0:T(8,128)S(1)} custom-call(bf16[128,1024]{1,0:T(8,128)(2,1)S(1)} %copy-done.1, bf16[1280,256]{1,0:T(8,128)(2,1)S(1)} %get-tuple-element.13.keys, bf16[256,1280]{1,0:T(8,128)(2,1)S(1)} %get-tuple-element.14.values_t, f32[4,128,128]{2,1,0:T(8,128)S(1)} %get-tuple-element.15.cosine, ...), custom_call_target="tpu_custom_call" | custom-call | tf_op jit(solution)/shard_map/pallas_call | solution.py:404
  27.9 0.0 collective-permute-done.9.third
  27.9 4.6 %collective-permute-done.5.first = bf16[1184,128]{1,0:T(8,128)(2,1)S(1)} collective-permute-done((bf16[1184,128]{1,0:T(8,128)(2,1)S(1)}, bf16[1184,128]{1,0:T(8,128)(2,1)S(1)}, u32[]{:S(2)}, u32[]{:S(2)}) %collective-permute-start.5) | collective-permute-done | bytes 303136 | tf_op jit(solution)/shard_map/ppermute | solution.py:363
  32.5 0.4 %collective-permute-done.7.second = bf16[1184,128]{1,0:T(8,128)(2,1)S(1)} collective-permute-done((bf16[1184,128]{1,0:T(8,128)(2,1)S(1)}, bf16[1184,128]{1,0:T(8,128)(2,1)S(1)}, u32[]{:S(2)}, u32[]{:S(2)}) %collective-permute-start.7) | collective-permute-done | bytes 303136 | tf_op jit(solution)/shard_map/ppermute | solution.py:363
  32.8 0.0 copy-done
  32.9 2.0 %shard_map.129 = (bf16[128,1024]{1,0:T(8,128)(2,1)}, bf16[4,1024]{1,0:T(4,128)(2,1)}) custom-call(s32[4]{0:T(128)S(1)} %copy-done.2, s32[32]{0:T(128)S(1)} %copy-done.3, f32[1032,128]{1,0:T(8,128)S(1)} %shard_map.123.own, bf16[1184,128]{1,0:T(8,128)(2,1)S(1)} %collective-permute-done.5.first, bf16[1184,128]{1,0:T(8,128)(2,1)S(1)} %collective-permute-done.7.second, ...), custom_call_target="tpu_custom_call" | custom-call | tf_op jit(solution)/shard_map/pallas_call | solution.py:404
  (6 shorter events, 0.0 us)
Async XLA Ops:
  0.6 13.1 %collective-permute-start.8 = (bf16[128,1024]{1,0:T(8,128)(2,1)}, bf16[128,1024]{1,0:T(8,128)(2,1)S(1)}, u32[]{:S(2)}, u32[]{:S(2)}) collective-permute-start(bf16[128,1024]{1,0:T(8,128)(2,1)} %query.1), channel_id=1, source_target_pairs={{0,12},{4,8},{8,4},{12,0},{16,28},{20,24},{24,20},{28,16},{1,13},{... | collective-permute-start | bytes 786440 | tf_op jit(solution)/shard_map/ppermute | solution.py:363
  4.6 15.3 %collective-permute-start = (bf16[128,1024]{1,0:T(8,128)(2,1)}, bf16[128,1024]{1,0:T(8,128)(2,1)S(1)}, u32[]{:S(2)}, u32[]{:S(2)}) collective-permute-start(bf16[128,1024]{1,0:T(8,128)(2,1)} %query.1), channel_id=1, source_target_pairs={{0,4},{4,0},{8,12},{12,8},{16,20},{20,16},{24,28},{28,24},{1,5},{5... | collective-permute-start | bytes 786440 | tf_op jit(solution)/shard_map/ppermute | solution.py:363
  5.2 18.3 %collective-permute-start.6 = (bf16[128,1024]{1,0:T(8,128)(2,1)}, bf16[128,1024]{1,0:T(8,128)(2,1)S(1)}, u32[]{:S(2)}, u32[]{:S(2)}) collective-permute-start(bf16[128,1024]{1,0:T(8,128)(2,1)} %query.1), channel_id=1, source_target_pairs={{0,8},{4,12},{8,0},{12,4},{16,24},{20,28},{24,16},{28,20},{1,9},{5... | collective-permute-start | bytes 786440 | tf_op jit(solution)/shard_map/ppermute | solution.py:363
  6.1 2.0 %collective-permute-start.1 = (bf16[16,128]{1,0:T(8,128)(2,1)S(1)}, bf16[16,128]{1,0:T(8,128)(2,1)S(1)}, u32[]{:S(2)}, u32[]{:S(2)}) collective-permute-start(bf16[16,128]{1,0:T(8,128)(2,1)S(1)} %get-tuple-element.19), channel_id=1, source_target_pairs={{0,1},{1,0},{2,3},{3,2},{4,5},{5,4},{6,7},{7,6},{8,9},{9,8},{10,11... | collective-permute-start | bytes 12296 | tf_op jit(solution)/shard_map/ppermute | solution.py:363
  6.1 4.7 %collective-permute-start.2 = (bf16[16,128]{1,0:T(8,128)(2,1)S(1)}, bf16[16,128]{1,0:T(8,128)(2,1)S(1)}, u32[]{:S(2)}, u32[]{:S(2)}) collective-permute-start(bf16[16,128]{1,0:T(8,128)(2,1)S(1)} %get-tuple-element.20), channel_id=1, source_target_pairs={{0,2},{1,3},{2,0},{3,1},{4,6},{5,7},{6,4},{7,5},{8,10},{9,11},{10,... | collective-permute-start | bytes 12296 | tf_op jit(solution)/shard_map/ppermute | solution.py:363
  8.1 3.0 %collective-permute-start.3 = (bf16[16,128]{1,0:T(8,128)(2,1)S(1)}, bf16[16,128]{1,0:T(8,128)(2,1)S(1)}, u32[]{:S(2)}, u32[]{:S(2)}) collective-permute-start(bf16[16,128]{1,0:T(8,128)(2,1)S(1)} %get-tuple-element.21), channel_id=1, source_target_pairs={{0,3},{1,2},{2,1},{3,0},{4,7},{5,6},{6,5},{7,4},{8,11},{9,10},{10,... | collective-permute-start | bytes 12296 | tf_op jit(solution)/shard_map/ppermute | solution.py:363
  11.1 5.3 %collective-permute-start.4 = (bf16[64,128]{1,0:T(8,128)(2,1)S(1)}, bf16[64,128]{1,0:T(8,128)(2,1)S(1)}, u32[]{:S(2)}, u32[]{:S(2)}) collective-permute-start(bf16[64,128]{1,0:T(8,128)(2,1)S(1)} %pad_maximum_fusion.refs_0_), channel_id=1, source_target_pairs={{0,16},{4,20},{8,24},{12,28},{16,0},{20,4},{24,8},{28,12},{1,17},{... | collective-permute-start | bytes 49160 | tf_op jit(solution)/shard_map/ppermute | solution.py:363
  16.4 11.4 %collective-permute-start.9 = (bf16[1184,128]{1,0:T(8,128)(2,1)S(1)}, bf16[1184,128]{1,0:T(8,128)(2,1)S(1)}, u32[]{:S(2)}, u32[]{:S(2)}) collective-permute-start(bf16[1184,128]{1,0:T(8,128)(2,1)S(1)} %shard_map.128), channel_id=1, source_target_pairs={{0,12},{4,8},{8,4},{12,0},{16,28},{20,24},{24,20},{28,16},{1,13},{... | collective-permute-start | bytes 909320 | tf_op jit(solution)/shard_map/ppermute | solution.py:363
  21.9 3.7 %copy-start.1 = (bf16[128,1024]{1,0:T(8,128)(2,1)S(1)}, bf16[128,1024]{1,0:T(8,128)(2,1)}, u32[]{:S(2)}) copy-start(bf16[128,1024]{1,0:T(8,128)(2,1)} %query.1) | copy-start | bytes 786436
  22.0 10.5 %collective-permute-start.5 = (bf16[1184,128]{1,0:T(8,128)(2,1)S(1)}, bf16[1184,128]{1,0:T(8,128)(2,1)S(1)}, u32[]{:S(2)}, u32[]{:S(2)}) collective-permute-start(bf16[1184,128]{1,0:T(8,128)(2,1)S(1)} %shard_map.125), channel_id=1, source_target_pairs={{0,4},{4,0},{8,12},{12,8},{16,20},{20,16},{24,28},{28,24},{1,5},{5... | collective-permute-start | bytes 909320 | tf_op jit(solution)/shard_map/ppermute | solution.py:363
  25.5 7.3 %copy-start = (bf16[2,4,512,256]{3,2,1,0:T(8,128)(2,1)S(1)}, bf16[2,4,512,256]{3,2,1,0:T(8,128)(2,1)}, u32[]{:S(2)}) copy-start(bf16[2,4,512,256]{3,2,1,0:T(8,128)(2,1)} %refs_2_.1) | copy-start | bytes 6291460
  25.6 7.3 %copy-start.2 = (s32[4]{0:T(128)S(1)}, s32[4]{0:T(128)}, u32[]{:S(2)}) copy-start(s32[4]{0:T(128)} %lengths.1) | copy-start | bytes 52
  25.6 7.3 %copy-start.3 = (s32[32]{0:T(128)S(1)}, s32[32]{0:T(128)}, u32[]{:S(2)}) copy-start(s32[32]{0:T(128)} %arrivals.1) | copy-start | bytes 388
  25.6 7.3 %collective-permute-start.7 = (bf16[1184,128]{1,0:T(8,128)(2,1)S(1)}, bf16[1184,128]{1,0:T(8,128)(2,1)S(1)}, u32[]{:S(2)}, u32[]{:S(2)}) collective-permute-start(bf16[1184,128]{1,0:T(8,128)(2,1)S(1)} %shard_map.126), channel_id=1, source_target_pairs={{0,8},{4,12},{8,0},{12,4},{16,24},{20,28},{24,16},{28,20},{1,9},{5... | collective-permute-start | bytes 909320 | tf_op jit(solution)/shard_map/ppermute | solution.py:363
